TPU v7x, 512 devices: a whole 4x8x8 slice. The times are simulated.
512 devices in a mesh: dp: 16 (over y, core), expert: 32 (over z, x).
Axes of the slice: x: 4, y: 8, z: 8, core: 2. Of those that a mesh axis runs over, the one named last changes fastest.
Arguments:
- inputs: bfloat16 [2, 65536, 2048], P(None, ('dp', 'expert')), may hold values from -24 to 24
- cotangents: bfloat16 [2, 65536, 2048], P(None, ('dp', 'expert')), may hold values from -24 to 24
- gates: bfloat16 [2, 65536], P(None, ('dp', 'expert')), may hold values from 0.099609375 to 1
- routing: int32 [2, 65536, 1], P(None, ('dp', 'expert')), may hold values from 0 to 15; in each aligned block of 128 rows (0 to 127, 128 to 255, ..., all dimensions but the last counted through in order) at most 12 rows name the same one
- w_gate: bfloat16 [2048, 8192], P('dp', 'expert'), may hold values from -0.125 to 0.125
- w_up: bfloat16 [2048, 8192], P('dp', 'expert'), may hold values from -0.125 to 0.125
- w_down: bfloat16 [8192, 2048], P('expert', 'dp'), may hold values from -0.25 to 0.25
Outputs:
- grad_inputs: bfloat16 [2, 65536, 2048], P(None, ('dp', 'expert'))
- grad_gates: bfloat16 [2, 65536], P(None, ('dp', 'expert'))
- grad_w_gate: float32 [2048, 8192], P('dp', 'expert')
- grad_w_up: float32 [2048, 8192], P('dp', 'expert')
- grad_w_down: float32 [8192, 2048], P('expert', 'dp')
Inputs may be any that keep to these rules, and one draw needn't show every extreme that they name: `routing`: in one layer, no expert is named by more than 12 of the 128 tokens of one device; some device's tokens name one expert exactly 12 times.
All inputs are finite; a program needn't handle non-finite values.
Results may differ from a plain program's by a relative error of at most 0.022.
Values may be sent and summed in bfloat16 or wider, within the bound.
No kernel may reach another device: no remote copies, remote signals or barrier semaphores. Data moves between devices by JAX's collectives and lax.ppermute only.
A program may use at most 128 MiB of HBM per device.

v0:
```python
import jax
import jax.numpy as jnp
from jax import lax
from jax.sharding import PartitionSpec as P


def slot_table(route, expert_count, capacity):
    onehot = (route[:, None] == jnp.arange(expert_count, dtype=jnp.int32)[None, :]).astype(
        jnp.int32
    )
    ranks = jnp.cumsum(onehot, axis=0) - 1
    placed = route * capacity + jnp.sum(onehot * ranks, axis=1)
    slots = jnp.arange(expert_count * capacity, dtype=jnp.int32)
    return (placed[None, :] == slots[:, None]).astype(jnp.bfloat16)


def outgoing(table, tokens_in, grads_in, gate_in, expert_count, capacity):
    peer_count = 2 * expert_count
    model_width = tokens_in.shape[1]
    features = jnp.concatenate([tokens_in, grads_in], axis=1)
    packed = jnp.dot(table, features, preferred_element_type=jnp.float32).astype(jnp.bfloat16)
    scales = jnp.dot(table, gate_in, preferred_element_type=jnp.float32).astype(jnp.bfloat16)
    packed = packed.reshape(expert_count, capacity, 2 * model_width)
    scales = scales.reshape(expert_count, capacity)
    packed = jnp.broadcast_to(
        packed[:, None], (expert_count, 2, capacity, 2 * model_width)
    ).reshape(peer_count, capacity, 2 * model_width)
    scales = jnp.broadcast_to(scales[:, None], (expert_count, 2, capacity)).reshape(
        peer_count, capacity
    )
    return (packed, scales)


def local(inputs, cotangents, gates, routing, w_gate, w_up, w_down):
    peer_count = lax.axis_size("expert")
    expert_count = peer_count // 2
    layers, token_count, model_width = inputs.shape
    capacity = 3 * token_count // (2 * expert_count)
    gate_full, up_full = (
        lax.all_gather(w_gate, "dp", axis=0, tiled=True),
        lax.all_gather(w_up, "dp", axis=0, tiled=True),
    )
    down_full = lax.all_gather(w_down, "dp", axis=1, tiled=True)
    half_width = gate_full.shape[1]
    tables = [slot_table(routing[layer, :, 0], expert_count, capacity) for layer in range(layers)]
    arrived = []
    for layer in range(layers):
        packed, scales = outgoing(
            tables[layer], inputs[layer], cotangents[layer], gates[layer], expert_count, capacity
        )
        arrived.append(
            (
                lax.all_to_all(packed, "expert", split_axis=0, concat_axis=0, tiled=True),
                lax.all_to_all(scales, "expert", split_axis=0, concat_axis=0, tiled=True),
            )
        )
    contract_rows = (((0,), (0,)), ((), ()))
    contract_cols = (((1,), (1,)), ((), ()))
    acc_gate = jnp.zeros((model_width, half_width), jnp.float32)
    acc_up = jnp.zeros((model_width, half_width), jnp.float32)
    acc_down = jnp.zeros((half_width, model_width), jnp.float32)
    token_grads = []
    gate_grads = []
    for layer in range(layers):
        got_packed, got_scales = arrived[layer]
        received = got_packed.reshape(peer_count * capacity, 2 * model_width)
        token_rows = received[:, :model_width]
        grad_rows = received[:, model_width:]
        gate_rows = got_scales.reshape(peer_count * capacity).astype(jnp.float32)[:, None]
        gate_pre = jnp.dot(token_rows, gate_full, preferred_element_type=jnp.float32)
        up_value = jnp.dot(token_rows, up_full, preferred_element_type=jnp.float32)
        back_hidden = lax.dot_general(
            grad_rows, down_full, contract_cols, preferred_element_type=jnp.float32
        )
        sigmoid_gate = jax.nn.sigmoid(gate_pre)
        swish_gate = gate_pre * sigmoid_gate
        hidden = swish_gate * up_value
        gate_part = jnp.sum(hidden * back_hidden, axis=1).astype(jnp.bfloat16)
        scaled = (gate_rows * hidden).astype(jnp.bfloat16)
        back_scaled = gate_rows * back_hidden
        grad_pre = (
            back_scaled * up_value * sigmoid_gate * (1.0 + gate_pre * (1.0 - sigmoid_gate))
        ).astype(jnp.bfloat16)
        grad_up = (back_scaled * swish_gate).astype(jnp.bfloat16)
        acc_down = acc_down + lax.dot_general(
            scaled, grad_rows, contract_rows, preferred_element_type=jnp.float32
        )
        acc_gate = acc_gate + lax.dot_general(
            token_rows, grad_pre, contract_rows, preferred_element_type=jnp.float32
        )
        acc_up = acc_up + lax.dot_general(
            token_rows, grad_up, contract_rows, preferred_element_type=jnp.float32
        )
        input_part = lax.dot_general(
            grad_pre, gate_full, contract_cols, preferred_element_type=jnp.float32
        )
        input_part = input_part + lax.dot_general(
            grad_up, up_full, contract_cols, preferred_element_type=jnp.float32
        )
        input_part = input_part.astype(jnp.bfloat16).reshape(peer_count, capacity, model_width)
        gate_part = gate_part.reshape(peer_count, capacity)
        back_input, back_gate = (
            lax.all_to_all(input_part, "expert", split_axis=0, concat_axis=0, tiled=True),
            lax.all_to_all(gate_part, "expert", split_axis=0, concat_axis=0, tiled=True),
        )
        combined = jnp.sum(
            back_input.reshape(expert_count, 2, capacity, model_width).astype(jnp.float32), axis=1
        )
        combined = combined.astype(jnp.bfloat16).reshape(expert_count * capacity, model_width)
        combined_gate = jnp.sum(
            back_gate.reshape(expert_count, 2, capacity).astype(jnp.float32), axis=1
        )
        combined_gate = combined_gate.astype(jnp.bfloat16).reshape(expert_count * capacity)
        token_grads.append(
            lax.dot_general(
                tables[layer], combined, contract_rows, preferred_element_type=jnp.float32
            ).astype(jnp.bfloat16)
        )
        gate_grads.append(
            jnp.dot(combined_gate, tables[layer], preferred_element_type=jnp.float32).astype(
                jnp.bfloat16
            )
        )
    grad_w_gate, grad_w_up = (
        lax.psum_scatter(
            acc_gate.astype(jnp.bfloat16), "dp", scatter_dimension=0, tiled=True
        ).astype(jnp.float32),
        lax.psum_scatter(acc_up.astype(jnp.bfloat16), "dp", scatter_dimension=0, tiled=True).astype(
            jnp.float32
        ),
    )
    grad_w_down = lax.psum_scatter(
        acc_down.astype(jnp.bfloat16), "dp", scatter_dimension=1, tiled=True
    ).astype(jnp.float32)
    return (jnp.stack(token_grads), jnp.stack(gate_grads), grad_w_gate, grad_w_up, grad_w_down)


def solution(mesh):
    placed = (
        P(None, ("dp", "expert"), None),
        P(None, ("dp", "expert"), None),
        P(None, ("dp", "expert")),
        P(None, ("dp", "expert"), None),
        P("dp", "expert"),
        P("dp", "expert"),
        P("expert", "dp"),
    )
    return jax.shard_map(
        local,
        mesh=mesh,
        in_specs=placed,
        out_specs=(
            P(None, ("dp", "expert"), None),
            P(None, ("dp", "expert")),
            P("dp", "expert"),
            P("dp", "expert"),
            P("expert", "dp"),
        ),
        check_vma=False,
    )
```

profile of v0, /device:TPU:2, one launch (start us, length us, event | category | flops | bytes accessed | tf_op | source)
XLA Modules:
  0.0 472.9 jit_solution(5274976813807621548)
XLA Ops:
  7.2 0.7 slice_bitcast_fusion.9
  8.5 0.7 multiply_add_fusion.1
  9.2 0.8 fusion.43
  10.2 0.6 copy.14
  10.8 13.5 %all-to-all-start = ((bf16[32,1,12]{2,1,0:T(2,128)(2,1)}), bf16[32,1,12]{2,1,0:T(2,128)(2,1)S(1)}, u32[]{:S(2)}, u32[]{:S(2)}) async-start(bf16[32,1,12]{2,1,0:T(2,128)(2,1)} %copy.14), calls=%async_computation | async-start | bytes 32768 | tf_op jit(solution)/shard_map/all_to_all | solution.py:54
  24.3 1.7 slice_bitcast_fusion.2
  26.9 5.9 %all-to-all-done = bf16[32,1,12]{2,1,0:T(2,128)(2,1)S(1)} async-done(((bf16[32,1,12]{2,1,0:T(2,128)(2,1)}), bf16[32,1,12]{2,1,0:T(2,128)(2,1)S(1)}, u32[]{:S(2)}, u32[]{:S(2)}) %all-to-all-start) | async-done | bytes 800 | tf_op jit(solution)/shard_map/all_to_all | solution.py:54
  32.7 4.9 %all-to-all-start.3 = ((bf16[32,1,12]{2,1,0:T(2,128)(2,1)}), bf16[32,1,12]{2,1,0:T(2,128)(2,1)S(1)}, u32[]{:S(2)}, u32[]{:S(2)}) async-start(bf16[32,1,12]{2,1,0:T(2,128)(2,1)} %copy.15), calls=%async_computation.3 | async-start | bytes 32768 | tf_op jit(solution)/shard_map/all_to_all | solution.py:54
  37.7 1.7 convolution_convert_fusion
  39.4 2.3 broadcast_in_dim.42
  41.7 4.5 all-to-all-done.3
  46.2 2.5 broadcast_in_dim.43
  48.7 5.9 %all-to-all-start.4 = ((bf16[32,12,4096]{2,1,0:T(8,128)(2,1)}), bf16[32,12,4096]{2,1,0:T(8,128)(2,1)}, u32[]{:S(2)}, u32[]{:S(2)}) async-start(bf16[32,12,4096]{2,1,0:T(8,128)(2,1)} %bitcast.81), calls=%async_computation.4 | async-start | bytes 8388608 | tf_op jit(solution)/shard_map/all_to_all | solution.py:53
  54.6 0.7 all-gather.8.cloned.1.call-update
  55.3 1.7 convolution_convert_fusion.1
  57.1 2.3 broadcast_in_dim.18
  59.4 87.5 %all-to-all-done.4 = bf16[32,12,4096]{2,1,0:T(8,128)(2,1)} async-done(((bf16[32,12,4096]{2,1,0:T(8,128)(2,1)}), bf16[32,12,4096]{2,1,0:T(8,128)(2,1)}, u32[]{:S(2)}, u32[]{:S(2)}) %all-to-all-start.4) | async-done | bytes 3145760 | tf_op jit(solution)/shard_map/all_to_all | solution.py:53
  146.9 2.5 broadcast_in_dim.19
  149.4 6.7 %all-to-all-start.1 = ((bf16[32,12,4096]{2,1,0:T(8,128)(2,1)}), bf16[32,12,4096]{2,1,0:T(8,128)(2,1)}, u32[]{:S(2)}, u32[]{:S(2)}) async-start(bf16[32,12,4096]{2,1,0:T(8,128)(2,1)} %bitcast.80), calls=%async_computation.1 | async-start | bytes 8388608 | tf_op jit(solution)/shard_map/all_to_all | solution.py:53
  156.1 0.7 all-gather.6.cloned.1.call-update
  156.9 0.7 all-gather.4.cloned.1.call-update
  157.6 0.7 reshape.146
  158.5 4.0 reshape.138
  162.5 2.7 fusion.24
  165.2 35.7 %all-gather.6.cloned.1.call-done = bf16[2048,256]{1,0:T(8,128)(2,1)} async-done(((bf16[128,256]{1,0:T(8,128)(2,1)}), bf16[2048,256]{1,0:T(8,128)(2,1)}) %all-gather.6.cloned.1.call-update) | async-done | bytes 1048592 | tf_op jit(solution)/shard_map/all_gather | solution.py:41
  200.9 2.7 fusion.26
  203.6 38.6 %all-gather.4.cloned.1.call-done = bf16[256,2048]{1,0:T(8,128)(2,1)} async-done(((bf16[256,128]{1,0:T(8,128)(2,1)}), bf16[256,2048]{1,0:T(8,128)(2,1)}) %all-gather.4.cloned.1.call-update) | async-done | bytes 1048592 | tf_op jit(solution)/shard_map/all_gather | solution.py:43
  242.2 2.3 multiply_reduce_fusion
  244.5 0.7 convert_element_type.165
  245.2 2.9 all-to-all-done.1
  248.2 7.6 %all-to-all-start.7 = ((bf16[32,1,12]{2,1,0:T(2,128)(2,1)}), bf16[32,1,12]{2,1,0:T(2,128)(2,1)S(1)}, u32[]{:S(2)}, u32[]{:S(2)}) async-start(bf16[32,1,12]{2,1,0:T(2,128)(2,1)} %convert_element_type.165), calls=%async_computation.7 | async-start | bytes 32768 | tf_op jit(solution)/shard_map/all_to_all | solution.py:104
  256.0 5.6 %reshape.133 = bf16[384,4096]{1,0:T(8,128)(2,1)} reshape(bf16[32,12,4096]{2,1,0:T(8,128)(2,1)} %all-to-all-done.1) | data formatting | bytes 6291456 | tf_op jit(solution)/shard_map/reshape | solution.py:66
  261.5 2.6 fusion.32
  264.2 2.1 fusion.34
  266.4 0.7 fusion.8
  267.7 1.8 fusion.2
  269.4 2.3 copy.18
  271.7 4.1 multiply_reduce_fusion.1
  275.8 2.3 fusion.59
  278.1 1.4 convert_element_type.164
  279.5 9.8 %all-to-all-start.6 = ((bf16[32,1,12]{2,1,0:T(2,128)(2,1)}), bf16[32,1,12]{2,1,0:T(2,128)(2,1)}, u32[]{:S(2)}, u32[]{:S(2)}) async-start(bf16[32,1,12]{2,1,0:T(2,128)(2,1)} %convert_element_type.164), calls=%async_computation.6 | async-start | bytes 32768 | tf_op jit(solution)/shard_map/all_to_all | solution.py:104
  289.4 4.0 add_convert_fusion
  293.4 3.6 reshape.139
  297.0 0.8 all-to-all-done.6
  297.9 9.0 %all-to-all-start.5 = ((bf16[32,12,2048]{2,1,0:T(8,128)(2,1)}), bf16[32,12,2048]{2,1,0:T(8,128)(2,1)}, u32[]{:S(2)}, u32[]{:S(2)}) async-start(bf16[32,12,2048]{2,1,0:T(8,128)(2,1)} %reshape.139), calls=%async_computation.5 | async-start | bytes 4194304 | tf_op jit(solution)/shard_map/all_to_all | solution.py:103
  306.9 2.2 fusion.28
  309.1 1.8 fusion.1
  310.9 2.0 fusion.58
  313.0 1.8 add_convert_fusion.1
  314.8 3.6 reshape.134
  318.4 37.3 %all-to-all-done.5 = bf16[32,12,2048]{2,1,0:T(8,128)(2,1)} async-done(((bf16[32,12,2048]{2,1,0:T(8,128)(2,1)}), bf16[32,12,2048]{2,1,0:T(8,128)(2,1)}, u32[]{:S(2)}, u32[]{:S(2)}) %all-to-all-start.5) | async-done | bytes 1572896 | tf_op jit(solution)/shard_map/all_to_all | solution.py:103
  355.7 6.7 %all-to-all-start.2 = ((bf16[32,12,2048]{2,1,0:T(8,128)(2,1)}), bf16[32,12,2048]{2,1,0:T(8,128)(2,1)}, u32[]{:S(2)}, u32[]{:S(2)}) async-start(bf16[32,12,2048]{2,1,0:T(8,128)(2,1)} %reshape.134), calls=%async_computation.2 | async-start | bytes 4194304 | tf_op jit(solution)/shard_map/all_to_all | solution.py:103
  362.7 2.2 fusion.30
  364.9 1.7 fusion
  366.8 0.7 copy.20
  368.5 0.9 copy.19
  369.4 0.7 convert_element_type.161
  370.1 26.3 %reduce-scatter.8.cloned.1.call-done = bf16[128,256]{1,0:T(8,128)(2,1)} async-done(((bf16[2048,256]{1,0:T(8,128)(2,1)}), bf16[128,256]{1,0:T(8,128)(2,1)}) %reduce-scatter.8.cloned.1.call-update) | async-done | bytes 65552 | tf_op jit(solution)/shard_map/reduce_scatter | solution.py:128
  396.4 1.5 convert_element_type.157
  397.9 60.4 %reduce-scatter.6.cloned.1.call-done = bf16[128,256]{1,0:T(8,128)(2,1)} async-done(((bf16[2048,256]{1,0:T(8,128)(2,1)}), bf16[128,256]{1,0:T(8,128)(2,1)}) %reduce-scatter.6.cloned.1.call-update) | async-done | bytes 65552 | tf_op jit(solution)/shard_map/reduce_scatter | solution.py:125
  458.3 1.5 convert_element_type.155
  459.8 2.0 bitcast_reduce_fusion
  462.4 2.0 bitcast_reduce_fusion.1
  465.0 1.1 pad_maximum_fusion
  (75 shorter events, 5.4 us)
Async XLA Ops:
  9.2 28.4 %copy-start.14 = (s32[128]{0:T(128)}, s32[128]{0:T(128)S(1)}, u32[]{:S(2)}) copy-start(s32[128]{0:T(128)S(1)} %get-tuple-element.16) | copy-start | bytes 1540
  9.2 46.1 %copy-start.12 = (s32[128]{0:T(128)}, s32[128]{0:T(128)S(1)}, u32[]{:S(2)}) copy-start(s32[128]{0:T(128)S(1)} %get-tuple-element.15) | copy-start | bytes 1540
  10.8 21.9 %all-to-all-start = ((bf16[32,1,12]{2,1,0:T(2,128)(2,1)}), bf16[32,1,12]{2,1,0:T(2,128)(2,1)S(1)}, u32[]{:S(2)}, u32[]{:S(2)}) async-start(bf16[32,1,12]{2,1,0:T(2,128)(2,1)} %copy.14), calls=%async_computation | async-start | bytes 32768 | tf_op jit(solution)/shard_map/all_to_all | solution.py:54
  24.3 1.7 copy-start.16
  32.7 13.5 %all-to-all-start.3 = ((bf16[32,1,12]{2,1,0:T(2,128)(2,1)}), bf16[32,1,12]{2,1,0:T(2,128)(2,1)S(1)}, u32[]{:S(2)}, u32[]{:S(2)}) async-start(bf16[32,1,12]{2,1,0:T(2,128)(2,1)} %copy.15), calls=%async_computation.3 | async-start | bytes 32768 | tf_op jit(solution)/shard_map/all_to_all | solution.py:54
  48.7 98.2 %all-to-all-start.4 = ((bf16[32,12,4096]{2,1,0:T(8,128)(2,1)}), bf16[32,12,4096]{2,1,0:T(8,128)(2,1)}, u32[]{:S(2)}, u32[]{:S(2)}) async-start(bf16[32,12,4096]{2,1,0:T(8,128)(2,1)} %bitcast.81), calls=%async_computation.4 | async-start | bytes 8388608 | tf_op jit(solution)/shard_map/all_to_all | solution.py:53
  54.6 107.9 %all-gather.8.cloned.1.call-start = ((), (), s32[]{:S(2)}) async-start(), calls=%async_computation.13 | async-start | bytes 1114112 | tf_op jit(solution)/shard_map/all_gather | solution.py:40
  149.4 98.8 %all-to-all-start.1 = ((bf16[32,12,4096]{2,1,0:T(8,128)(2,1)}), bf16[32,12,4096]{2,1,0:T(8,128)(2,1)}, u32[]{:S(2)}, u32[]{:S(2)}) async-start(bf16[32,12,4096]{2,1,0:T(8,128)(2,1)} %bitcast.80), calls=%async_computation.1 | async-start | bytes 8388608 | tf_op jit(solution)/shard_map/all_to_all | solution.py:53
  156.1 44.9 %all-gather.6.cloned.1.call-start = ((), (), s32[]{:S(2)}) async-start(), calls=%async_computation.12 | async-start | bytes 1114112 | tf_op jit(solution)/shard_map/all_gather | solution.py:41
  156.8 85.4 %all-gather.4.cloned.1.call-start = ((), (), s32[]{:S(2)}) async-start(), calls=%async_computation.11 | async-start | bytes 1114112 | tf_op jit(solution)/shard_map/all_gather | solution.py:43
  158.5 83.8 %copy-start.9 = (f32[384]{0:T(512)}, f32[384]{0:T(512)S(1)}, u32[]{:S(2)}) copy-start(f32[384]{0:T(512)S(1)} %reshape.147) | copy-start | bytes 4612
  248.2 31.4 %all-to-all-start.7 = ((bf16[32,1,12]{2,1,0:T(2,128)(2,1)}), bf16[32,1,12]{2,1,0:T(2,128)(2,1)S(1)}, u32[]{:S(2)}, u32[]{:S(2)}) async-start(bf16[32,1,12]{2,1,0:T(2,128)(2,1)} %convert_element_type.165), calls=%async_computation.7 | async-start | bytes 32768 | tf_op jit(solution)/shard_map/all_to_all | solution.py:104
  255.7 112.7 %reduce-scatter.10.cloned.1.call-start = ((), (), s32[]{:S(2)}) async-start(), calls=%async_computation.16 | async-start | bytes 1114112
  261.5 2.7 copy-start
  264.2 3.0 copy-start.7
  264.2 2.2 copy-start.11
  266.4 0.8 copy-start.8
  266.4 1.1 copy-start.5
  266.4 1.2 copy-start.6
  266.4 1.2 copy-start.10
  271.7 4.1 copy-start.1
  279.5 18.3 %all-to-all-start.6 = ((bf16[32,1,12]{2,1,0:T(2,128)(2,1)}), bf16[32,1,12]{2,1,0:T(2,128)(2,1)}, u32[]{:S(2)}, u32[]{:S(2)}) async-start(bf16[32,1,12]{2,1,0:T(2,128)(2,1)} %convert_element_type.164), calls=%async_computation.6 | async-start | bytes 32768 | tf_op jit(solution)/shard_map/all_to_all | solution.py:104
  297.9 57.8 %all-to-all-start.5 = ((bf16[32,12,2048]{2,1,0:T(8,128)(2,1)}), bf16[32,12,2048]{2,1,0:T(8,128)(2,1)}, u32[]{:S(2)}, u32[]{:S(2)}) async-start(bf16[32,12,2048]{2,1,0:T(8,128)(2,1)} %reshape.139), calls=%async_computation.5 | async-start | bytes 4194304 | tf_op jit(solution)/shard_map/all_to_all | solution.py:103
  306.9 89.5 %reduce-scatter.8.cloned.1.call-start = ((), (), s32[]{:S(2)}) async-start(), calls=%async_computation.15 | async-start | bytes 1114112 | tf_op jit(solution)/shard_map/reduce_scatter | solution.py:128
  310.9 2.1 copy-start.2
  310.9 2.1 copy-start.4
  318.4 44.3 %copy-start.3 = (bf16[384,256]{0,1:T(8,128)(2,1)S(1)}, bf16[384,256]{0,1:T(8,128)(2,1)}, u32[]{:S(2)}) copy-start(bf16[384,256]{0,1:T(8,128)(2,1)} %get-tuple-element.6) | copy-start | bytes 589828
  355.7 106.8 %all-to-all-start.2 = ((bf16[32,12,2048]{2,1,0:T(8,128)(2,1)}), bf16[32,12,2048]{2,1,0:T(8,128)(2,1)}, u32[]{:S(2)}, u32[]{:S(2)}) async-start(bf16[32,12,2048]{2,1,0:T(8,128)(2,1)} %reshape.134), calls=%async_computation.2 | async-start | bytes 4194304 | tf_op jit(solution)/shard_map/all_to_all | solution.py:103
  362.4 96.0 %reduce-scatter.6.cloned.1.call-start = ((), (), s32[]{:S(2)}) async-start(), calls=%async_computation.14 | async-start | bytes 1114112 | tf_op jit(solution)/shard_map/reduce_scatter | solution.py:125
  364.8 2.8 copy-start.15
  364.8 2.9 copy-start.13
Sparse Core Ops, SparseCore 0:
  57.5 41.9 all-gather.7
  159.0 41.8 all-gather.5
  203.0 39.1 all-gather.3
  271.8 60.4 reduce-scatter.9
  335.2 61.1 reduce-scatter.7
  399.6 58.6 reduce-scatter.5
where the time goes:
time: 475 us; the launch traced here: 473 us
  waiting for transfers between devices  302 us (64%)
  starting transfers between devices  64.7 us (14%)
  matrix products  42.5 us (9%)
  local copies, waits for them, and re-layouts  38.2 us (8%)
  between operations  14.6 us (3%)
  other arithmetic  10.9 us (2%)
    all_to_all x2, waiting for transfers between devices, local(): lax.all_to_all(packed, 'expert', split_axis=0, concat_axis=0, tiled=True)  90.5 us
    reduce_scatter x1, waiting for transfers between devices, local(): lax.psum_scatter(acc_gate.astype(jnp.bfloat16), 'dp', scatter_dimension=0...  60.4 us
    all_gather x1, waiting for transfers between devices, local(): down_full = lax.all_gather(w_down, 'dp', axis=1, tiled=True)  38.6 us
    all_to_all x2, waiting for transfers between devices, local(): lax.all_to_all(input_part, 'expert', split_axis=0, concat_axis=0, tiled=T...  37.3 us
    all_gather x1, waiting for transfers between devices, local(): lax.all_gather(w_up, 'dp', axis=0, tiled=True)  35.7 us
    reduce_scatter x1, waiting for transfers between devices, local(): lax.psum_scatter(acc_up.astype(jnp.bfloat16), 'dp', scatter_dimension=0,...  26.3 us
    all_to_all x2, starting transfers between devices, local(): lax.all_to_all(scales, 'expert', split_axis=0, concat_axis=0, tiled=True)  18.4 us
    all_to_all x2, starting transfers between devices, local(): lax.all_to_all(gate_part, 'expert', split_axis=0, concat_axis=0, tiled=True)  17.4 us
  transfers between devices with their start and end apart: 14, of which 10 were waited for; matrix products, arithmetic and copies ran while one was open for 17% of the time, Pallas kernels for 0%

commit v1 on v0

v1 whole, which is shorter than its diff:
```python
import functools

import jax
import jax.numpy as jnp
from jax import lax
from jax.experimental import pallas as pl
from jax.experimental.pallas import tpu as pltpu
from jax.sharding import Mesh
from jax.sharding import PartitionSpec as P

VMEM_LIMIT = 48 * 1024 * 1024
CONTRACT_ROWS = (((0,), (0,)), ((), ()))
CONTRACT_COLS = (((1,), (1,)), ((), ()))


def whole(memory_space=pltpu.VMEM):
    return pl.BlockSpec(memory_space=memory_space)


def cost(flops, moved):
    return pl.CostEstimate(flops=flops, bytes_accessed=moved, transcendentals=0)


def slot_match(route, experts, capacity):
    layers, tokens = route.shape
    span = layers * capacity
    upto = (
        lax.broadcasted_iota(jnp.int32, (tokens, tokens), 0)
        <= lax.broadcasted_iota(jnp.int32, (tokens, tokens), 1)
    ).astype(jnp.bfloat16)
    numbers = lax.broadcasted_iota(jnp.int32, (experts, tokens), 0)
    keys = []
    for layer in range(layers):
        row = route[layer : layer + 1, :]
        onehot = (numbers == row).astype(jnp.float32)
        ranks = jnp.dot(onehot.astype(jnp.bfloat16), upto, preferred_element_type=jnp.float32)
        rank = jnp.sum(onehot * ranks, axis=0, keepdims=True).astype(jnp.int32) - 1
        key = row * span + layer * capacity + rank
        keys.append(jnp.where(rank < capacity, key, -1))
    key = jnp.concatenate(keys, axis=1)
    slots = lax.broadcasted_iota(jnp.int32, (experts * span, layers * tokens), 0)
    return slots == key


def pack_kernel(x_ref, dy_ref, gate_ref, route_ref, out_ref, table_ref, *, capacity):
    layers, tokens, columns = x_ref.shape
    experts = out_ref.shape[0] // (layers * capacity)
    step = pl.program_id(0)

    @pl.when(step == 0)
    def _():
        table_ref[...] = slot_match(route_ref[...], experts, capacity).astype(jnp.bfloat16)

    @pl.when(step == 2)
    def _():
        scale = jnp.concatenate([gate_ref[layer : layer + 1, :] for layer in range(layers)], axis=1)
        table_ref[...] = table_ref[...] * scale

    def fill(src_ref):
        got = jnp.dot(
            table_ref[...],
            src_ref[...].reshape(layers * tokens, columns),
            preferred_element_type=jnp.float32,
        )
        out_ref[...] = got.astype(jnp.bfloat16)

    pl.when(step < 2)(lambda: fill(x_ref))
    pl.when(step >= 2)(lambda: fill(dy_ref))


def fixed(shape):
    return pl.BlockSpec(shape, lambda t: (0,) * len(shape))


def pack(x, dy, gates, route, experts, capacity):
    layers, tokens, width = x.shape
    rows, half = experts * layers * capacity, width // 2
    block = (layers, tokens, half)
    return pl.pallas_call(
        functools.partial(pack_kernel, capacity=capacity),
        grid=(4,),
        out_shape=jax.ShapeDtypeStruct((rows, 2 * width), jnp.bfloat16),
        in_specs=[
            pl.BlockSpec(block, lambda t: (0, 0, jnp.minimum(t, 1))),
            pl.BlockSpec(block, lambda t: (0, 0, jnp.maximum(t - 2, 0))),
            fixed(gates.shape),
            fixed(route.shape),
        ],
        out_specs=pl.BlockSpec((rows, half), lambda t: (0, t)),
        scratch_shapes=[pltpu.VMEM((rows, layers * tokens), jnp.bfloat16)],
        compiler_params=pltpu.CompilerParams(vmem_limit_bytes=VMEM_LIMIT),
        cost_estimate=cost(2 * rows * layers * tokens * 2 * width, 5 << 20),
        name="pack",
    )(x, dy, gates, route)


def forward_kernel(core_ref, recv_ref, weight_ref, grads_ref, hidden_ref, gate_ref, term_ref):
    width, columns = weight_ref.shape
    unit = columns // 6
    gate_sum = 0.0
    for part in range(2):
        base = part * 3 * unit
        pre = jnp.dot(
            recv_ref[:, :width],
            weight_ref[:, base : base + 2 * unit],
            preferred_element_type=jnp.float32,
        )
        back = jnp.dot(
            recv_ref[:, width:],
            weight_ref[:, base + 2 * unit : base + 3 * unit],
            preferred_element_type=jnp.float32,
        )
        gate_pre, up_value = pre[:, :unit], pre[:, unit:]
        sigmoid = jax.nn.sigmoid(gate_pre)
        swish = gate_pre * sigmoid
        hidden = swish * up_value
        gate_sum = gate_sum + jnp.sum(hidden * back, axis=1, keepdims=True)
        grad_pre = back * up_value * sigmoid * (1.0 + gate_pre * (1.0 - sigmoid))
        grads_ref[:, 2 * part * unit : (2 * part + 1) * unit] = grad_pre.astype(jnp.bfloat16)
        grads_ref[:, (2 * part + 1) * unit : (2 * part + 2) * unit] = (back * swish).astype(
            jnp.bfloat16
        )
        hidden_ref[:, part * unit : (part + 1) * unit] = hidden.astype(jnp.bfloat16)
    gate_ref[...] = jnp.broadcast_to(gate_sum, gate_ref.shape).astype(jnp.bfloat16)
    weight_terms(recv_ref, grads_ref, hidden_ref, 1 - core_ref[0], term_ref, None)


def weight_terms(recv_ref, grads_ref, hidden_ref, side, out_ref, add_ref):
    half, columns = out_ref.shape
    unit = columns // 6
    piece = 128

    @pl.loop(0, half // (2 * piece))
    def _(at):
        rows = pl.ds(pl.multiple_of(at * 2 * piece, 2 * piece), 2 * piece)

        def pick(offset):
            first = pl.multiple_of(offset + (4 * at + side) * piece, piece)
            second = pl.multiple_of(offset + (4 * at + 2 + side) * piece, piece)
            return jnp.concatenate(
                [recv_ref[:, pl.ds(first, piece)], recv_ref[:, pl.ds(second, piece)]], axis=1
            )

        up = lax.dot_general(
            pick(0), grads_ref[...], CONTRACT_ROWS, preferred_element_type=jnp.float32
        )
        down = lax.dot_general(
            pick(2 * half), hidden_ref[...], CONTRACT_ROWS, preferred_element_type=jnp.float32
        )
        for part in range(2):
            base = part * 3 * unit
            first = up[:, 2 * part * unit : (2 * part + 2) * unit]
            second = down[:, part * unit : (part + 1) * unit]
            if add_ref is not None:
                first = first + add_ref[rows, base : base + 2 * unit].astype(jnp.float32)
                second = second + add_ref[rows, base + 2 * unit : base + 3 * unit].astype(jnp.float32)
            out_ref[rows, base : base + 2 * unit] = first.astype(jnp.bfloat16)
            out_ref[rows, base + 2 * unit : base + 3 * unit] = second.astype(jnp.bfloat16)


def forward(core, recv, weights):
    rows = recv.shape[0]
    width, columns = weights.shape
    return pl.pallas_call(
        forward_kernel,
        out_shape=(
            jax.ShapeDtypeStruct((rows, columns // 6 * 4), jnp.bfloat16),
            jax.ShapeDtypeStruct((rows, columns // 3), jnp.bfloat16),
            jax.ShapeDtypeStruct((rows, 128), jnp.bfloat16),
            jax.ShapeDtypeStruct((width // 2, columns), jnp.bfloat16),
        ),
        in_specs=[whole(pltpu.SMEM), whole(), whole()],
        out_specs=(whole(),) * 4,
        compiler_params=pltpu.CompilerParams(vmem_limit_bytes=VMEM_LIMIT),
        cost_estimate=cost(3 * rows * width * columns, 14 << 20),
        name="forward",
    )(core, recv, weights)


def input_kernel(grads_ref, weight_ref, gate_ref, out_ref):
    width, columns = weight_ref.shape
    unit = columns // 6
    chunk = min(256, width)

    @pl.loop(0, width // chunk)
    def _(at):
        start = pl.ds(pl.multiple_of(at * chunk, chunk), chunk)
        got = 0.0
        for part in range(2):
            got = got + lax.dot_general(
                grads_ref[:, 2 * part * unit : (2 * part + 2) * unit],
                weight_ref[start, 3 * part * unit : (3 * part + 2) * unit],
                CONTRACT_COLS,
                preferred_element_type=jnp.float32,
            )
        out_ref[:, start] = got.astype(jnp.bfloat16)

    out_ref[:, width:] = gate_ref[...]


def input_terms(grads, weights, gate):
    rows = grads.shape[0]
    width, columns = weights.shape
    return pl.pallas_call(
        input_kernel,
        out_shape=jax.ShapeDtypeStruct((rows, width + gate.shape[1]), jnp.bfloat16),
        in_specs=[whole()] * 3,
        out_specs=whole(),
        compiler_params=pltpu.CompilerParams(vmem_limit_bytes=VMEM_LIMIT),
        cost_estimate=cost(4 * rows * width * columns // 3, 9 << 20),
        name="input_terms",
    )(grads, weights, gate)


def own_kernel(core_ref, recv_ref, grads_ref, hidden_ref, arrived_ref, out_ref):
    weight_terms(recv_ref, grads_ref, hidden_ref, core_ref[0], out_ref, arrived_ref)


def own_terms(core, recv, grads, hidden, arrived):
    rows = recv.shape[0]
    half, columns = arrived.shape
    return pl.pallas_call(
        own_kernel,
        out_shape=jax.ShapeDtypeStruct((half, columns), jnp.bfloat16),
        in_specs=[whole(pltpu.SMEM)] + [whole()] * 4,
        out_specs=whole(),
        compiler_params=pltpu.CompilerParams(vmem_limit_bytes=VMEM_LIMIT),
        cost_estimate=cost(2 * rows * half * columns, 10 << 20),
        name="own_terms",
    )(core, recv, grads, hidden, arrived)


def unpack_kernel(back_ref, sum_ref, gate_ref, route_ref, out_ref, gate_out_ref, table_ref, *, capacity):
    layers, tokens = route_ref.shape
    experts = back_ref.shape[0] // (layers * capacity)

    @pl.when(pl.program_id(0) == 0)
    def _():
        match = slot_match(route_ref[...], experts, capacity)
        table_ref[...] = match.astype(jnp.bfloat16)
        sums = sum_ref[:, 0:1].astype(jnp.float32)
        picked = jnp.sum(jnp.where(match, sums, 0.0), axis=0, keepdims=True)
        for layer in range(layers):
            gate = gate_ref[layer : layer + 1, :].astype(jnp.float32)
            value = picked[:, layer * tokens : (layer + 1) * tokens] / gate
            gate_out_ref[layer : layer + 1, :] = value.astype(jnp.bfloat16)

    got = lax.dot_general(
        table_ref[...], back_ref[...], CONTRACT_ROWS, preferred_element_type=jnp.float32
    ).astype(jnp.bfloat16)
    out_ref[...] = got.reshape(out_ref.shape)


def unpack(back, gates, route, capacity):
    rows, columns = back.shape
    layers, tokens = route.shape
    width = columns - 128
    steps = 4
    block = width // steps
    return pl.pallas_call(
        functools.partial(unpack_kernel, capacity=capacity),
        grid=(steps,),
        out_shape=(
            jax.ShapeDtypeStruct((layers, tokens, width), jnp.bfloat16),
            jax.ShapeDtypeStruct((layers, tokens), jnp.bfloat16),
        ),
        in_specs=[
            pl.BlockSpec((rows, block), lambda t: (0, t)),
            pl.BlockSpec((rows, 128), lambda t: (0, width // 128)),
            fixed(gates.shape),
            fixed(route.shape),
        ],
        out_specs=(
            pl.BlockSpec((layers, tokens, block), lambda t: (0, 0, t)),
            fixed((layers, tokens)),
        ),
        scratch_shapes=[pltpu.VMEM((rows, layers * tokens), jnp.bfloat16)],
        compiler_params=pltpu.CompilerParams(vmem_limit_bytes=VMEM_LIMIT),
        cost_estimate=cost(2 * rows * layers * tokens * width, 3 << 20),
        name="unpack",
    )(back, back, gates, route)


def local(inputs, cotangents, gates, routing, w_gate, w_up, w_down):
    experts = lax.axis_size("e")
    layers, tokens, width = inputs.shape
    capacity = 3 * tokens // (2 * experts)
    unit = w_gate.shape[1]
    route = routing[:, :, 0]
    core = lax.axis_index("c").astype(jnp.int32).reshape(1)
    swap = [(0, 1), (1, 0)]

    mine = jnp.concatenate([w_gate, w_up, w_down.T], axis=1)
    both = jnp.concatenate([mine, lax.ppermute(mine, "k", swap)], axis=1)
    weights = lax.all_gather(both, ("y", "c"), axis=0, tiled=True)

    sent = pack(inputs, cotangents, gates, route, experts, capacity)
    recv = lax.all_to_all(
        sent.reshape(experts, layers * capacity, 2 * width), "e", 0, 0, tiled=True
    ).reshape(experts * layers * capacity, 2 * width)

    grads, hidden, gate_sum, term = forward(core, recv, weights)
    arrived = lax.ppermute(term, "c", swap)
    back = input_terms(grads, weights, gate_sum)
    total = own_terms(core, recv, grads, hidden, arrived)
    total, back = lax.optimization_barrier((total, back))
    reduced = lax.psum_scatter(total, "y", scatter_dimension=0, tiled=True)
    back = lax.all_to_all(
        back.reshape(experts, layers * capacity, back.shape[1]), "e", 0, 0, tiled=True
    ).reshape(back.shape)
    grad_inputs, grad_gates = unpack(back, gates, route, capacity)
    reduced, grad_gates = lax.optimization_barrier((reduced, grad_gates))

    partner = lax.ppermute(reduced[:, 3 * unit :], "k", swap)
    final = reduced[:, : 3 * unit].astype(jnp.float32) + partner.astype(jnp.float32)
    return (
        grad_inputs,
        grad_gates,
        final[:, :unit],
        final[:, unit : 2 * unit],
        final[:, 2 * unit :].T,
    )


def solution(mesh):
    count, peers = mesh.devices.shape
    fine = Mesh(mesh.devices.reshape(count // 2, 2, peers // 2, 2), ("y", "c", "e", "k"))
    dp, expert, both = ("y", "c"), ("e", "k"), ("y", "c", "e", "k")
    return jax.shard_map(
        local,
        mesh=fine,
        in_specs=(
            P(None, both, None),
            P(None, both, None),
            P(None, both),
            P(None, both, None),
            P(dp, expert),
            P(dp, expert),
            P(expert, dp),
        ),
        out_specs=(
            P(None, both, None),
            P(None, both),
            P(dp, expert),
            P(dp, expert),
            P(expert, dp),
        ),
        check_vma=False,
    )
```

time: 475 us -> 210 us (0.44)
  the two profiles are of different devices: /device:TPU:2 before, /device:TPU:40 now
where the time goes in v1:
time: 210 us
  waiting for transfers between devices  83.7 us (40%)
  blocking collectives  48.7 us (23%)
  Pallas kernels  28.4 us (14%)
  starting transfers between devices  20.8 us (10%)
  between operations  14.1 us (7%)
  local copies, waits for them, and re-layouts  10.5 us (5%)
  other arithmetic  3.5 us (2%)
    all_to_all x1, waiting for transfers between devices, local(): lax.all_to_all(sent.reshape(experts, layers * capacity, 2 * width), 'e',...  73.5 us
    all_to_all x1, blocking collectives, local(): lax.all_to_all(back.reshape(experts, layers * capacity, back.shape[1]), '...  48.7 us
    all_to_all x1, starting transfers between devices, local(): lax.all_to_all(sent.reshape(experts, layers * capacity, 2 * width), 'e',...  12.9 us
    pallas_call x1, Pallas kernels, forward(): pl.pallas_call(forward_kernel, out_shape=(jax.ShapeDtypeStruct((rows, col...  9.03 us
    unnamed x18, local copies, waits for them, and re-layouts  8.87 us
    pallas_call x1, Pallas kernels, own_terms(): pl.pallas_call(own_kernel, out_shape=jax.ShapeDtypeStruct((half, columns)...  6.99 us
    pallas_call x1, Pallas kernels, input_terms(): pl.pallas_call(input_kernel, out_shape=jax.ShapeDtypeStruct((rows, width...  6.06 us
    ppermute x1, waiting for transfers between devices, local(): both = jnp.concatenate([mine, lax.ppermute(mine, 'k', swap)], axis=1)  5.13 us
  transfers between devices with their start and end apart: 6, of which 3 were waited for; matrix products, arithmetic and copies ran while one was open for 0% of the time, Pallas kernels for 6%

profile of v1, /device:TPU:40, one launch (start us, length us, event | category | flops | bytes accessed | tf_op | source)
XLA Modules:
  0.0 209.8 jit_solution(16270795208059892871)
XLA Ops:
  7.2 0.0 all-gather.2.cloned.1.call-start
  7.2 0.9 copy.12
  8.2 0.9 pad_maximum_fusion.1
  9.0 3.4 %collective-permute-start = (bf16[128,768]{1,0:T(8,128)(2,1)S(1)}, bf16[128,768]{1,0:T(8,128)(2,1)S(1)}, u32[]{:S(2)}, u32[]{:S(2)}) collective-permute-start(bf16[128,768]{1,0:T(8,128)(2,1)S(1)} %pad_maximum_fusion.1), channel_id=1, source_target_pairs={{0,1},{1,0},{2,3},{3,2},{4,5},{5,4},{6,7},{7,6},{8,9},{9,8},{10,11... | collective-permute-start | bytes 589832 | tf_op jit(solution)/shard_map/ppermute | solution.py:294
  12.5 5.1 %collective-permute-done = bf16[128,768]{1,0:T(8,128)(2,1)S(1)} collective-permute-done((bf16[128,768]{1,0:T(8,128)(2,1)S(1)}, bf16[128,768]{1,0:T(8,128)(2,1)S(1)}, u32[]{:S(2)}, u32[]{:S(2)}) %collective-permute-start) | collective-permute-done | bytes 196640 | tf_op jit(solution)/shard_map/ppermute | solution.py:294
  17.6 1.6 pad_maximum_fusion
  19.2 0.0 all-gather.2.cloned.1.call-update
  19.2 0.0 copy-start
  19.3 1.2 copy-done
  20.5 0.0 copy-start.1
  20.5 1.2 copy-done.1
  21.7 0.0 copy-start.2
  21.7 0.7 copy-done.2
  22.4 0.0 copy-start.4
  22.4 0.7 copy-done.4
  23.0 3.5 %pack.1 = bf16[384,4096]{1,0:T(8,128)(2,1)} custom-call(bf16[2,128,2048]{2,1,0:T(8,128)(2,1)S(1)} %copy-done, bf16[2,128,2048]{2,1,0:T(8,128)(2,1)S(1)} %copy-done.1, bf16[2,128]{1,0:T(2,128)(2,1)S(1)} %copy-done.4, s32[2,128]{1,0:T(2,128)S(1)} %bitcast.12), custom_call_target="tpu_custom_call" | custom-call | flops 805306368 | bytes 5242880 | tf_op jit(solution)/shard_map/pack/pallas_call | solution.py:79
  26.5 12.9 %all-to-all-start = ((bf16[16,24,4096]{2,1,0:T(8,128)(2,1)}), bf16[16,24,4096]{2,1,0:T(8,128)(2,1)S(1)}, u32[]{:S(2)}, u32[]{:S(2)}) async-start(bf16[16,24,4096]{2,1,0:T(8,128)(2,1)} %bitcast.2), calls=%async_computation | async-start | bytes 6291456 | tf_op jit(solution)/shard_map/all_to_all | solution.py:298
  39.4 0.0 reduce-scatter.2.cloned.1.call-start
  39.5 73.5 %all-to-all-done = bf16[16,24,4096]{2,1,0:T(8,128)(2,1)S(1)} async-done(((bf16[16,24,4096]{2,1,0:T(8,128)(2,1)}), bf16[16,24,4096]{2,1,0:T(8,128)(2,1)S(1)}, u32[]{:S(2)}, u32[]{:S(2)}) %all-to-all-start) | async-done | bytes 3145760 | tf_op jit(solution)/shard_map/all_to_all | solution.py:298
  113.0 0.0 copy-start.6
  113.0 0.0 all-gather.2.cloned.1.call-done.weight_ref
  113.0 1.7 copy-done.6
  114.7 9.0 %forward.1 = (bf16[384,1024]{1,0:T(8,128)(2,1)S(1)}, bf16[384,512]{1,0:T(8,128)(2,1)S(1)}, bf16[384,128]{1,0:T(8,128)(2,1)S(1)}, bf16[1024,1536]{1,0:T(8,128)(2,1)S(1)}) custom-call(s32[1]{0:T(128)} %bitcast.core_ref, bf16[384,4096]{1,0:T(8,128)(2,1)} %bitcast.14, bf16[2048,1536]{1,0:T(8,128)(2,1)} %all-gather.2.cloned.1.call-done.weight_ref), custom_call_target="tpu_custom_call" | custom-call | flops 3623878656 | bytes 14680064 | tf_op jit(solution)/shard_map/forward/pallas_call | solution.py:164
  123.7 1.9 collective-permute-start.1
  125.7 6.1 %input_terms.1 = bf16[384,2176]{1,0:T(8,128)(2,1)S(1)} custom-call(bf16[384,1024]{1,0:T(8,128)(2,1)S(1)} %get-tuple-element.15.grads_ref, bf16[2048,1536]{1,0:T(8,128)(2,1)} %all-gather.2.cloned.1.call-done.weight_ref, bf16[384,128]{1,0:T(8,128)(2,1)S(1)} %get-tuple-element.18.gate_ref), custom_call_target="tpu_custom_call" | custom-call | flops 1610612736 | bytes 9437184 | tf_op jit(solution)/shard_map/input_terms/pallas_call | solution.py:204
  131.7 0.0 collective-permute-done.1.arrived_ref
  131.7 0.0 copy-start.7
  131.7 1.7 copy-done.7
  133.4 7.0 %own_terms.1 = bf16[1024,1536]{1,0:T(8,128)(2,1)} custom-call(s32[1]{0:T(128)} %bitcast.core_ref, bf16[384,4096]{1,0:T(8,128)(2,1)} %bitcast.15, bf16[384,1024]{1,0:T(8,128)(2,1)S(1)} %get-tuple-element.15.grads_ref, bf16[384,512]{1,0:T(8,128)(2,1)S(1)} %get-tuple-element.16.hidden_ref, bf16[1024,1536]{1,0:T(8,128)(2,1)} %copy-done.7), custom_call_target="tpu_custom_call" | custom-call | flops 1207959552 | bytes 10485760 | tf_op jit(solution)/shard_map/own_terms/pallas_call | solution.py:222
  140.4 0.0 copy-start.3
  140.4 0.0 copy-start.5
  140.4 0.0 reduce-scatter.2.cloned.1.call-update
  140.4 48.7 %all_to_all.10 = bf16[16,24,2176]{2,1,0:T(8,128)(2,1)S(1)} all-to-all(bf16[16,24,2176]{2,1,0:T(8,128)(2,1)S(1)} %bitcast.11), channel_id=1, replica_groups=mesh['y'=8,'c'=2,'e'=16,'k'=2] {'e'}, dimensions={0} | all-to-all | bytes 3342336 | tf_op jit(solution)/shard_map/all_to_all | solution.py:308
  189.1 0.0 copy-done.3
  189.1 0.0 copy-done.5
  189.1 2.9 %unpack.1 = (bf16[2,128,2048]{2,1,0:T(8,128)(2,1)}, bf16[2,128]{1,0:T(2,128)(2,1)}) custom-call(bf16[384,2176]{1,0:T(8,128)(2,1)S(1)} %bitcast.9, bf16[384,2176]{1,0:T(8,128)(2,1)S(1)} %bitcast.10, bf16[2,128]{1,0:T(2,128)(2,1)S(1)} %copy-done.5, s32[2,128]{1,0:T(2,128)S(1)} %bitcast.13), custom_call_target="tpu_custom_call" | custom-call | flops 402653184 | bytes 3145728 | tf_op jit(solution)/shard_map/unpack/pallas_call | solution.py:260
  192.0 0.0 reduce-scatter.2.cloned.1.call-done
  192.0 0.9 slice.16
  192.9 2.5 %collective-permute-start.2 = (bf16[128,768]{1,0:T(8,128)(2,1)S(1)}, bf16[128,768]{1,0:T(8,128)(2,1)S(1)}, u32[]{:S(2)}, u32[]{:S(2)}) collective-permute-start(bf16[128,768]{1,0:T(8,128)(2,1)S(1)} %slice.16), channel_id=1, source_target_pairs={{0,1},{1,0},{2,3},{3,2},{4,5},{5,4},{6,7},{7,6},{8,9},{9,8},{10,11... | collective-permute-start | bytes 589832 | tf_op jit(solution)/shard_map/ppermute | solution.py:314
  195.4 5.1 %collective-permute-done.2 = bf16[128,768]{1,0:T(8,128)(2,1)S(1)} collective-permute-done((bf16[128,768]{1,0:T(8,128)(2,1)S(1)}, bf16[128,768]{1,0:T(8,128)(2,1)S(1)}, u32[]{:S(2)}, u32[]{:S(2)}) %collective-permute-start.2) | collective-permute-done | bytes 196640 | tf_op jit(solution)/shard_map/ppermute | solution.py:314
  200.5 1.0 convert_add_fusion
  201.5 0.7 slice_bitcast_fusion
  202.2 0.8 copy.13
Async XLA Ops:
  7.2 105.8 %all-gather.2.cloned.1.call-start = ((), (), s32[]{:S(2)}) async-start(), calls=%async_computation.3 | async-start | bytes 6684672 | tf_op jit(solution)/shard_map/all_gather | solution.py:295
  9.0 8.5 %collective-permute-start = (bf16[128,768]{1,0:T(8,128)(2,1)S(1)}, bf16[128,768]{1,0:T(8,128)(2,1)S(1)}, u32[]{:S(2)}, u32[]{:S(2)}) collective-permute-start(bf16[128,768]{1,0:T(8,128)(2,1)S(1)} %pad_maximum_fusion.1), channel_id=1, source_target_pairs={{0,1},{1,0},{2,3},{3,2},{4,5},{5,4},{6,7},{7,6},{8,9},{9,8},{10,11... | collective-permute-start | bytes 589832 | tf_op jit(solution)/shard_map/ppermute | solution.py:294
  19.2 1.2 copy-start
  20.5 1.2 copy-start.1
  21.7 0.7 copy-start.2
  22.4 0.7 copy-start.4
  26.5 86.4 %all-to-all-start = ((bf16[16,24,4096]{2,1,0:T(8,128)(2,1)}), bf16[16,24,4096]{2,1,0:T(8,128)(2,1)S(1)}, u32[]{:S(2)}, u32[]{:S(2)}) async-start(bf16[16,24,4096]{2,1,0:T(8,128)(2,1)} %bitcast.2), calls=%async_computation | async-start | bytes 6291456 | tf_op jit(solution)/shard_map/all_to_all | solution.py:298
  39.4 152.6 %reduce-scatter.2.cloned.1.call-start = ((), (), s32[]{:S(2)}) async-start(), calls=%async_computation.4 | async-start | bytes 3538944 | tf_op jit(solution)/shard_map/reduce_scatter | solution.py:307
  113.0 1.7 copy-start.6
  123.7 8.0 %collective-permute-start.1 = (bf16[1024,1536]{1,0:T(8,128)(2,1)S(1)}, bf16[1024,1536]{1,0:T(8,128)(2,1)S(1)}, u32[]{:S(2)}, u32[]{:S(2)}) collective-permute-start(bf16[1024,1536]{1,0:T(8,128)(2,1)S(1)} %get-tuple-element.17), channel_id=1, source_target_pairs={{0,32},{32,0},{1,33},{33,1},{2,34},{34,2},{3,35},{35,3},{4,36},{36... | collective-permute-start | bytes 9437192 | tf_op jit(solution)/shard_map/ppermute | solution.py:303
  131.7 1.7 copy-start.7
  140.4 48.7 %copy-start.3 = (s32[2,128,1]{1,2,0:T(1,128)S(1)}, s32[2,128,1]{1,2,0:T(1,128)}, u32[]{:S(2)}) copy-start(s32[2,128,1]{1,2,0:T(1,128)} %param.10) | copy-start | bytes 3076
  140.4 48.7 %copy-start.5 = (bf16[2,128]{1,0:T(2,128)(2,1)S(1)}, bf16[2,128]{1,0:T(2,128)(2,1)}, u32[]{:S(2)}) copy-start(bf16[2,128]{1,0:T(2,128)(2,1)} %gate_ref.3) | copy-start | bytes 1540
  192.9 7.6 %collective-permute-start.2 = (bf16[128,768]{1,0:T(8,128)(2,1)S(1)}, bf16[128,768]{1,0:T(8,128)(2,1)S(1)}, u32[]{:S(2)}, u32[]{:S(2)}) collective-permute-start(bf16[128,768]{1,0:T(8,128)(2,1)S(1)} %slice.16), channel_id=1, source_target_pairs={{0,1},{1,0},{2,3},{3,2},{4,5},{5,4},{6,7},{7,6},{8,9},{9,8},{10,11... | collective-permute-start | bytes 589832 | tf_op jit(solution)/shard_map/ppermute | solution.py:314
Sparse Core Ops, SparseCore 0:
  19.4 51.1 all-gather.1
  140.6 43.2 reduce-scatter.1

commit v2 on v1

--- a/solution.py
+++ b/solution.py
@@ -8,7 +8,8 @@
 from jax.sharding import Mesh
 from jax.sharding import PartitionSpec as P
 
-VMEM_LIMIT = 48 * 1024 * 1024
+MIB = 1024 * 1024
+PACK_LIMIT = 56 * MIB
 CONTRACT_ROWS = (((0,), (0,)), ((), ()))
 CONTRACT_COLS = (((1,), (1,)), ((), ()))
 
@@ -42,30 +43,33 @@
     return slots == key
 
 
-def pack_kernel(x_ref, dy_ref, gate_ref, route_ref, out_ref, table_ref, *, capacity):
-    layers, tokens, columns = x_ref.shape
-    experts = out_ref.shape[0] // (layers * capacity)
-    step = pl.program_id(0)
-
-    @pl.when(step == 0)
-    def _():
-        table_ref[...] = slot_match(route_ref[...], experts, capacity).astype(jnp.bfloat16)
-
-    @pl.when(step == 2)
-    def _():
-        scale = jnp.concatenate([gate_ref[layer : layer + 1, :] for layer in range(layers)], axis=1)
-        table_ref[...] = table_ref[...] * scale
-
-    def fill(src_ref):
-        got = jnp.dot(
-            table_ref[...],
-            src_ref[...].reshape(layers * tokens, columns),
-            preferred_element_type=jnp.float32,
-        )
-        out_ref[...] = got.astype(jnp.bfloat16)
-
-    pl.when(step < 2)(lambda: fill(x_ref))
-    pl.when(step >= 2)(lambda: fill(dy_ref))
+def pack_kernel(
+    x_hbm, dy_hbm, gate_hbm, route_hbm, out_ref, x_ref, dy_ref, gate_ref, route_ref, sems, *, capacity
+):
+    layers, tokens, width = x_ref.shape
+    rows = out_ref.shape[0]
+    experts = rows // (layers * capacity)
+    halves = (slice(0, width // 2), slice(width // 2, width))
+    moves = [(route_hbm, route_ref), (gate_hbm, gate_ref)]
+    for src, dst in ((x_hbm, x_ref), (dy_hbm, dy_ref)):
+        moves += [(src.at[:, :, half], dst.at[:, :, half]) for half in halves]
+    copies = [pltpu.make_async_copy(src, dst, sems.at[i]) for i, (src, dst) in enumerate(moves)]
+    for copy in copies:
+        copy.start()
+    copies[0].wait()
+    match = slot_match(route_ref[...], experts, capacity).astype(jnp.bfloat16)
+    copies[1].wait()
+    scale = jnp.concatenate([gate_ref[layer : layer + 1, :] for layer in range(layers)], axis=1)
+    for i, (src, table) in enumerate(((x_ref, match), (dy_ref, match * scale))):
+        for j, half in enumerate(halves):
+            copies[2 + 2 * i + j].wait()
+            got = jnp.dot(
+                table,
+                src[:, :, half].reshape(layers * tokens, width // 2),
+                preferred_element_type=jnp.float32,
+            )
+            at = i * width + j * (width // 2)
+            out_ref[:, at : at + width // 2] = got.astype(jnp.bfloat16)
 
 
 def fixed(shape):
@@ -74,24 +78,43 @@
 
 def pack(x, dy, gates, route, experts, capacity):
     layers, tokens, width = x.shape
-    rows, half = experts * layers * capacity, width // 2
-    block = (layers, tokens, half)
+    rows = experts * layers * capacity
     return pl.pallas_call(
         functools.partial(pack_kernel, capacity=capacity),
-        grid=(4,),
         out_shape=jax.ShapeDtypeStruct((rows, 2 * width), jnp.bfloat16),
-        in_specs=[
-            pl.BlockSpec(block, lambda t: (0, 0, jnp.minimum(t, 1))),
-            pl.BlockSpec(block, lambda t: (0, 0, jnp.maximum(t - 2, 0))),
-            fixed(gates.shape),
-            fixed(route.shape),
+        in_specs=[whole(pltpu.HBM)] * 4,
+        out_specs=whole(),
+        scratch_shapes=[
+            pltpu.VMEM(x.shape, x.dtype),
+            pltpu.VMEM(dy.shape, dy.dtype),
+            pltpu.VMEM(gates.shape, gates.dtype),
+            pltpu.VMEM(route.shape, route.dtype),
+            pltpu.SemaphoreType.DMA((6,)),
         ],
-        out_specs=pl.BlockSpec((rows, half), lambda t: (0, t)),
-        scratch_shapes=[pltpu.VMEM((rows, layers * tokens), jnp.bfloat16)],
-        compiler_params=pltpu.CompilerParams(vmem_limit_bytes=VMEM_LIMIT),
-        cost_estimate=cost(2 * rows * layers * tokens * 2 * width, 5 << 20),
+        compiler_params=pltpu.CompilerParams(vmem_limit_bytes=PACK_LIMIT),
+        cost_estimate=cost(2 * rows * layers * tokens * 2 * width, 5 * MIB),
         name="pack",
     )(x, dy, gates, route)
+
+
+def join_kernel(wg_ref, wu_ref, wd_ref, out_ref):
+    unit = wg_ref.shape[1]
+    out_ref[:, :unit] = wg_ref[...]
+    out_ref[:, unit : 2 * unit] = wu_ref[...]
+    out_ref[:, 2 * unit :] = wd_ref[...].T
+
+
+def join(w_gate, w_up, w_down):
+    piece, unit = w_gate.shape
+    return pl.pallas_call(
+        join_kernel,
+        out_shape=jax.ShapeDtypeStruct((piece, 3 * unit), jnp.bfloat16),
+        in_specs=[whole()] * 3,
+        out_specs=whole(),
+        compiler_params=pltpu.CompilerParams(vmem_limit_bytes=PACK_LIMIT),
+        cost_estimate=cost(0, MIB),
+        name="join",
+    )(w_gate, w_up, w_down)
 
 
 def forward_kernel(core_ref, recv_ref, weight_ref, grads_ref, hidden_ref, gate_ref, term_ref):
@@ -129,17 +152,16 @@
     half, columns = out_ref.shape
     unit = columns // 6
     piece = 128
-
-    @pl.loop(0, half // (2 * piece))
-    def _(at):
-        rows = pl.ds(pl.multiple_of(at * 2 * piece, 2 * piece), 2 * piece)
+    blocks = min(4, half // piece)
+
+    for at in range(0, half // piece, blocks):
+        rows = slice(at * piece, (at + blocks) * piece)
 
         def pick(offset):
-            first = pl.multiple_of(offset + (4 * at + side) * piece, piece)
-            second = pl.multiple_of(offset + (4 * at + 2 + side) * piece, piece)
-            return jnp.concatenate(
-                [recv_ref[:, pl.ds(first, piece)], recv_ref[:, pl.ds(second, piece)]], axis=1
-            )
+            starts = [
+                pl.multiple_of(offset + (2 * (at + j) + side) * piece, piece) for j in range(blocks)
+            ]
+            return jnp.concatenate([recv_ref[:, pl.ds(start, piece)] for start in starts], axis=1)
 
         up = lax.dot_general(
             pick(0), grads_ref[...], CONTRACT_ROWS, preferred_element_type=jnp.float32
@@ -171,7 +193,7 @@
         ),
         in_specs=[whole(pltpu.SMEM), whole(), whole()],
         out_specs=(whole(),) * 4,
-        compiler_params=pltpu.CompilerParams(vmem_limit_bytes=VMEM_LIMIT),
+        compiler_params=pltpu.CompilerParams(vmem_limit_bytes=24 * MIB),
         cost_estimate=cost(3 * rows * width * columns, 14 << 20),
         name="forward",
     )(core, recv, weights)
@@ -180,21 +202,18 @@
 def input_kernel(grads_ref, weight_ref, gate_ref, out_ref):
     width, columns = weight_ref.shape
     unit = columns // 6
-    chunk = min(256, width)
-
-    @pl.loop(0, width // chunk)
-    def _(at):
-        start = pl.ds(pl.multiple_of(at * chunk, chunk), chunk)
+    chunk = width // 2
+    for at in range(2):
+        rows = slice(at * chunk, (at + 1) * chunk)
         got = 0.0
         for part in range(2):
             got = got + lax.dot_general(
                 grads_ref[:, 2 * part * unit : (2 * part + 2) * unit],
-                weight_ref[start, 3 * part * unit : (3 * part + 2) * unit],
+                weight_ref[rows, 3 * part * unit : (3 * part + 2) * unit],
                 CONTRACT_COLS,
                 preferred_element_type=jnp.float32,
             )
-        out_ref[:, start] = got.astype(jnp.bfloat16)
-
+        out_ref[:, rows] = got.astype(jnp.bfloat16)
     out_ref[:, width:] = gate_ref[...]
 
 
@@ -206,7 +225,7 @@
         out_shape=jax.ShapeDtypeStruct((rows, width + gate.shape[1]), jnp.bfloat16),
         in_specs=[whole()] * 3,
         out_specs=whole(),
-        compiler_params=pltpu.CompilerParams(vmem_limit_bytes=VMEM_LIMIT),
+        compiler_params=pltpu.CompilerParams(vmem_limit_bytes=16 * MIB),
         cost_estimate=cost(4 * rows * width * columns // 3, 9 << 20),
         name="input_terms",
     )(grads, weights, gate)
@@ -224,7 +243,7 @@
         out_shape=jax.ShapeDtypeStruct((half, columns), jnp.bfloat16),
         in_specs=[whole(pltpu.SMEM)] + [whole()] * 4,
         out_specs=whole(),
-        compiler_params=pltpu.CompilerParams(vmem_limit_bytes=VMEM_LIMIT),
+        compiler_params=pltpu.CompilerParams(vmem_limit_bytes=20 * MIB),
         cost_estimate=cost(2 * rows * half * columns, 10 << 20),
         name="own_terms",
     )(core, recv, grads, hidden, arrived)
@@ -275,10 +294,37 @@
             fixed((layers, tokens)),
         ),
         scratch_shapes=[pltpu.VMEM((rows, layers * tokens), jnp.bfloat16)],
-        compiler_params=pltpu.CompilerParams(vmem_limit_bytes=VMEM_LIMIT),
+        compiler_params=pltpu.CompilerParams(vmem_limit_bytes=12 * MIB),
         cost_estimate=cost(2 * rows * layers * tokens * width, 3 << 20),
         name="unpack",
     )(back, back, gates, route)
+
+
+def finish_kernel(reduced_ref, partner_ref, gate_ref, up_ref, down_ref):
+    unit = gate_ref.shape[1]
+    for i, ref in enumerate((gate_ref, up_ref, down_ref)):
+        at = slice(i * unit, (i + 1) * unit)
+        value = reduced_ref[:, at].astype(jnp.float32) + partner_ref[:, at].astype(jnp.float32)
+        ref[...] = value if i < 2 else value.T
+
+
+def finish(reduced, partner):
+    piece, columns = partner.shape
+    unit = columns // 3
+    return pl.pallas_call(
+        finish_kernel,
+        out_shape=(
+            jax.ShapeDtypeStruct((piece, unit), jnp.float32),
+            jax.ShapeDtypeStruct((piece, unit), jnp.float32),
+            jax.ShapeDtypeStruct((unit, piece), jnp.float32),
+        ),
+        in_specs=[pl.BlockSpec((piece, columns), lambda t: (0, 0))] * 2,
+        out_specs=(fixed((piece, unit)), fixed((piece, unit)), fixed((unit, piece))),
+        grid=(1,),
+        compiler_params=pltpu.CompilerParams(vmem_limit_bytes=8 * MIB),
+        cost_estimate=cost(piece * columns, MIB),
+        name="finish",
+    )(reduced, partner)
 
 
 def local(inputs, cotangents, gates, routing, w_gate, w_up, w_down):
@@ -290,36 +336,29 @@
     core = lax.axis_index("c").astype(jnp.int32).reshape(1)
     swap = [(0, 1), (1, 0)]
 
-    mine = jnp.concatenate([w_gate, w_up, w_down.T], axis=1)
-    both = jnp.concatenate([mine, lax.ppermute(mine, "k", swap)], axis=1)
-    weights = lax.all_gather(both, ("y", "c"), axis=0, tiled=True)
-
+    mine = join(w_gate, w_up, w_down)
+    paired = lax.ppermute(mine, "k", swap)
     sent = pack(inputs, cotangents, gates, route, experts, capacity)
+    paired, sent = lax.optimization_barrier((paired, sent))
     recv = lax.all_to_all(
         sent.reshape(experts, layers * capacity, 2 * width), "e", 0, 0, tiled=True
     ).reshape(experts * layers * capacity, 2 * width)
+    both = jnp.concatenate([mine, paired], axis=1)
+    weights = lax.all_gather(both, ("y", "c"), axis=0, tiled=True)
 
     grads, hidden, gate_sum, term = forward(core, recv, weights)
     arrived = lax.ppermute(term, "c", swap)
     back = input_terms(grads, weights, gate_sum)
+    hidden, back = lax.optimization_barrier((hidden, back))
     total = own_terms(core, recv, grads, hidden, arrived)
-    total, back = lax.optimization_barrier((total, back))
     reduced = lax.psum_scatter(total, "y", scatter_dimension=0, tiled=True)
     back = lax.all_to_all(
         back.reshape(experts, layers * capacity, back.shape[1]), "e", 0, 0, tiled=True
     ).reshape(back.shape)
     grad_inputs, grad_gates = unpack(back, gates, route, capacity)
     reduced, grad_gates = lax.optimization_barrier((reduced, grad_gates))
-
     partner = lax.ppermute(reduced[:, 3 * unit :], "k", swap)
-    final = reduced[:, : 3 * unit].astype(jnp.float32) + partner.astype(jnp.float32)
-    return (
-        grad_inputs,
-        grad_gates,
-        final[:, :unit],
-        final[:, unit : 2 * unit],
-        final[:, 2 * unit :].T,
-    )
+    return (grad_inputs, grad_gates, *finish(reduced, partner))
 
 
 def solution(mesh):

time: 210 us -> 194 us (0.924)
  the two profiles are of different devices: /device:TPU:40 before, /device:TPU:48 now
where the time goes in v2:
time: 194 us; the launch traced here: 193 us
  waiting for transfers between devices  82.1 us (42%)
  blocking collectives  48.3 us (25%)
  starting transfers between devices  20.9 us (11%)
  Pallas kernels  17.8 us (9%)
  between operations  14.1 us (7%)
  local copies, waits for them, and re-layouts  9.02 us (5%)
    all_to_all x1, waiting for transfers between devices, local(): lax.all_to_all(sent.reshape(experts, layers * capacity, 2 * width), 'e',...  73.5 us
    all_to_all x1, blocking collectives, local(): lax.all_to_all(back.reshape(experts, layers * capacity, back.shape[1]), '...  48.3 us
    all_to_all x1, starting transfers between devices, local(): lax.all_to_all(sent.reshape(experts, layers * capacity, 2 * width), 'e',...  12.9 us
    unnamed x18, local copies, waits for them, and re-layouts  8.08 us
    ppermute x1, waiting for transfers between devices, local(): partner = lax.ppermute(reduced[:, 3 * unit:], 'k', swap)  5.05 us
    pallas_call x1, Pallas kernels, forward(): pl.pallas_call(forward_kernel, out_shape=(jax.ShapeDtypeStruct((rows, col...  4.5 us
    pallas_call x1, Pallas kernels, pack(): pl.pallas_call(functools.partial(pack_kernel, capacity=capacity), out_sha...  4.35 us
  transfers between devices with their start and end apart: 6, of which 4 were waited for; matrix products, arithmetic and copies ran while one was open for 0% of the time, Pallas kernels for 5%

profile of v2, /device:TPU:48, one launch (start us, length us, event | category | flops | bytes accessed | tf_op | source)
XLA Modules:
  0.0 193.1 jit_solution(104294876581444981)
XLA Ops:
  7.2 0.0 all-gather.2.cloned.1.call-start
  7.2 1.7 join.1
  8.9 0.0 copy-start.8
  8.9 3.5 %collective-permute-start = (bf16[128,768]{1,0:T(8,128)(2,1)}, bf16[128,768]{1,0:T(8,128)(2,1)S(1)}, u32[]{:S(2)}, u32[]{:S(2)}) collective-permute-start(bf16[128,768]{1,0:T(8,128)(2,1)} %join.1), channel_id=1, source_target_pairs={{0,1},{1,0},{2,3},{3,2},{4,5},{5,4},{6,7},{7,6},{8,9},{9,8},{10,11... | collective-permute-start | bytes 589832 | tf_op jit(solution)/shard_map/ppermute | solution.py:340
  12.4 4.3 %pack.1 = bf16[384,4096]{1,0:T(8,128)(2,1)} custom-call(bf16[2,128,2048]{2,1,0:T(8,128)(2,1)} %x_hbm.1, bf16[2,128,2048]{2,1,0:T(8,128)(2,1)} %dy_hbm.1, bf16[2,128]{1,0:T(2,128)(2,1)} %gate_ref.1, s32[2,128]{1,0:T(2,128)} %bitcast.11), custom_call_target="tpu_custom_call" | custom-call | flops 805306368 | bytes 5242880 | tf_op jit(solution)/shard_map/pack/pallas_call | solution.py:82
  16.7 1.0 collective-permute-done
  17.7 0.0 copy-done.8
  17.7 0.8 pad_maximum_fusion
  18.5 0.0 all-gather.2.cloned.1.call-update
  18.5 12.9 %all-to-all-start = ((bf16[16,24,4096]{2,1,0:T(8,128)(2,1)}), bf16[16,24,4096]{2,1,0:T(8,128)(2,1)S(1)}, u32[]{:S(2)}, u32[]{:S(2)}) async-start(bf16[16,24,4096]{2,1,0:T(8,128)(2,1)} %bitcast.13), calls=%async_computation | async-start | bytes 6291456 | tf_op jit(solution)/shard_map/all_to_all | solution.py:343
  31.4 0.0 reduce-scatter.2.cloned.1.call-start
  31.5 73.5 %all-to-all-done = bf16[16,24,4096]{2,1,0:T(8,128)(2,1)S(1)} async-done(((bf16[16,24,4096]{2,1,0:T(8,128)(2,1)}), bf16[16,24,4096]{2,1,0:T(8,128)(2,1)S(1)}, u32[]{:S(2)}, u32[]{:S(2)}) %all-to-all-start) | async-done | bytes 3145760 | tf_op jit(solution)/shard_map/all_to_all | solution.py:343
  105.0 0.0 all-gather.2.cloned.1.call-done.weight_ref
  105.0 0.0 copy-start.3
  105.0 2.8 %copy-done.3 = bf16[2048,1536]{1,0:T(8,128)(2,1)S(1)} copy-done((bf16[2048,1536]{1,0:T(8,128)(2,1)S(1)}, bf16[2048,1536]{1,0:T(8,128)(2,1)}, u32[]{:S(2)}) %copy-start.3) | copy-done | bytes 6291480
  107.8 0.0 copy-start.4
  107.8 4.5 %forward.1 = (bf16[384,1024]{1,0:T(8,128)(2,1)S(1)}, bf16[384,512]{1,0:T(8,128)(2,1)S(1)}, bf16[384,128]{1,0:T(8,128)(2,1)S(1)}, bf16[1024,1536]{1,0:T(8,128)(2,1)S(1)}) custom-call(s32[1]{0:T(128)} %bitcast.core_ref, bf16[384,4096]{1,0:T(8,128)(2,1)S(1)} %bitcast.8, bf16[2048,1536]{1,0:T(8,128)(2,1)S(1)} %copy-done.3), custom_call_target="tpu_custom_call" | custom-call | flops 3623878656 | bytes 14680064 | tf_op jit(solution)/shard_map/forward/pallas_call | solution.py:186
  112.3 1.9 collective-permute-start.1
  114.2 0.0 copy-done.4
  114.2 1.8 input_terms.1
  116.0 0.0 copy-start.1
  116.0 1.2 copy-done.1
  117.3 2.6 %collective-permute-done.1.arrived_ref = bf16[1024,1536]{1,0:T(8,128)(2,1)S(1)} collective-permute-done((bf16[1024,1536]{1,0:T(8,128)(2,1)S(1)}, bf16[1024,1536]{1,0:T(8,128)(2,1)S(1)}, u32[]{:S(2)}, u32[]{:S(2)}) %collective-permute-start.1) | collective-permute-done | bytes 3145760 | tf_op jit(solution)/shard_map/ppermute | solution.py:350
  119.8 1.9 own_terms.1
  121.7 0.0 copy-start
  121.7 1.6 copy-done
  123.3 0.0 copy-start.2
  123.3 0.0 copy-start.6
  123.3 0.0 copy-start.7
  123.3 0.0 reduce-scatter.2.cloned.1.call-update
  123.4 1.4 copy-done.2
  124.8 48.3 %all_to_all.10 = bf16[16,24,2176]{2,1,0:T(8,128)(2,1)S(1)} all-to-all(bf16[16,24,2176]{2,1,0:T(8,128)(2,1)S(1)} %bitcast.10), channel_id=1, replica_groups=mesh['y'=8,'c'=2,'e'=16,'k'=2] {'e'}, dimensions={0} | all-to-all | bytes 3342336 | tf_op jit(solution)/shard_map/all_to_all | solution.py:355
  173.1 0.0 copy-done.6
  173.1 0.0 copy-done.7
  173.1 2.9 %unpack.1 = (bf16[2,128,2048]{2,1,0:T(8,128)(2,1)}, bf16[2,128]{1,0:T(2,128)(2,1)}) custom-call(bf16[384,2176]{1,0:T(8,128)(2,1)S(1)} %bitcast.6, bf16[384,2176]{1,0:T(8,128)(2,1)S(1)} %bitcast.7, bf16[2,128]{1,0:T(2,128)(2,1)S(1)} %copy-done.7, s32[2,128]{1,0:T(2,128)S(1)} %bitcast.12), custom_call_target="tpu_custom_call" | custom-call | flops 402653184 | bytes 3145728 | tf_op jit(solution)/shard_map/unpack/pallas_call | solution.py:279
  176.0 0.0 reduce-scatter.2.cloned.1.call-done.reduced_ref
  176.0 0.9 slice.3
  176.9 2.5 %collective-permute-start.2 = (bf16[128,768]{1,0:T(8,128)(2,1)S(1)}, bf16[128,768]{1,0:T(8,128)(2,1)S(1)}, u32[]{:S(2)}, u32[]{:S(2)}) collective-permute-start(bf16[128,768]{1,0:T(8,128)(2,1)S(1)} %slice.3), channel_id=1, source_target_pairs={{0,1},{1,0},{2,3},{3,2},{4,5},{5,4},{6,7},{7,6},{8,9},{9,8},{10,11... | collective-permute-start | bytes 589832 | tf_op jit(solution)/shard_map/ppermute | solution.py:360
  179.4 5.1 %collective-permute-done.2.partner_ref = bf16[128,768]{1,0:T(8,128)(2,1)S(1)} collective-permute-done((bf16[128,768]{1,0:T(8,128)(2,1)S(1)}, bf16[128,768]{1,0:T(8,128)(2,1)S(1)}, u32[]{:S(2)}, u32[]{:S(2)}) %collective-permute-start.2) | collective-permute-done | bytes 196640 | tf_op jit(solution)/shard_map/ppermute | solution.py:360
  184.5 0.0 copy-start.5
  184.5 1.0 copy-done.5
  185.5 0.8 finish.1
Async XLA Ops:
  7.2 97.8 %all-gather.2.cloned.1.call-start = ((), (), s32[]{:S(2)}) async-start(), calls=%async_computation.3 | async-start | bytes 6684672 | tf_op jit(solution)/shard_map/all_gather | solution.py:347
  8.9 8.9 %copy-start.8 = (bf16[128,768]{1,0:T(8,128)(2,1)S(1)}, bf16[128,768]{1,0:T(8,128)(2,1)}, u32[]{:S(2)}) copy-start(bf16[128,768]{1,0:T(8,128)(2,1)} %join.1) | copy-start | bytes 589828
  8.9 8.9 %collective-permute-start = (bf16[128,768]{1,0:T(8,128)(2,1)}, bf16[128,768]{1,0:T(8,128)(2,1)S(1)}, u32[]{:S(2)}, u32[]{:S(2)}) collective-permute-start(bf16[128,768]{1,0:T(8,128)(2,1)} %join.1), channel_id=1, source_target_pairs={{0,1},{1,0},{2,3},{3,2},{4,5},{5,4},{6,7},{7,6},{8,9},{9,8},{10,11... | collective-permute-start | bytes 589832 | tf_op jit(solution)/shard_map/ppermute | solution.py:340
  18.5 86.4 %all-to-all-start = ((bf16[16,24,4096]{2,1,0:T(8,128)(2,1)}), bf16[16,24,4096]{2,1,0:T(8,128)(2,1)S(1)}, u32[]{:S(2)}, u32[]{:S(2)}) async-start(bf16[16,24,4096]{2,1,0:T(8,128)(2,1)} %bitcast.13), calls=%async_computation | async-start | bytes 6291456 | tf_op jit(solution)/shard_map/all_to_all | solution.py:343
  31.4 144.5 %reduce-scatter.2.cloned.1.call-start = ((), (), s32[]{:S(2)}) async-start(), calls=%async_computation.4 | async-start | bytes 3538944 | tf_op jit(solution)/shard_map/reduce_scatter | solution.py:354
  105.0 2.8 %copy-start.3 = (bf16[2048,1536]{1,0:T(8,128)(2,1)S(1)}, bf16[2048,1536]{1,0:T(8,128)(2,1)}, u32[]{:S(2)}) copy-start(bf16[2048,1536]{1,0:T(8,128)(2,1)} %all-gather.2.cloned.1.call-done.weight_ref) | copy-start | bytes 18874372
  107.8 6.4 %copy-start.4 = (bf16[2048,1536]{1,0:T(8,128)(2,1)S(1)}, bf16[2048,1536]{1,0:T(8,128)(2,1)}, u32[]{:S(2)}) copy-start(bf16[2048,1536]{1,0:T(8,128)(2,1)} %all-gather.2.cloned.1.call-done.weight_ref) | copy-start | bytes 18874372
  112.3 7.6 %collective-permute-start.1 = (bf16[1024,1536]{1,0:T(8,128)(2,1)S(1)}, bf16[1024,1536]{1,0:T(8,128)(2,1)S(1)}, u32[]{:S(2)}, u32[]{:S(2)}) collective-permute-start(bf16[1024,1536]{1,0:T(8,128)(2,1)S(1)} %get-tuple-element.28), channel_id=1, source_target_pairs={{0,32},{32,0},{1,33},{33,1},{2,34},{34,2},{3,35},{35,3},{4,36},{36... | collective-permute-start | bytes 9437192 | tf_op jit(solution)/shard_map/ppermute | solution.py:350
  116.0 1.2 copy-start.1
  121.7 1.7 copy-start
  123.3 1.4 copy-start.2
  123.3 49.8 %copy-start.6 = (s32[2,128,1]{1,2,0:T(1,128)S(1)}, s32[2,128,1]{1,2,0:T(1,128)}, u32[]{:S(2)}) copy-start(s32[2,128,1]{1,2,0:T(1,128)} %param.10) | copy-start | bytes 3076
  123.3 49.8 %copy-start.7 = (bf16[2,128]{1,0:T(2,128)(2,1)S(1)}, bf16[2,128]{1,0:T(2,128)(2,1)}, u32[]{:S(2)}) copy-start(bf16[2,128]{1,0:T(2,128)(2,1)} %gate_ref.1) | copy-start | bytes 1540
  176.9 7.6 %collective-permute-start.2 = (bf16[128,768]{1,0:T(8,128)(2,1)S(1)}, bf16[128,768]{1,0:T(8,128)(2,1)S(1)}, u32[]{:S(2)}, u32[]{:S(2)}) collective-permute-start(bf16[128,768]{1,0:T(8,128)(2,1)S(1)} %slice.3), channel_id=1, source_target_pairs={{0,1},{1,0},{2,3},{3,2},{4,5},{5,4},{6,7},{7,6},{8,9},{9,8},{10,11... | collective-permute-start | bytes 589832 | tf_op jit(solution)/shard_map/ppermute | solution.py:360
  184.5 1.0 copy-start.5
Sparse Core Ops, SparseCore 0:
  18.7 51.0 all-gather.1
  123.5 42.5 reduce-scatter.1

commit v3 on v2

--- a/solution.py
+++ b/solution.py
@@ -44,7 +44,8 @@
 
 
 def pack_kernel(
-    x_hbm, dy_hbm, gate_hbm, route_hbm, out_ref, x_ref, dy_ref, gate_ref, route_ref, sems, *, capacity
+    x_hbm, dy_hbm, gate_hbm, route_hbm, out_hbm,
+    x_ref, dy_ref, gate_ref, route_ref, out_ref, sems, out_sems, *, capacity
 ):
     layers, tokens, width = x_ref.shape
     rows = out_ref.shape[0]
@@ -60,6 +61,7 @@
     match = slot_match(route_ref[...], experts, capacity).astype(jnp.bfloat16)
     copies[1].wait()
     scale = jnp.concatenate([gate_ref[layer : layer + 1, :] for layer in range(layers)], axis=1)
+    leaving = []
     for i, (src, table) in enumerate(((x_ref, match), (dy_ref, match * scale))):
         for j, half in enumerate(halves):
             copies[2 + 2 * i + j].wait()
@@ -68,8 +70,14 @@
                 src[:, :, half].reshape(layers * tokens, width // 2),
                 preferred_element_type=jnp.float32,
             )
-            at = i * width + j * (width // 2)
-            out_ref[:, at : at + width // 2] = got.astype(jnp.bfloat16)
+            at = slice(i * width + j * (width // 2), i * width + (j + 1) * (width // 2))
+            out_ref[:, at] = got.astype(jnp.bfloat16)
+            leaving.append(
+                pltpu.make_async_copy(out_ref.at[:, at], out_hbm.at[:, at], out_sems.at[2 * i + j])
+            )
+            leaving[-1].start()
+    for copy in leaving:
+        copy.wait()
 
 
 def fixed(shape):
@@ -81,15 +89,17 @@
     rows = experts * layers * capacity
     return pl.pallas_call(
         functools.partial(pack_kernel, capacity=capacity),
-        out_shape=jax.ShapeDtypeStruct((rows, 2 * width), jnp.bfloat16),
-        in_specs=[whole(pltpu.HBM)] * 4,
-        out_specs=whole(),
+        out_shape=pltpu.HBM((rows, 2 * width), jnp.bfloat16),
+        in_specs=[whole(pl.ANY)] * 4,
+        out_specs=whole(pl.ANY),
         scratch_shapes=[
             pltpu.VMEM(x.shape, x.dtype),
             pltpu.VMEM(dy.shape, dy.dtype),
             pltpu.VMEM(gates.shape, gates.dtype),
             pltpu.VMEM(route.shape, route.dtype),
+            pltpu.VMEM((rows, 2 * width), jnp.bfloat16),
             pltpu.SemaphoreType.DMA((6,)),
+            pltpu.SemaphoreType.DMA((4,)),
         ],
         compiler_params=pltpu.CompilerParams(vmem_limit_bytes=PACK_LIMIT),
         cost_estimate=cost(2 * rows * layers * tokens * 2 * width, 5 * MIB),
@@ -117,20 +127,36 @@
     )(w_gate, w_up, w_down)
 
 
-def forward_kernel(core_ref, recv_ref, weight_ref, grads_ref, hidden_ref, gate_ref, term_ref):
+def weight_copies(weight_hbm, weight_ref, sems, pieces):
+    copies = [
+        pltpu.make_async_copy(weight_hbm.at[:, piece], weight_ref.at[:, piece], sems.at[i])
+        for i, piece in enumerate(pieces)
+    ]
+    for copy in copies:
+        copy.start()
+    return copies
+
+
+def forward_kernel(
+    core_ref, recv_ref, weight_hbm, grads_ref, hidden_ref, gate_ref, term_ref, weight_ref, sems
+):
     width, columns = weight_ref.shape
     unit = columns // 6
+    pieces = []
+    for part in range(2):
+        base = part * 3 * unit
+        pieces += [slice(base, base + 2 * unit), slice(base + 2 * unit, base + 3 * unit)]
+    copies = weight_copies(weight_hbm, weight_ref, sems, pieces)
     gate_sum = 0.0
     for part in range(2):
-        base = part * 3 * unit
+        copies[2 * part].wait()
         pre = jnp.dot(
-            recv_ref[:, :width],
-            weight_ref[:, base : base + 2 * unit],
-            preferred_element_type=jnp.float32,
-        )
+            recv_ref[:, :width], weight_ref[:, pieces[2 * part]], preferred_element_type=jnp.float32
+        )
+        copies[2 * part + 1].wait()
         back = jnp.dot(
             recv_ref[:, width:],
-            weight_ref[:, base + 2 * unit : base + 3 * unit],
+            weight_ref[:, pieces[2 * part + 1]],
             preferred_element_type=jnp.float32,
         )
         gate_pre, up_value = pre[:, :unit], pre[:, unit:]
@@ -148,7 +174,7 @@
     weight_terms(recv_ref, grads_ref, hidden_ref, 1 - core_ref[0], term_ref, None)
 
 
-def weight_terms(recv_ref, grads_ref, hidden_ref, side, out_ref, add_ref):
+def weight_terms(recv_ref, grads_ref, hidden_ref, side, out_ref, add_ref, done=None):
     half, columns = out_ref.shape
     unit = columns // 6
     piece = 128
@@ -178,6 +204,8 @@
                 second = second + add_ref[rows, base + 2 * unit : base + 3 * unit].astype(jnp.float32)
             out_ref[rows, base : base + 2 * unit] = first.astype(jnp.bfloat16)
             out_ref[rows, base + 2 * unit : base + 3 * unit] = second.astype(jnp.bfloat16)
+        if done is not None:
+            done(at // blocks, rows)
 
 
 def forward(core, recv, weights):
@@ -191,25 +219,39 @@
             jax.ShapeDtypeStruct((rows, 128), jnp.bfloat16),
             jax.ShapeDtypeStruct((width // 2, columns), jnp.bfloat16),
         ),
-        in_specs=[whole(pltpu.SMEM), whole(), whole()],
+        in_specs=[whole(pltpu.SMEM), whole(), whole(pl.ANY)],
         out_specs=(whole(),) * 4,
-        compiler_params=pltpu.CompilerParams(vmem_limit_bytes=24 * MIB),
+        scratch_shapes=[pltpu.VMEM(weights.shape, weights.dtype), pltpu.SemaphoreType.DMA((4,))],
+        compiler_params=pltpu.CompilerParams(vmem_limit_bytes=44 * MIB),
         cost_estimate=cost(3 * rows * width * columns, 14 << 20),
         name="forward",
     )(core, recv, weights)
 
 
-def input_kernel(grads_ref, weight_ref, gate_ref, out_ref):
+def input_kernel(grads_ref, weight_hbm, gate_ref, out_ref, weight_ref, sems):
     width, columns = weight_ref.shape
     unit = columns // 6
     chunk = width // 2
+    pieces = [slice(3 * part * unit, (3 * part + 2) * unit) for part in range(2)]
+    copies = [
+        pltpu.make_async_copy(
+            weight_hbm.at[pl.ds(at * chunk, chunk), piece],
+            weight_ref.at[pl.ds(at * chunk, chunk), piece],
+            sems.at[2 * at + part],
+        )
+        for at in range(2)
+        for part, piece in enumerate(pieces)
+    ]
+    for copy in copies:
+        copy.start()
     for at in range(2):
         rows = slice(at * chunk, (at + 1) * chunk)
         got = 0.0
         for part in range(2):
+            copies[2 * at + part].wait()
             got = got + lax.dot_general(
                 grads_ref[:, 2 * part * unit : (2 * part + 2) * unit],
-                weight_ref[rows, 3 * part * unit : (3 * part + 2) * unit],
+                weight_ref[rows, pieces[part]],
                 CONTRACT_COLS,
                 preferred_element_type=jnp.float32,
             )
@@ -223,16 +265,25 @@
     return pl.pallas_call(
         input_kernel,
         out_shape=jax.ShapeDtypeStruct((rows, width + gate.shape[1]), jnp.bfloat16),
-        in_specs=[whole()] * 3,
+        in_specs=[whole(), whole(pl.ANY), whole()],
         out_specs=whole(),
-        compiler_params=pltpu.CompilerParams(vmem_limit_bytes=16 * MIB),
+        scratch_shapes=[pltpu.VMEM(weights.shape, weights.dtype), pltpu.SemaphoreType.DMA((4,))],
+        compiler_params=pltpu.CompilerParams(vmem_limit_bytes=20 * MIB),
         cost_estimate=cost(4 * rows * width * columns // 3, 9 << 20),
         name="input_terms",
     )(grads, weights, gate)
 
 
-def own_kernel(core_ref, recv_ref, grads_ref, hidden_ref, arrived_ref, out_ref):
-    weight_terms(recv_ref, grads_ref, hidden_ref, core_ref[0], out_ref, arrived_ref)
+def own_kernel(core_ref, recv_ref, grads_ref, hidden_ref, arrived_ref, out_hbm, out_ref, sems):
+    copies = []
+
+    def done(i, rows):
+        copies.append(pltpu.make_async_copy(out_ref.at[rows], out_hbm.at[rows], sems.at[i]))
+        copies[-1].start()
+
+    weight_terms(recv_ref, grads_ref, hidden_ref, core_ref[0], out_ref, arrived_ref, done)
+    for copy in copies:
+        copy.wait()
 
 
 def own_terms(core, recv, grads, hidden, arrived):
@@ -240,10 +291,11 @@
     half, columns = arrived.shape
     return pl.pallas_call(
         own_kernel,
-        out_shape=jax.ShapeDtypeStruct((half, columns), jnp.bfloat16),
+        out_shape=pltpu.HBM((half, columns), jnp.bfloat16),
         in_specs=[whole(pltpu.SMEM)] + [whole()] * 4,
-        out_specs=whole(),
-        compiler_params=pltpu.CompilerParams(vmem_limit_bytes=20 * MIB),
+        out_specs=whole(pl.ANY),
+        scratch_shapes=[pltpu.VMEM(arrived.shape, jnp.bfloat16), pltpu.SemaphoreType.DMA((2,))],
+        compiler_params=pltpu.CompilerParams(vmem_limit_bytes=24 * MIB),
         cost_estimate=cost(2 * rows * half * columns, 10 << 20),
         name="own_terms",
     )(core, recv, grads, hidden, arrived)
@@ -321,7 +373,7 @@
         in_specs=[pl.BlockSpec((piece, columns), lambda t: (0, 0))] * 2,
         out_specs=(fixed((piece, unit)), fixed((piece, unit)), fixed((unit, piece))),
         grid=(1,),
-        compiler_params=pltpu.CompilerParams(vmem_limit_bytes=8 * MIB),
+        compiler_params=pltpu.CompilerParams(vmem_limit_bytes=50 * MIB),
         cost_estimate=cost(piece * columns, MIB),
         name="finish",
     )(reduced, partner)
@@ -356,7 +408,6 @@
         back.reshape(experts, layers * capacity, back.shape[1]), "e", 0, 0, tiled=True
     ).reshape(back.shape)
     grad_inputs, grad_gates = unpack(back, gates, route, capacity)
-    reduced, grad_gates = lax.optimization_barrier((reduced, grad_gates))
     partner = lax.ppermute(reduced[:, 3 * unit :], "k", swap)
     return (grad_inputs, grad_gates, *finish(reduced, partner))
 

time: 194 us -> 185 us (0.954)
  the two profiles are of different devices: /device:TPU:48 before, /device:TPU:2 now
where the time goes in v3:
time: 185 us
  waiting for transfers between devices  120 us (65%)
  starting transfers between devices  25.6 us (14%)
  Pallas kernels  23.3 us (13%)
  between operations  14.2 us (8%)
    all_to_all x1, waiting for transfers between devices, local(): lax.all_to_all(sent.reshape(experts, layers * capacity, 2 * width), 'e',...  73.5 us
    reduce_scatter x1, waiting for transfers between devices, local(): reduced = lax.psum_scatter(total, 'y', scatter_dimension=0, tiled=True)  42 us
    all_to_all x1, starting transfers between devices, local(): lax.all_to_all(sent.reshape(experts, layers * capacity, 2 * width), 'e',...  9.07 us
    ppermute x1, starting transfers between devices, local(): paired = lax.ppermute(mine, 'k', swap)  7.94 us
    pallas_call x1, Pallas kernels, forward(): pl.pallas_call(forward_kernel, out_shape=(jax.ShapeDtypeStruct((rows, col...  7.54 us
    all_to_all x1, starting transfers between devices, local(): lax.all_to_all(back.reshape(experts, layers * capacity, back.shape[1]), '...  4.06 us
    pallas_call x1, Pallas kernels, input_terms(): pl.pallas_call(input_kernel, out_shape=jax.ShapeDtypeStruct((rows, width...  3.74 us
  transfers between devices with their start and end apart: 7, of which 5 were waited for; matrix products, arithmetic and copies ran while one was open for 1% of the time, Pallas kernels for 6%

profile of v3, /device:TPU:2, one launch (start us, length us, event | category | flops | bytes accessed | tf_op | source)
XLA Modules:
  0.0 184.5 jit_solution(9596706400948901643)
XLA Ops:
  7.2 0.0 all-gather.2.cloned.1.call-start
  7.2 1.7 join.1
  8.9 0.0 copy-start.4
  8.9 7.9 %collective-permute-start = (bf16[128,768]{1,0:T(8,128)(2,1)}, bf16[128,768]{1,0:T(8,128)(2,1)S(1)}, u32[]{:S(2)}, u32[]{:S(2)}) collective-permute-start(bf16[128,768]{1,0:T(8,128)(2,1)} %join.1), channel_id=1, source_target_pairs={{0,1},{1,0},{2,3},{3,2},{4,5},{5,4},{6,7},{7,6},{8,9},{9,8},{10,11... | collective-permute-start | bytes 589832 | tf_op jit(solution)/shard_map/ppermute | solution.py:392
  16.8 3.6 %pack.1 = bf16[384,4096]{1,0:T(8,128)(2,1)} custom-call(bf16[2,128,2048]{2,1,0:T(8,128)(2,1)} %x_hbm.1, bf16[2,128,2048]{2,1,0:T(8,128)(2,1)} %dy_hbm.1, bf16[2,128]{1,0:T(2,128)(2,1)} %gate_ref.1, s32[2,128]{1,0:T(2,128)} %bitcast.10), custom_call_target="tpu_custom_call" | custom-call | flops 805306368 | bytes 5242880 | tf_op jit(solution)/shard_map/pack/pallas_call | solution.py:90
  20.4 0.2 collective-permute-done
  20.7 0.0 copy-done.4
  20.7 0.8 pad_maximum_fusion
  21.4 0.0 all-gather.2.cloned.1.call-update
  21.5 9.1 %all-to-all-start = ((bf16[16,24,4096]{2,1,0:T(8,128)(2,1)}), bf16[16,24,4096]{2,1,0:T(8,128)(2,1)S(1)}, u32[]{:S(2)}, u32[]{:S(2)}) async-start(bf16[16,24,4096]{2,1,0:T(8,128)(2,1)} %bitcast.12), calls=%async_computation | async-start | bytes 6291456 | tf_op jit(solution)/shard_map/all_to_all | solution.py:395
  30.5 0.0 reduce-scatter.2.cloned.1.call-start
  30.6 73.5 %all-to-all-done = bf16[16,24,4096]{2,1,0:T(8,128)(2,1)S(1)} async-done(((bf16[16,24,4096]{2,1,0:T(8,128)(2,1)}), bf16[16,24,4096]{2,1,0:T(8,128)(2,1)S(1)}, u32[]{:S(2)}, u32[]{:S(2)}) %all-to-all-start) | async-done | bytes 3145760 | tf_op jit(solution)/shard_map/all_to_all | solution.py:395
  104.1 0.0 all-gather.2.cloned.1.call-done.weight_hbm
  104.1 0.0 copy-start
  104.1 7.5 %forward.1 = (bf16[384,1024]{1,0:T(8,128)(2,1)S(1)}, bf16[384,512]{1,0:T(8,128)(2,1)S(1)}, bf16[384,128]{1,0:T(8,128)(2,1)S(1)}, bf16[1024,1536]{1,0:T(8,128)(2,1)S(1)}) custom-call(s32[1]{0:T(128)} %bitcast.core_ref, bf16[384,4096]{1,0:T(8,128)(2,1)S(1)} %bitcast.8, bf16[2048,1536]{1,0:T(8,128)(2,1)} %all-gather.2.cloned.1.call-done.weight_hbm), custom_call_target="tpu_custom_call" | custom-call | flops 3623878656 | bytes 14680064 | tf_op jit(solution)/shard_map/forward/pallas_call | solution.py:214
  111.6 1.9 %collective-permute-start.1 = (bf16[1024,1536]{1,0:T(8,128)(2,1)S(1)}, bf16[1024,1536]{1,0:T(8,128)(2,1)S(1)}, u32[]{:S(2)}, u32[]{:S(2)}) collective-permute-start(bf16[1024,1536]{1,0:T(8,128)(2,1)S(1)} %get-tuple-element.27), channel_id=1, source_target_pairs={{0,32},{32,0},{1,33},{33,1},{2,34},{34,2},{3,35},{35,3},{4,36},{36... | collective-permute-start | bytes 9437192 | tf_op jit(solution)/shard_map/ppermute | solution.py:402
  113.6 0.0 copy-done
  113.6 3.7 %input_terms.1 = bf16[384,2176]{1,0:T(8,128)(2,1)} custom-call(bf16[384,1024]{1,0:T(8,128)(2,1)S(1)} %get-tuple-element.21.grads_ref, bf16[2048,1536]{1,0:T(8,128)(2,1)S(1)} %copy-done, bf16[384,128]{1,0:T(8,128)(2,1)S(1)} %get-tuple-element.22.gate_ref), custom_call_target="tpu_custom_call" | custom-call | flops 1610612736 | bytes 9437184 | tf_op jit(solution)/shard_map/input_terms/pallas_call | solution.py:265
  117.3 1.9 %collective-permute-done.1.arrived_ref = bf16[1024,1536]{1,0:T(8,128)(2,1)S(1)} collective-permute-done((bf16[1024,1536]{1,0:T(8,128)(2,1)S(1)}, bf16[1024,1536]{1,0:T(8,128)(2,1)S(1)}, u32[]{:S(2)}, u32[]{:S(2)}) %collective-permute-start.1) | collective-permute-done | bytes 3145760 | tf_op jit(solution)/shard_map/ppermute | solution.py:402
  119.2 3.0 %own_terms.1 = bf16[1024,1536]{1,0:T(8,128)(2,1)} custom-call(s32[1]{0:T(128)} %bitcast.core_ref, bf16[384,4096]{1,0:T(8,128)(2,1)S(1)} %bitcast.9, bf16[384,1024]{1,0:T(8,128)(2,1)S(1)} %get-tuple-element.21.grads_ref, bf16[384,512]{1,0:T(8,128)(2,1)S(1)} %get-tuple-element.26.hidden_ref, bf16[1024,1536]{1,0:T(8,128)(2,1)S(1)} %collective-permute-done.1.arrived_ref), custom_call_target="tpu_custom_call" | custom-call | flops 1207959552 | bytes 10485760 | tf_op jit(solution)/shard_map/own_terms/pallas_call | solution.py:292
  122.2 0.0 copy-start.2
  122.2 0.0 copy-start.3
  122.2 0.0 reduce-scatter.2.cloned.1.call-update
  122.2 4.1 %all-to-all-start.1 = ((bf16[16,24,2176]{2,1,0:T(8,128)(2,1)}), bf16[16,24,2176]{2,1,0:T(8,128)(2,1)S(1)}, u32[]{:S(2)}, u32[]{:S(2)}) async-start(bf16[16,24,2176]{2,1,0:T(8,128)(2,1)} %bitcast.4), calls=%async_computation.1 | async-start | bytes 3342336 | tf_op jit(solution)/shard_map/all_to_all | solution.py:407
  126.3 42.0 %reduce-scatter.2.cloned.1.call-done.reduced_ref = bf16[128,1536]{1,0:T(8,128)(2,1)} async-done(((bf16[1024,1536]{1,0:T(8,128)(2,1)}), bf16[128,1536]{1,0:T(8,128)(2,1)}) %reduce-scatter.2.cloned.1.call-update) | async-done | bytes 393232 | tf_op jit(solution)/shard_map/reduce_scatter | solution.py:406
  168.3 0.0 copy-start.1
  168.3 1.0 slice.4
  169.3 2.5 %collective-permute-start.2 = (bf16[128,768]{1,0:T(8,128)(2,1)S(1)}, bf16[128,768]{1,0:T(8,128)(2,1)S(1)}, u32[]{:S(2)}, u32[]{:S(2)}) collective-permute-start(bf16[128,768]{1,0:T(8,128)(2,1)S(1)} %slice.4), channel_id=1, source_target_pairs={{0,1},{1,0},{2,3},{3,2},{4,5},{5,4},{6,7},{7,6},{8,9},{9,8},{10,11... | collective-permute-start | bytes 589832 | tf_op jit(solution)/shard_map/ppermute | solution.py:411
  171.9 0.0 all-to-all-done.1
  171.9 0.0 copy-done.2
  171.9 0.0 copy-done.3
  171.9 2.9 %unpack.1 = (bf16[2,128,2048]{2,1,0:T(8,128)(2,1)}, bf16[2,128]{1,0:T(2,128)(2,1)}) custom-call(bf16[384,2176]{1,0:T(8,128)(2,1)S(1)} %bitcast.6, bf16[384,2176]{1,0:T(8,128)(2,1)S(1)} %bitcast.7, bf16[2,128]{1,0:T(2,128)(2,1)S(1)} %copy-done.3, s32[2,128]{1,0:T(2,128)S(1)} %bitcast.11), custom_call_target="tpu_custom_call" | custom-call | flops 402653184 | bytes 3145728 | tf_op jit(solution)/shard_map/unpack/pallas_call | solution.py:331
  174.8 2.1 %collective-permute-done.2.partner_ref = bf16[128,768]{1,0:T(8,128)(2,1)S(1)} collective-permute-done((bf16[128,768]{1,0:T(8,128)(2,1)S(1)}, bf16[128,768]{1,0:T(8,128)(2,1)S(1)}, u32[]{:S(2)}, u32[]{:S(2)}) %collective-permute-start.2) | collective-permute-done | bytes 196640 | tf_op jit(solution)/shard_map/ppermute | solution.py:411
  176.9 0.0 copy-done.1
  176.9 0.8 finish.1
Async XLA Ops:
  7.2 96.9 %all-gather.2.cloned.1.call-start = ((), (), s32[]{:S(2)}) async-start(), calls=%async_computation.3 | async-start | bytes 6684672 | tf_op jit(solution)/shard_map/all_gather | solution.py:399
  8.9 11.8 %copy-start.4 = (bf16[128,768]{1,0:T(8,128)(2,1)S(1)}, bf16[128,768]{1,0:T(8,128)(2,1)}, u32[]{:S(2)}) copy-start(bf16[128,768]{1,0:T(8,128)(2,1)} %join.1) | copy-start | bytes 589828
  8.9 11.8 %collective-permute-start = (bf16[128,768]{1,0:T(8,128)(2,1)}, bf16[128,768]{1,0:T(8,128)(2,1)S(1)}, u32[]{:S(2)}, u32[]{:S(2)}) collective-permute-start(bf16[128,768]{1,0:T(8,128)(2,1)} %join.1), channel_id=1, source_target_pairs={{0,1},{1,0},{2,3},{3,2},{4,5},{5,4},{6,7},{7,6},{8,9},{9,8},{10,11... | collective-permute-start | bytes 589832 | tf_op jit(solution)/shard_map/ppermute | solution.py:392
  21.5 82.6 %all-to-all-start = ((bf16[16,24,4096]{2,1,0:T(8,128)(2,1)}), bf16[16,24,4096]{2,1,0:T(8,128)(2,1)S(1)}, u32[]{:S(2)}, u32[]{:S(2)}) async-start(bf16[16,24,4096]{2,1,0:T(8,128)(2,1)} %bitcast.12), calls=%async_computation | async-start | bytes 6291456 | tf_op jit(solution)/shard_map/all_to_all | solution.py:395
  30.5 137.8 %reduce-scatter.2.cloned.1.call-start = ((), (), s32[]{:S(2)}) async-start(), calls=%async_computation.4 | async-start | bytes 3538944 | tf_op jit(solution)/shard_map/reduce_scatter | solution.py:406
  104.1 9.5 %copy-start = (bf16[2048,1536]{1,0:T(8,128)(2,1)S(1)}, bf16[2048,1536]{1,0:T(8,128)(2,1)}, u32[]{:S(2)}) copy-start(bf16[2048,1536]{1,0:T(8,128)(2,1)} %all-gather.2.cloned.1.call-done.weight_hbm) | copy-start | bytes 18874372
  111.6 7.6 %collective-permute-start.1 = (bf16[1024,1536]{1,0:T(8,128)(2,1)S(1)}, bf16[1024,1536]{1,0:T(8,128)(2,1)S(1)}, u32[]{:S(2)}, u32[]{:S(2)}) collective-permute-start(bf16[1024,1536]{1,0:T(8,128)(2,1)S(1)} %get-tuple-element.27), channel_id=1, source_target_pairs={{0,32},{32,0},{1,33},{33,1},{2,34},{34,2},{3,35},{35,3},{4,36},{36... | collective-permute-start | bytes 9437192 | tf_op jit(solution)/shard_map/ppermute | solution.py:402
  122.2 49.7 %copy-start.2 = (s32[2,128,1]{1,2,0:T(1,128)S(1)}, s32[2,128,1]{1,2,0:T(1,128)}, u32[]{:S(2)}) copy-start(s32[2,128,1]{1,2,0:T(1,128)} %param.10) | copy-start | bytes 3076
  122.2 49.7 %copy-start.3 = (bf16[2,128]{1,0:T(2,128)(2,1)S(1)}, bf16[2,128]{1,0:T(2,128)(2,1)}, u32[]{:S(2)}) copy-start(bf16[2,128]{1,0:T(2,128)(2,1)} %gate_ref.1) | copy-start | bytes 1540
  122.2 49.6 %all-to-all-start.1 = ((bf16[16,24,2176]{2,1,0:T(8,128)(2,1)}), bf16[16,24,2176]{2,1,0:T(8,128)(2,1)S(1)}, u32[]{:S(2)}, u32[]{:S(2)}) async-start(bf16[16,24,2176]{2,1,0:T(8,128)(2,1)} %bitcast.4), calls=%async_computation.1 | async-start | bytes 3342336 | tf_op jit(solution)/shard_map/all_to_all | solution.py:407
  168.3 8.6 %copy-start.1 = (bf16[128,1536]{1,0:T(8,128)(2,1)S(1)}, bf16[128,1536]{1,0:T(8,128)(2,1)}, u32[]{:S(2)}) copy-start(bf16[128,1536]{1,0:T(8,128)(2,1)} %reduce-scatter.2.cloned.1.call-done.reduced_ref) | copy-start | bytes 1179652
  169.3 7.6 %collective-permute-start.2 = (bf16[128,768]{1,0:T(8,128)(2,1)S(1)}, bf16[128,768]{1,0:T(8,128)(2,1)S(1)}, u32[]{:S(2)}, u32[]{:S(2)}) collective-permute-start(bf16[128,768]{1,0:T(8,128)(2,1)S(1)} %slice.4), channel_id=1, source_target_pairs={{0,1},{1,0},{2,3},{3,2},{4,5},{5,4},{6,7},{7,6},{8,9},{9,8},{10,11... | collective-permute-start | bytes 589832 | tf_op jit(solution)/shard_map/ppermute | solution.py:411
Sparse Core Ops, SparseCore 0:
  21.6 50.2 all-gather.1
  122.4 45.8 reduce-scatter.1

commit v4 on v3

--- a/solution.py
+++ b/solution.py
@@ -10,6 +10,7 @@
 
 MIB = 1024 * 1024
 PACK_LIMIT = 56 * MIB
+FORWARD_LIMIT = 38 * MIB
 CONTRACT_ROWS = (((0,), (0,)), ((), ()))
 CONTRACT_COLS = (((1,), (1,)), ((), ()))
 
@@ -107,24 +108,28 @@
     )(x, dy, gates, route)
 
 
-def join_kernel(wg_ref, wu_ref, wd_ref, out_ref):
-    unit = wg_ref.shape[1]
-    out_ref[:, :unit] = wg_ref[...]
-    out_ref[:, unit : 2 * unit] = wu_ref[...]
-    out_ref[:, 2 * unit :] = wd_ref[...].T
-
-
-def join(w_gate, w_up, w_down):
-    piece, unit = w_gate.shape
+def join_kernel(*refs):
+    out_ref = refs[-1]
+    unit = refs[0].shape[1]
+    for part in range(2):
+        gate_ref, up_ref, down_ref = refs[3 * part : 3 * part + 3]
+        base = 3 * part * unit
+        out_ref[:, base : base + unit] = gate_ref[...]
+        out_ref[:, base + unit : base + 2 * unit] = up_ref[...]
+        out_ref[:, base + 2 * unit : base + 3 * unit] = down_ref[...].T
+
+
+def join(own, partner):
+    piece, unit = own[0].shape
     return pl.pallas_call(
         join_kernel,
-        out_shape=jax.ShapeDtypeStruct((piece, 3 * unit), jnp.bfloat16),
-        in_specs=[whole()] * 3,
+        out_shape=pltpu.HBM((piece, 6 * unit), jnp.bfloat16),
+        in_specs=[whole()] * 6,
         out_specs=whole(),
-        compiler_params=pltpu.CompilerParams(vmem_limit_bytes=PACK_LIMIT),
+        compiler_params=pltpu.CompilerParams(vmem_limit_bytes=8 * MIB),
         cost_estimate=cost(0, MIB),
         name="join",
-    )(w_gate, w_up, w_down)
+    )(*own, *partner)
 
 
 def weight_copies(weight_hbm, weight_ref, sems, pieces):
@@ -171,10 +176,10 @@
         )
         hidden_ref[:, part * unit : (part + 1) * unit] = hidden.astype(jnp.bfloat16)
     gate_ref[...] = jnp.broadcast_to(gate_sum, gate_ref.shape).astype(jnp.bfloat16)
-    weight_terms(recv_ref, grads_ref, hidden_ref, 1 - core_ref[0], term_ref, None)
-
-
-def weight_terms(recv_ref, grads_ref, hidden_ref, side, out_ref, add_ref, done=None):
+    weight_terms(recv_ref, grads_ref, hidden_ref, 1 - core_ref[0], term_ref)
+
+
+def weight_terms(recv_ref, grads_ref, hidden_ref, side, out_ref):
     half, columns = out_ref.shape
     unit = columns // 6
     piece = 128
@@ -197,15 +202,12 @@
         )
         for part in range(2):
             base = part * 3 * unit
-            first = up[:, 2 * part * unit : (2 * part + 2) * unit]
-            second = down[:, part * unit : (part + 1) * unit]
-            if add_ref is not None:
-                first = first + add_ref[rows, base : base + 2 * unit].astype(jnp.float32)
-                second = second + add_ref[rows, base + 2 * unit : base + 3 * unit].astype(jnp.float32)
-            out_ref[rows, base : base + 2 * unit] = first.astype(jnp.bfloat16)
-            out_ref[rows, base + 2 * unit : base + 3 * unit] = second.astype(jnp.bfloat16)
-        if done is not None:
-            done(at // blocks, rows)
+            out_ref[rows, base : base + 2 * unit] = up[
+                :, 2 * part * unit : (2 * part + 2) * unit
+            ].astype(out_ref.dtype)
+            out_ref[rows, base + 2 * unit : base + 3 * unit] = down[
+                :, part * unit : (part + 1) * unit
+            ].astype(out_ref.dtype)
 
 
 def forward(core, recv, weights):
@@ -218,40 +220,28 @@
             jax.ShapeDtypeStruct((rows, columns // 3), jnp.bfloat16),
             jax.ShapeDtypeStruct((rows, 128), jnp.bfloat16),
             jax.ShapeDtypeStruct((width // 2, columns), jnp.bfloat16),
+            pltpu.VMEM(weights.shape, weights.dtype),
         ),
         in_specs=[whole(pltpu.SMEM), whole(), whole(pl.ANY)],
-        out_specs=(whole(),) * 4,
-        scratch_shapes=[pltpu.VMEM(weights.shape, weights.dtype), pltpu.SemaphoreType.DMA((4,))],
-        compiler_params=pltpu.CompilerParams(vmem_limit_bytes=44 * MIB),
+        out_specs=(whole(),) * 5,
+        scratch_shapes=[pltpu.SemaphoreType.DMA((4,))],
+        compiler_params=pltpu.CompilerParams(vmem_limit_bytes=FORWARD_LIMIT),
         cost_estimate=cost(3 * rows * width * columns, 14 << 20),
         name="forward",
     )(core, recv, weights)
 
 
-def input_kernel(grads_ref, weight_hbm, gate_ref, out_ref, weight_ref, sems):
+def input_kernel(grads_ref, weight_ref, gate_ref, out_ref):
     width, columns = weight_ref.shape
     unit = columns // 6
     chunk = width // 2
-    pieces = [slice(3 * part * unit, (3 * part + 2) * unit) for part in range(2)]
-    copies = [
-        pltpu.make_async_copy(
-            weight_hbm.at[pl.ds(at * chunk, chunk), piece],
-            weight_ref.at[pl.ds(at * chunk, chunk), piece],
-            sems.at[2 * at + part],
-        )
-        for at in range(2)
-        for part, piece in enumerate(pieces)
-    ]
-    for copy in copies:
-        copy.start()
     for at in range(2):
         rows = slice(at * chunk, (at + 1) * chunk)
         got = 0.0
         for part in range(2):
-            copies[2 * at + part].wait()
             got = got + lax.dot_general(
                 grads_ref[:, 2 * part * unit : (2 * part + 2) * unit],
-                weight_ref[rows, pieces[part]],
+                weight_ref[rows, 3 * part * unit : (3 * part + 2) * unit],
                 CONTRACT_COLS,
                 preferred_element_type=jnp.float32,
             )
@@ -265,40 +255,56 @@
     return pl.pallas_call(
         input_kernel,
         out_shape=jax.ShapeDtypeStruct((rows, width + gate.shape[1]), jnp.bfloat16),
-        in_specs=[whole(), whole(pl.ANY), whole()],
+        in_specs=[whole()] * 3,
         out_specs=whole(),
-        scratch_shapes=[pltpu.VMEM(weights.shape, weights.dtype), pltpu.SemaphoreType.DMA((4,))],
         compiler_params=pltpu.CompilerParams(vmem_limit_bytes=20 * MIB),
         cost_estimate=cost(4 * rows * width * columns // 3, 9 << 20),
         name="input_terms",
     )(grads, weights, gate)
 
 
-def own_kernel(core_ref, recv_ref, grads_ref, hidden_ref, arrived_ref, out_hbm, out_ref, sems):
+def own_kernel(core_ref, recv_ref, grads_ref, hidden_ref, out_ref):
+    weight_terms(recv_ref, grads_ref, hidden_ref, core_ref[0], out_ref)
+
+
+def own_terms(core, recv, grads, hidden, columns):
+    rows, width = recv.shape
+    return pl.pallas_call(
+        own_kernel,
+        out_shape=jax.ShapeDtypeStruct((width // 4, columns), jnp.float32),
+        in_specs=[whole(pltpu.SMEM)] + [whole()] * 3,
+        out_specs=whole(),
+        compiler_params=pltpu.CompilerParams(vmem_limit_bytes=20 * MIB),
+        cost_estimate=cost(rows * width * columns // 2, 10 * MIB),
+        name="own_terms",
+    )(core, recv, grads, hidden)
+
+
+def add_kernel(own_ref, arrived_ref, out_hbm, out_ref, sems):
+    count = sems.shape[0]
+    rows = out_ref.shape[0] // count
     copies = []
-
-    def done(i, rows):
-        copies.append(pltpu.make_async_copy(out_ref.at[rows], out_hbm.at[rows], sems.at[i]))
+    for i in range(count):
+        at = slice(i * rows, (i + 1) * rows)
+        total = own_ref[at, :] + arrived_ref[at, :].astype(jnp.float32)
+        out_ref[at, :] = total.astype(jnp.bfloat16)
+        copies.append(pltpu.make_async_copy(out_ref.at[at], out_hbm.at[at], sems.at[i]))
         copies[-1].start()
-
-    weight_terms(recv_ref, grads_ref, hidden_ref, core_ref[0], out_ref, arrived_ref, done)
     for copy in copies:
         copy.wait()
 
 
-def own_terms(core, recv, grads, hidden, arrived):
-    rows = recv.shape[0]
-    half, columns = arrived.shape
-    return pl.pallas_call(
-        own_kernel,
-        out_shape=pltpu.HBM((half, columns), jnp.bfloat16),
-        in_specs=[whole(pltpu.SMEM)] + [whole()] * 4,
+def add(own, arrived):
+    return pl.pallas_call(
+        add_kernel,
+        out_shape=pltpu.HBM(arrived.shape, jnp.bfloat16),
+        in_specs=[whole()] * 2,
         out_specs=whole(pl.ANY),
-        scratch_shapes=[pltpu.VMEM(arrived.shape, jnp.bfloat16), pltpu.SemaphoreType.DMA((2,))],
-        compiler_params=pltpu.CompilerParams(vmem_limit_bytes=24 * MIB),
-        cost_estimate=cost(2 * rows * half * columns, 10 << 20),
-        name="own_terms",
-    )(core, recv, grads, hidden, arrived)
+        scratch_shapes=[pltpu.VMEM(arrived.shape, jnp.bfloat16), pltpu.SemaphoreType.DMA((4,))],
+        compiler_params=pltpu.CompilerParams(vmem_limit_bytes=20 * MIB),
+        cost_estimate=cost(arrived.size, 12 * MIB),
+        name="add",
+    )(own, arrived)
 
 
 def unpack_kernel(back_ref, sum_ref, gate_ref, route_ref, out_ref, gate_out_ref, table_ref, *, capacity):
@@ -388,21 +394,21 @@
     core = lax.axis_index("c").astype(jnp.int32).reshape(1)
     swap = [(0, 1), (1, 0)]
 
-    mine = join(w_gate, w_up, w_down)
-    paired = lax.ppermute(mine, "k", swap)
+    own = (w_gate, w_up, w_down)
+    partner = tuple(lax.ppermute(block, "k", swap) for block in own)
     sent = pack(inputs, cotangents, gates, route, experts, capacity)
-    paired, sent = lax.optimization_barrier((paired, sent))
+    partner, sent = lax.optimization_barrier((partner, sent))
     recv = lax.all_to_all(
         sent.reshape(experts, layers * capacity, 2 * width), "e", 0, 0, tiled=True
     ).reshape(experts * layers * capacity, 2 * width)
-    both = jnp.concatenate([mine, paired], axis=1)
-    weights = lax.all_gather(both, ("y", "c"), axis=0, tiled=True)
-
-    grads, hidden, gate_sum, term = forward(core, recv, weights)
+    weights = lax.all_gather(join(own, partner), ("y", "c"), axis=0, tiled=True)
+
+    grads, hidden, gate_sum, term, held = forward(core, recv, weights)
     arrived = lax.ppermute(term, "c", swap)
-    back = input_terms(grads, weights, gate_sum)
+    back = input_terms(grads, held, gate_sum)
     hidden, back = lax.optimization_barrier((hidden, back))
-    total = own_terms(core, recv, grads, hidden, arrived)
+    total = own_terms(core, recv, grads, hidden, weights.shape[1])
+    total = add(total, arrived)
     reduced = lax.psum_scatter(total, "y", scatter_dimension=0, tiled=True)
     back = lax.all_to_all(
         back.reshape(experts, layers * capacity, back.shape[1]), "e", 0, 0, tiled=True

time: 185 us -> 186 us (level)
  starting transfers between devices: 25.6 us -> 29.2 us
    ppermute x1 -> x3, starting transfers between devices: 7.94 us -> 13.8 us  [local(): partner = tuple((lax.ppermute(block, 'k', swap) for block in own))]
    all_to_all x1, starting transfers between devices: 9.07 us -> 6.91 us  [local(): lax.all_to_all(sent.reshape(experts, layers * capacity, 2 * width), 'e',...]
    pallas_call x2 -> x3, Pallas kernels: 4.66 us -> 4.5 us  [the longest x1 1.85 us: own_terms(): pl.pallas_call(own_kernel, out_shape=jax.ShapeDtypeStruct((width // 4, co...]
  transfers between devices with their start and end apart: 7 -> 9, of which waited for: 5 -> 4; matrix products, arithmetic and copies ran while one was open for 1% -> 1% of each run, Pallas kernels for 6% -> 6%
where the time goes in v4:
time: 186 us; the launch traced here: 185 us
  waiting for transfers between devices  119 us (64%)
  starting transfers between devices  29.2 us (16%)
  Pallas kernels  22.2 us (12%)
  between operations  14.2 us (8%)
    all_to_all x1, waiting for transfers between devices, local(): lax.all_to_all(sent.reshape(experts, layers * capacity, 2 * width), 'e',...  73.5 us
    reduce_scatter x1, waiting for transfers between devices, local(): reduced = lax.psum_scatter(total, 'y', scatter_dimension=0, tiled=True)  42.3 us
    ppermute x3, starting transfers between devices, local(): partner = tuple((lax.ppermute(block, 'k', swap) for block in own))  13.8 us
    pallas_call x1, Pallas kernels, forward(): pl.pallas_call(forward_kernel, out_shape=(jax.ShapeDtypeStruct((rows, col...  7.39 us
    all_to_all x1, starting transfers between devices, local(): lax.all_to_all(sent.reshape(experts, layers * capacity, 2 * width), 'e',...  6.91 us
    all_to_all x1, starting transfers between devices, local(): lax.all_to_all(back.reshape(experts, layers * capacity, back.shape[1]), '...  4.04 us
  transfers between devices with their start and end apart: 9, of which 4 were waited for; matrix products, arithmetic and copies ran while one was open for 1% of the time, Pallas kernels for 6%

profile of v4, /device:TPU:2, one launch (start us, length us, event | category | flops | bytes accessed | tf_op | source)
XLA Modules:
  0.0 185.5 jit_solution(5271061095149031117)
XLA Ops:
  7.2 0.0 copy-start.1
  7.2 0.0 copy-start.2
  7.2 0.0 copy-start.3
  7.2 0.0 all-gather.2.cloned.1.call-start
  7.2 7.9 %collective-permute-start = (bf16[128,256]{1,0:T(8,128)(2,1)}, bf16[128,256]{1,0:T(8,128)(2,1)S(1)}, u32[]{:S(2)}, u32[]{:S(2)}) collective-permute-start(bf16[128,256]{1,0:T(8,128)(2,1)} %refs_0_.1), channel_id=1, source_target_pairs={{0,1},{1,0},{2,3},{3,2},{4,5},{5,4},{6,7},{7,6},{8,9},{9,8},{10,11... | collective-permute-start | bytes 196616 | tf_op jit(solution)/shard_map/ppermute | solution.py:398
  15.2 1.9 %collective-permute-start.1 = (bf16[128,256]{1,0:T(8,128)(2,1)}, bf16[128,256]{1,0:T(8,128)(2,1)S(1)}, u32[]{:S(2)}, u32[]{:S(2)}) collective-permute-start(bf16[128,256]{1,0:T(8,128)(2,1)} %refs_1_.1), channel_id=1, source_target_pairs={{0,1},{1,0},{2,3},{3,2},{4,5},{5,4},{6,7},{7,6},{8,9},{9,8},{10,11... | collective-permute-start | bytes 196616 | tf_op jit(solution)/shard_map/ppermute | solution.py:398
  17.1 3.9 %collective-permute-start.2 = (bf16[256,128]{1,0:T(8,128)(2,1)}, bf16[256,128]{1,0:T(8,128)(2,1)S(1)}, u32[]{:S(2)}, u32[]{:S(2)}) collective-permute-start(bf16[256,128]{1,0:T(8,128)(2,1)} %refs_2_.1), channel_id=1, source_target_pairs={{0,1},{1,0},{2,3},{3,2},{4,5},{5,4},{6,7},{7,6},{8,9},{9,8},{10,11... | collective-permute-start | bytes 196616 | tf_op jit(solution)/shard_map/ppermute | solution.py:398
  21.1 3.6 %pack.1 = bf16[384,4096]{1,0:T(8,128)(2,1)} custom-call(bf16[2,128,2048]{2,1,0:T(8,128)(2,1)} %x_hbm.1, bf16[2,128,2048]{2,1,0:T(8,128)(2,1)} %dy_hbm.1, bf16[2,128]{1,0:T(2,128)(2,1)} %gate_ref.1, s32[2,128]{1,0:T(2,128)} %bitcast.10), custom_call_target="tpu_custom_call" | custom-call | flops 805306368 | bytes 5242880 | tf_op jit(solution)/shard_map/pack/pallas_call | solution.py:91
  24.6 0.0 collective-permute-done.refs_3_
  24.6 0.0 collective-permute-done.1.refs_4_
  24.7 0.0 collective-permute-done.2.refs_5_
  24.7 0.0 copy-done.1
  24.7 0.0 copy-done.2
  24.7 0.0 copy-done.3
  24.7 0.8 join.1
  25.5 0.0 all-gather.2.cloned.1.call-update
  25.6 6.9 %all-to-all-start = ((bf16[16,24,4096]{2,1,0:T(8,128)(2,1)}), bf16[16,24,4096]{2,1,0:T(8,128)(2,1)S(1)}, u32[]{:S(2)}, u32[]{:S(2)}) async-start(bf16[16,24,4096]{2,1,0:T(8,128)(2,1)} %bitcast.12), calls=%async_computation | async-start | bytes 6291456 | tf_op jit(solution)/shard_map/all_to_all | solution.py:401
  32.5 0.0 reduce-scatter.2.cloned.1.call-start
  32.5 73.5 %all-to-all-done = bf16[16,24,4096]{2,1,0:T(8,128)(2,1)S(1)} async-done(((bf16[16,24,4096]{2,1,0:T(8,128)(2,1)}), bf16[16,24,4096]{2,1,0:T(8,128)(2,1)S(1)}, u32[]{:S(2)}, u32[]{:S(2)}) %all-to-all-start) | async-done | bytes 3145760 | tf_op jit(solution)/shard_map/all_to_all | solution.py:401
  106.1 0.0 all-gather.2.cloned.1.call-done.weight_hbm
  106.1 7.4 %forward.1 = (bf16[384,1024]{1,0:T(8,128)(2,1)S(1)}, bf16[384,512]{1,0:T(8,128)(2,1)S(1)}, bf16[384,128]{1,0:T(8,128)(2,1)S(1)}, bf16[1024,1536]{1,0:T(8,128)(2,1)S(1)}, bf16[2048,1536]{1,0:T(8,128)(2,1)S(1)}) custom-call(s32[1]{0:T(128)} %bitcast.core_ref, bf16[384,4096]{1,0:T(8,128)(2,1)S(1)} %bitcast.8, ...), custom_call_target="tpu_custom_call" | custom-call | flops 3623878656 | bytes 14680064 | tf_op jit(solution)/shard_map/forward/pallas_call | solution.py:216
  113.5 1.9 %collective-permute-start.3 = (bf16[1024,1536]{1,0:T(8,128)(2,1)S(1)}, bf16[1024,1536]{1,0:T(8,128)(2,1)S(1)}, u32[]{:S(2)}, u32[]{:S(2)}) collective-permute-start(bf16[1024,1536]{1,0:T(8,128)(2,1)S(1)} %get-tuple-element.33), channel_id=1, source_target_pairs={{0,32},{32,0},{1,33},{33,1},{2,34},{34,2},{3,35},{35,3},{4,36},{36... | collective-permute-start | bytes 9437192 | tf_op jit(solution)/shard_map/ppermute | solution.py:407
  115.4 3.0 %input_terms.1 = bf16[384,2176]{1,0:T(8,128)(2,1)} custom-call(bf16[384,1024]{1,0:T(8,128)(2,1)S(1)} %get-tuple-element.26.grads_ref, bf16[2048,1536]{1,0:T(8,128)(2,1)S(1)} %get-tuple-element.27.weight_ref, bf16[384,128]{1,0:T(8,128)(2,1)S(1)} %get-tuple-element.28.gate_ref), custom_call_target="tpu_custom_call" | custom-call | flops 1610612736 | bytes 9437184 | tf_op jit(solution)/shard_map/input_terms/pallas_call | solution.py:255
  118.4 1.8 own_terms.1.own_ref
  120.3 0.7 collective-permute-done.3.arrived_ref
  121.0 1.8 add.4
  122.8 0.0 copy-start.4
  122.8 0.0 copy-start.5
  122.9 0.0 reduce-scatter.2.cloned.1.call-update
  122.9 4.0 %all-to-all-start.1 = ((bf16[16,24,2176]{2,1,0:T(8,128)(2,1)}), bf16[16,24,2176]{2,1,0:T(8,128)(2,1)S(1)}, u32[]{:S(2)}, u32[]{:S(2)}) async-start(bf16[16,24,2176]{2,1,0:T(8,128)(2,1)} %bitcast.4), calls=%async_computation.1 | async-start | bytes 3342336 | tf_op jit(solution)/shard_map/all_to_all | solution.py:413
  126.9 42.3 %reduce-scatter.2.cloned.1.call-done.reduced_ref = bf16[128,1536]{1,0:T(8,128)(2,1)} async-done(((bf16[1024,1536]{1,0:T(8,128)(2,1)}), bf16[128,1536]{1,0:T(8,128)(2,1)}) %reduce-scatter.2.cloned.1.call-update) | async-done | bytes 393232 | tf_op jit(solution)/shard_map/reduce_scatter | solution.py:412
  169.2 0.0 copy-start
  169.3 1.0 slice.4
  170.3 2.5 %collective-permute-start.4 = (bf16[128,768]{1,0:T(8,128)(2,1)S(1)}, bf16[128,768]{1,0:T(8,128)(2,1)S(1)}, u32[]{:S(2)}, u32[]{:S(2)}) collective-permute-start(bf16[128,768]{1,0:T(8,128)(2,1)S(1)} %slice.4), channel_id=1, source_target_pairs={{0,1},{1,0},{2,3},{3,2},{4,5},{5,4},{6,7},{7,6},{8,9},{9,8},{10,11... | collective-permute-start | bytes 589832 | tf_op jit(solution)/shard_map/ppermute | solution.py:417
  172.7 0.0 all-to-all-done.1
  172.7 0.0 copy-done.4
  172.7 0.0 copy-done.5
  172.8 2.9 %unpack.1 = (bf16[2,128,2048]{2,1,0:T(8,128)(2,1)}, bf16[2,128]{1,0:T(2,128)(2,1)}) custom-call(bf16[384,2176]{1,0:T(8,128)(2,1)S(1)} %bitcast.6, bf16[384,2176]{1,0:T(8,128)(2,1)S(1)} %bitcast.7, bf16[2,128]{1,0:T(2,128)(2,1)S(1)} %copy-done.5, s32[2,128]{1,0:T(2,128)S(1)} %bitcast.11), custom_call_target="tpu_custom_call" | custom-call | flops 402653184 | bytes 3145728 | tf_op jit(solution)/shard_map/unpack/pallas_call | solution.py:337
  175.7 2.2 %collective-permute-done.4.partner_ref = bf16[128,768]{1,0:T(8,128)(2,1)S(1)} collective-permute-done((bf16[128,768]{1,0:T(8,128)(2,1)S(1)}, bf16[128,768]{1,0:T(8,128)(2,1)S(1)}, u32[]{:S(2)}, u32[]{:S(2)}) %collective-permute-start.4) | collective-permute-done | bytes 196640 | tf_op jit(solution)/shard_map/ppermute | solution.py:417
  177.8 0.0 copy-done
  177.8 0.8 finish.1
Async XLA Ops:
  7.2 17.5 %copy-start.1 = (bf16[128,256]{1,0:T(8,128)(2,1)S(1)}, bf16[128,256]{1,0:T(8,128)(2,1)}, u32[]{:S(2)}) copy-start(bf16[128,256]{1,0:T(8,128)(2,1)} %refs_0_.1) | copy-start | bytes 196612
  7.2 17.5 %copy-start.2 = (bf16[128,256]{1,0:T(8,128)(2,1)S(1)}, bf16[128,256]{1,0:T(8,128)(2,1)}, u32[]{:S(2)}) copy-start(bf16[128,256]{1,0:T(8,128)(2,1)} %refs_1_.1) | copy-start | bytes 196612
  7.2 17.5 %copy-start.3 = (bf16[256,128]{1,0:T(8,128)(2,1)S(1)}, bf16[256,128]{1,0:T(8,128)(2,1)}, u32[]{:S(2)}) copy-start(bf16[256,128]{1,0:T(8,128)(2,1)} %refs_2_.1) | copy-start | bytes 196612
  7.2 98.9 %all-gather.2.cloned.1.call-start = ((), (), s32[]{:S(2)}) async-start(), calls=%async_computation.3 | async-start | bytes 6684672 | tf_op jit(solution)/shard_map/all_gather | solution.py:404
  7.2 17.4 %collective-permute-start = (bf16[128,256]{1,0:T(8,128)(2,1)}, bf16[128,256]{1,0:T(8,128)(2,1)S(1)}, u32[]{:S(2)}, u32[]{:S(2)}) collective-permute-start(bf16[128,256]{1,0:T(8,128)(2,1)} %refs_0_.1), channel_id=1, source_target_pairs={{0,1},{1,0},{2,3},{3,2},{4,5},{5,4},{6,7},{7,6},{8,9},{9,8},{10,11... | collective-permute-start | bytes 196616 | tf_op jit(solution)/shard_map/ppermute | solution.py:398
  15.2 9.5 %collective-permute-start.1 = (bf16[128,256]{1,0:T(8,128)(2,1)}, bf16[128,256]{1,0:T(8,128)(2,1)S(1)}, u32[]{:S(2)}, u32[]{:S(2)}) collective-permute-start(bf16[128,256]{1,0:T(8,128)(2,1)} %refs_1_.1), channel_id=1, source_target_pairs={{0,1},{1,0},{2,3},{3,2},{4,5},{5,4},{6,7},{7,6},{8,9},{9,8},{10,11... | collective-permute-start | bytes 196616 | tf_op jit(solution)/shard_map/ppermute | solution.py:398
  17.1 7.5 %collective-permute-start.2 = (bf16[256,128]{1,0:T(8,128)(2,1)}, bf16[256,128]{1,0:T(8,128)(2,1)S(1)}, u32[]{:S(2)}, u32[]{:S(2)}) collective-permute-start(bf16[256,128]{1,0:T(8,128)(2,1)} %refs_2_.1), channel_id=1, source_target_pairs={{0,1},{1,0},{2,3},{3,2},{4,5},{5,4},{6,7},{7,6},{8,9},{9,8},{10,11... | collective-permute-start | bytes 196616 | tf_op jit(solution)/shard_map/ppermute | solution.py:398
  25.6 80.5 %all-to-all-start = ((bf16[16,24,4096]{2,1,0:T(8,128)(2,1)}), bf16[16,24,4096]{2,1,0:T(8,128)(2,1)S(1)}, u32[]{:S(2)}, u32[]{:S(2)}) async-start(bf16[16,24,4096]{2,1,0:T(8,128)(2,1)} %bitcast.12), calls=%async_computation | async-start | bytes 6291456 | tf_op jit(solution)/shard_map/all_to_all | solution.py:401
  32.5 136.8 %reduce-scatter.2.cloned.1.call-start = ((), (), s32[]{:S(2)}) async-start(), calls=%async_computation.4 | async-start | bytes 3538944 | tf_op jit(solution)/shard_map/reduce_scatter | solution.py:412
  113.5 7.6 %collective-permute-start.3 = (bf16[1024,1536]{1,0:T(8,128)(2,1)S(1)}, bf16[1024,1536]{1,0:T(8,128)(2,1)S(1)}, u32[]{:S(2)}, u32[]{:S(2)}) collective-permute-start(bf16[1024,1536]{1,0:T(8,128)(2,1)S(1)} %get-tuple-element.33), channel_id=1, source_target_pairs={{0,32},{32,0},{1,33},{33,1},{2,34},{34,2},{3,35},{35,3},{4,36},{36... | collective-permute-start | bytes 9437192 | tf_op jit(solution)/shard_map/ppermute | solution.py:407
  122.8 49.9 %copy-start.4 = (s32[2,128,1]{1,2,0:T(1,128)S(1)}, s32[2,128,1]{1,2,0:T(1,128)}, u32[]{:S(2)}) copy-start(s32[2,128,1]{1,2,0:T(1,128)} %param.10) | copy-start | bytes 3076
  122.8 49.9 %copy-start.5 = (bf16[2,128]{1,0:T(2,128)(2,1)S(1)}, bf16[2,128]{1,0:T(2,128)(2,1)}, u32[]{:S(2)}) copy-start(bf16[2,128]{1,0:T(2,128)(2,1)} %gate_ref.1) | copy-start | bytes 1540
  122.9 49.9 %all-to-all-start.1 = ((bf16[16,24,2176]{2,1,0:T(8,128)(2,1)}), bf16[16,24,2176]{2,1,0:T(8,128)(2,1)S(1)}, u32[]{:S(2)}, u32[]{:S(2)}) async-start(bf16[16,24,2176]{2,1,0:T(8,128)(2,1)} %bitcast.4), calls=%async_computation.1 | async-start | bytes 3342336 | tf_op jit(solution)/shard_map/all_to_all | solution.py:413
  169.2 8.6 %copy-start = (bf16[128,1536]{1,0:T(8,128)(2,1)S(1)}, bf16[128,1536]{1,0:T(8,128)(2,1)}, u32[]{:S(2)}) copy-start(bf16[128,1536]{1,0:T(8,128)(2,1)} %reduce-scatter.2.cloned.1.call-done.reduced_ref) | copy-start | bytes 1179652
  170.3 7.6 %collective-permute-start.4 = (bf16[128,768]{1,0:T(8,128)(2,1)S(1)}, bf16[128,768]{1,0:T(8,128)(2,1)S(1)}, u32[]{:S(2)}, u32[]{:S(2)}) collective-permute-start(bf16[128,768]{1,0:T(8,128)(2,1)S(1)} %slice.4), channel_id=1, source_target_pairs={{0,1},{1,0},{2,3},{3,2},{4,5},{5,4},{6,7},{7,6},{8,9},{9,8},{10,11... | collective-permute-start | bytes 589832 | tf_op jit(solution)/shard_map/ppermute | solution.py:417
Sparse Core Ops, SparseCore 0:
  25.7 48.4 all-gather.1
  123.0 46.2 reduce-scatter.1

commit v5 on v4

--- a/solution.py
+++ b/solution.py
@@ -11,6 +11,7 @@
 MIB = 1024 * 1024
 PACK_LIMIT = 56 * MIB
 FORWARD_LIMIT = 38 * MIB
+JOIN_LIMIT = 60 * MIB
 CONTRACT_ROWS = (((0,), (0,)), ((), ()))
 CONTRACT_COLS = (((1,), (1,)), ((), ()))
 
@@ -108,60 +109,114 @@
     )(x, dy, gates, route)
 
 
-def join_kernel(*refs):
-    out_ref = refs[-1]
-    unit = refs[0].shape[1]
-    for part in range(2):
-        gate_ref, up_ref, down_ref = refs[3 * part : 3 * part + 3]
-        base = 3 * part * unit
-        out_ref[:, base : base + unit] = gate_ref[...]
-        out_ref[:, base + unit : base + 2 * unit] = up_ref[...]
-        out_ref[:, base + 2 * unit : base + 3 * unit] = down_ref[...].T
-
-
-def join(own, partner):
-    piece, unit = own[0].shape
+def join_kernel(gate_hbm, up_hbm, down_hbm, out_ref, down_ref, sems):
+    unit = gate_hbm.shape[1]
+    moves = (
+        (down_hbm, down_ref),
+        (gate_hbm, out_ref.at[:, :unit]),
+        (up_hbm, out_ref.at[:, unit : 2 * unit]),
+    )
+    copies = [pltpu.make_async_copy(src, dst, sems.at[i]) for i, (src, dst) in enumerate(moves)]
+    for copy in copies:
+        copy.start()
+    copies[0].wait()
+    out_ref[:, 2 * unit :] = down_ref[...].T
+    for copy in copies[1:]:
+        copy.wait()
+
+
+def join(w_gate, w_up, w_down):
+    piece, unit = w_gate.shape
     return pl.pallas_call(
         join_kernel,
-        out_shape=pltpu.HBM((piece, 6 * unit), jnp.bfloat16),
-        in_specs=[whole()] * 6,
+        out_shape=jax.ShapeDtypeStruct((piece, 3 * unit), jnp.bfloat16),
+        in_specs=[whole(pl.ANY)] * 3,
         out_specs=whole(),
-        compiler_params=pltpu.CompilerParams(vmem_limit_bytes=8 * MIB),
+        scratch_shapes=[pltpu.VMEM(w_down.shape, w_down.dtype), pltpu.SemaphoreType.DMA((3,))],
+        compiler_params=pltpu.CompilerParams(vmem_limit_bytes=JOIN_LIMIT),
         cost_estimate=cost(0, MIB),
         name="join",
-    )(*own, *partner)
-
-
-def weight_copies(weight_hbm, weight_ref, sems, pieces):
+    )(w_gate, w_up, w_down)
+
+
+def order_kernel(place_ref, *refs):
+    count = len(refs) - 2
+    out_hbm, sems = refs[count], refs[count + 1]
     copies = [
-        pltpu.make_async_copy(weight_hbm.at[:, piece], weight_ref.at[:, piece], sems.at[i])
-        for i, piece in enumerate(pieces)
+        pltpu.make_async_copy(refs[i], out_hbm.at[lax.rem(place_ref[0] + i, count)], sems.at[i])
+        for i in range(count)
     ]
     for copy in copies:
         copy.start()
-    return copies
+    for copy in copies:
+        copy.wait()
+
+
+def order(place, blocks):
+    shape = (len(blocks),) + blocks[0].shape
+    return pl.pallas_call(
+        order_kernel,
+        out_shape=pltpu.HBM(shape, blocks[0].dtype),
+        in_specs=[whole(pltpu.SMEM)] + [whole(pl.ANY)] * len(blocks),
+        out_specs=whole(pl.ANY),
+        scratch_shapes=[pltpu.SemaphoreType.DMA((len(blocks),))],
+        compiler_params=pltpu.CompilerParams(vmem_limit_bytes=JOIN_LIMIT),
+        cost_estimate=cost(0, 6 * MIB),
+        name="order",
+    )(place, *blocks)
+
+
+def ring_gather(block):
+    count = lax.axis_size("y")
+    place = lax.axis_index("y").astype(jnp.int32).reshape(1)
+    up = [(j, (j + 1) % count) for j in range(count)]
+    down = [(j, (j - 1) % count) for j in range(count)]
+    blocks = [block] * count
+    fromdown = fromup = block
+    for step in range(1, count // 2 + 1):
+        fromdown = lax.ppermute(fromdown, "y", up)
+        blocks[count - step] = fromdown
+        if step < count - count // 2:
+            fromup = lax.ppermute(fromup, "y", down)
+            blocks[step] = fromup
+    return order(place, blocks)
 
 
 def forward_kernel(
-    core_ref, recv_ref, weight_hbm, grads_ref, hidden_ref, gate_ref, term_ref, weight_ref, sems
+    core_ref, recv_ref, own_hbm, other_hbm, grads_ref, hidden_ref, gate_ref, term_ref, held_ref, sems
 ):
-    width, columns = weight_ref.shape
+    count, piece, columns = own_hbm.shape
+    width = 2 * count * piece
     unit = columns // 6
     pieces = []
     for part in range(2):
         base = part * 3 * unit
         pieces += [slice(base, base + 2 * unit), slice(base + 2 * unit, base + 3 * unit)]
-    copies = weight_copies(weight_hbm, weight_ref, sems, pieces)
+    copies = []
+    for part in range(2):
+        at = slice(3 * part * unit, 3 * (part + 1) * unit)
+        for side, src in enumerate((own_hbm, other_hbm)):
+            copies.append(
+                pltpu.make_async_copy(
+                    src.at[:, :, at],
+                    held_ref.at[:, lax.rem(core_ref[0] + side, 2), :, at],
+                    sems.at[2 * part + side],
+                )
+            )
+    for copy in copies:
+        copy.start()
     gate_sum = 0.0
     for part in range(2):
         copies[2 * part].wait()
+        copies[2 * part + 1].wait()
         pre = jnp.dot(
-            recv_ref[:, :width], weight_ref[:, pieces[2 * part]], preferred_element_type=jnp.float32
+            recv_ref[:, :width],
+            held_ref[:, :, :, pieces[2 * part]].reshape(width, 2 * unit),
+            preferred_element_type=jnp.float32,
         )
-        copies[2 * part + 1].wait()
         back = jnp.dot(
             recv_ref[:, width:],
-            weight_ref[:, pieces[2 * part + 1]],
+            held_ref[:, :, :, pieces[2 * part + 1]].reshape(width, unit),
             preferred_element_type=jnp.float32,
         )
         gate_pre, up_value = pre[:, :unit], pre[:, unit:]
@@ -210,9 +265,10 @@
             ].astype(out_ref.dtype)
 
 
-def forward(core, recv, weights):
+def forward(core, recv, own, other):
     rows = recv.shape[0]
-    width, columns = weights.shape
+    count, piece, columns = own.shape
+    width = 2 * count * piece
     return pl.pallas_call(
         forward_kernel,
         out_shape=(
@@ -220,38 +276,42 @@
             jax.ShapeDtypeStruct((rows, columns // 3), jnp.bfloat16),
             jax.ShapeDtypeStruct((rows, 128), jnp.bfloat16),
             jax.ShapeDtypeStruct((width // 2, columns), jnp.bfloat16),
-            pltpu.VMEM(weights.shape, weights.dtype),
+            pltpu.VMEM((count, 2, piece, columns), own.dtype),
         ),
-        in_specs=[whole(pltpu.SMEM), whole(), whole(pl.ANY)],
+        in_specs=[whole(pltpu.SMEM), whole(), whole(pl.ANY), whole(pl.ANY)],
         out_specs=(whole(),) * 5,
         scratch_shapes=[pltpu.SemaphoreType.DMA((4,))],
         compiler_params=pltpu.CompilerParams(vmem_limit_bytes=FORWARD_LIMIT),
         cost_estimate=cost(3 * rows * width * columns, 14 << 20),
         name="forward",
-    )(core, recv, weights)
-
-
-def input_kernel(grads_ref, weight_ref, gate_ref, out_ref):
-    width, columns = weight_ref.shape
+    )(core, recv, own, other)
+
+
+def input_kernel(grads_ref, held_ref, gate_ref, out_ref):
+    count, _, piece, columns = held_ref.shape
     unit = columns // 6
+    width = 2 * count * piece
     chunk = width // 2
     for at in range(2):
-        rows = slice(at * chunk, (at + 1) * chunk)
+        blocks = slice(at * count // 2, (at + 1) * count // 2)
         got = 0.0
         for part in range(2):
             got = got + lax.dot_general(
                 grads_ref[:, 2 * part * unit : (2 * part + 2) * unit],
-                weight_ref[rows, 3 * part * unit : (3 * part + 2) * unit],
+                held_ref[blocks, :, :, 3 * part * unit : (3 * part + 2) * unit].reshape(
+                    chunk, 2 * unit
+                ),
                 CONTRACT_COLS,
                 preferred_element_type=jnp.float32,
             )
-        out_ref[:, rows] = got.astype(jnp.bfloat16)
+        out_ref[:, at * chunk : (at + 1) * chunk] = got.astype(jnp.bfloat16)
     out_ref[:, width:] = gate_ref[...]
 
 
 def input_terms(grads, weights, gate):
     rows = grads.shape[0]
-    width, columns = weights.shape
+    count, _, piece, columns = weights.shape
+    width = 2 * count * piece
     return pl.pallas_call(
         input_kernel,
         out_shape=jax.ShapeDtypeStruct((rows, width + gate.shape[1]), jnp.bfloat16),
@@ -394,20 +454,21 @@
     core = lax.axis_index("c").astype(jnp.int32).reshape(1)
     swap = [(0, 1), (1, 0)]
 
-    own = (w_gate, w_up, w_down)
-    partner = tuple(lax.ppermute(block, "k", swap) for block in own)
     sent = pack(inputs, cotangents, gates, route, experts, capacity)
-    partner, sent = lax.optimization_barrier((partner, sent))
+    sent, w_gate = lax.optimization_barrier((sent, w_gate))
+    mine = join(w_gate, w_up, w_down)
+    paired = lax.ppermute(mine, "k", swap)
     recv = lax.all_to_all(
         sent.reshape(experts, layers * capacity, 2 * width), "e", 0, 0, tiled=True
     ).reshape(experts * layers * capacity, 2 * width)
-    weights = lax.all_gather(join(own, partner), ("y", "c"), axis=0, tiled=True)
-
-    grads, hidden, gate_sum, term, held = forward(core, recv, weights)
+    own = ring_gather(jnp.concatenate([mine, paired], axis=1))
+    other = lax.ppermute(own, "c", swap)
+
+    grads, hidden, gate_sum, term, held = forward(core, recv, own, other)
     arrived = lax.ppermute(term, "c", swap)
     back = input_terms(grads, held, gate_sum)
     hidden, back = lax.optimization_barrier((hidden, back))
-    total = own_terms(core, recv, grads, hidden, weights.shape[1])
+    total = own_terms(core, recv, grads, hidden, own.shape[2])
     total = add(total, arrived)
     reduced = lax.psum_scatter(total, "y", scatter_dimension=0, tiled=True)
     back = lax.all_to_all(

time: 186 us -> 270 us (1.45)
  Pallas kernels: 22.2 us -> 119 us
  waiting for transfers between devices: 119 us -> 80.9 us
  starting transfers between devices: 29.2 us -> 52.5 us
    pallas_call x1 -> x2, Pallas kernels: 0.84 us -> 98.1 us  [the longest x1 96.5 us: order(): pl.pallas_call(order_kernel, out_shape=pltpu.HBM(shape, blocks[0].dtype),...]
    all_to_all x1, waiting for transfers between devices: 73.5 us -> 0.01 us  [local(): lax.all_to_all(sent.reshape(experts, layers * capacity, 2 * width), 'e',...]
    ppermute x3 -> x9, waiting for transfers between devices: 0.01 us -> 36.6 us  [the longest x4 25.3 us: ring_gather(): fromdown = lax.ppermute(fromdown, 'y', up)]
    ppermute x3 -> x9, starting transfers between devices: 13.8 us -> 28.6 us  [the longest x3 14.1 us: ring_gather(): fromup = lax.ppermute(fromup, 'y', down)]
    all_to_all x1, starting transfers between devices: 6.91 us -> 12 us  [local(): lax.all_to_all(sent.reshape(experts, layers * capacity, 2 * width), 'e',...]
    all_to_all x1, starting transfers between devices: 4.04 us -> 7.44 us  [local(): lax.all_to_all(back.reshape(experts, layers * capacity, back.shape[1]), '...]
  transfers between devices with their start and end apart: 9 -> 14, of which waited for: 4 -> 9; matrix products, arithmetic and copies ran while one was open for 1% -> 1% of each run, Pallas kernels for 6% -> 39%
where the time goes in v5:
time: 270 us; the launch traced here: 269 us
  Pallas kernels  119 us (44%)
  waiting for transfers between devices  80.9 us (30%)
  starting transfers between devices  52.5 us (19%)
  between operations  14.3 us (5%)
    pallas_call x1, Pallas kernels, order(): pl.pallas_call(order_kernel, out_shape=pltpu.HBM(shape, blocks[0].dtype),...  96.5 us
    reduce_scatter x1, waiting for transfers between devices, local(): reduced = lax.psum_scatter(total, 'y', scatter_dimension=0, tiled=True)  41.5 us
    ppermute x4, waiting for transfers between devices, ring_gather(): fromdown = lax.ppermute(fromdown, 'y', up)  25.3 us
    ppermute x3, starting transfers between devices, ring_gather(): fromup = lax.ppermute(fromup, 'y', down)  14.1 us
    all_to_all x1, starting transfers between devices, local(): lax.all_to_all(sent.reshape(experts, layers * capacity, 2 * width), 'e',...  12 us
    ppermute x4, starting transfers between devices, ring_gather(): fromdown = lax.ppermute(fromdown, 'y', up)  9.22 us
    all_to_all x1, starting transfers between devices, local(): lax.all_to_all(back.reshape(experts, layers * capacity, back.shape[1]), '...  7.44 us
    pallas_call x1, Pallas kernels, forward(): pl.pallas_call(forward_kernel, out_shape=(jax.ShapeDtypeStruct((rows, col...  7.44 us
  transfers between devices with their start and end apart: 14, of which 9 were waited for; matrix products, arithmetic and copies ran while one was open for 1% of the time, Pallas kernels for 39%

profile of v5, /device:TPU:2, one launch (start us, length us, event | category | flops | bytes accessed | tf_op | source)
XLA Modules:
  0.0 269.2 jit_solution(4712994064861731495)
XLA Ops:
  7.2 3.6 %pack.1 = bf16[384,4096]{1,0:T(8,128)(2,1)} custom-call(bf16[2,128,2048]{2,1,0:T(8,128)(2,1)} %x_hbm.1, bf16[2,128,2048]{2,1,0:T(8,128)(2,1)} %dy_hbm.1, bf16[2,128]{1,0:T(2,128)(2,1)} %gate_ref.1, s32[2,128]{1,0:T(2,128)} %bitcast.11), custom_call_target="tpu_custom_call" | custom-call | flops 805306368 | bytes 5242880 | tf_op jit(solution)/shard_map/pack/pallas_call | solution.py:92
  10.8 12.0 %all-to-all-start = ((bf16[16,24,4096]{2,1,0:T(8,128)(2,1)}), bf16[16,24,4096]{2,1,0:T(8,128)(2,1)S(1)}, u32[]{:S(2)}, u32[]{:S(2)}) async-start(bf16[16,24,4096]{2,1,0:T(8,128)(2,1)} %bitcast.13), calls=%async_computation | async-start | bytes 6291456 | tf_op jit(solution)/shard_map/all_to_all | solution.py:461
  22.8 0.0 reduce-scatter.2.cloned.1.call-start
  22.8 1.6 join.1
  24.5 3.3 %collective-permute-start = (bf16[128,768]{1,0:T(8,128)(2,1)}, bf16[128,768]{1,0:T(8,128)(2,1)S(1)}, u32[]{:S(2)}, u32[]{:S(2)}) collective-permute-start(bf16[128,768]{1,0:T(8,128)(2,1)} %join.1), channel_id=1, source_target_pairs={{0,1},{1,0},{2,3},{3,2},{4,5},{5,4},{6,7},{7,6},{8,9},{9,8},{10,11... | collective-permute-start | bytes 589832 | tf_op jit(solution)/shard_map/ppermute | solution.py:460
  27.8 5.4 %collective-permute-done = bf16[128,768]{1,0:T(8,128)(2,1)S(1)} collective-permute-done((bf16[128,768]{1,0:T(8,128)(2,1)}, bf16[128,768]{1,0:T(8,128)(2,1)S(1)}, u32[]{:S(2)}, u32[]{:S(2)}) %collective-permute-start) | collective-permute-done | bytes 196640 | tf_op jit(solution)/shard_map/ppermute | solution.py:460
  33.2 1.0 pad_maximum_fusion.refs_0_
  34.1 0.0 copy-start.3
  34.1 3.5 %collective-permute-start.4 = (bf16[128,1536]{1,0:T(8,128)(2,1)S(1)}, bf16[128,1536]{1,0:T(8,128)(2,1)S(1)}, u32[]{:S(2)}, u32[]{:S(2)}) collective-permute-start(bf16[128,1536]{1,0:T(8,128)(2,1)S(1)} %pad_maximum_fusion.refs_0_), channel_id=1, source_target_pairs={{0,64},{64,128},{128,192},{192,256},{256,320},{320,384},{384,448},... | collective-permute-start | bytes 1179656 | tf_op jit(solution)/shard_map/ppermute | solution.py:177
  37.6 3.8 %collective-permute-start.1 = (bf16[128,1536]{1,0:T(8,128)(2,1)S(1)}, bf16[128,1536]{1,0:T(8,128)(2,1)S(1)}, u32[]{:S(2)}, u32[]{:S(2)}) collective-permute-start(bf16[128,1536]{1,0:T(8,128)(2,1)S(1)} %pad_maximum_fusion.refs_0_), channel_id=1, source_target_pairs={{0,448},{64,0},{128,64},{192,128},{256,192},{320,256},{384,320},{4... | collective-permute-start | bytes 1179656 | tf_op jit(solution)/shard_map/ppermute | solution.py:180
  41.5 6.2 %collective-permute-done.4.refs_7_ = bf16[128,1536]{1,0:T(8,128)(2,1)S(1)} collective-permute-done((bf16[128,1536]{1,0:T(8,128)(2,1)S(1)}, bf16[128,1536]{1,0:T(8,128)(2,1)S(1)}, u32[]{:S(2)}, u32[]{:S(2)}) %collective-permute-start.4) | collective-permute-done | bytes 393248 | tf_op jit(solution)/shard_map/ppermute | solution.py:177
  47.7 0.0 copy-start.4
  47.7 1.9 collective-permute-start.5
  49.6 0.0 collective-permute-done.1.refs_1_
  49.6 0.0 copy-done.4
  49.6 0.0 copy-start.5
  49.6 5.1 %collective-permute-start.2 = (bf16[128,1536]{1,0:T(8,128)(2,1)S(1)}, bf16[128,1536]{1,0:T(8,128)(2,1)}, u32[]{:S(2)}, u32[]{:S(2)}) collective-permute-start(bf16[128,1536]{1,0:T(8,128)(2,1)S(1)} %collective-permute-done.1.refs_1_), channel_id=1, source_target_pairs={{0,448},{64,0},{128,64},{192,128},{256,192},{320,256},{384,320},{4... | collective-permute-start | bytes 1179656 | tf_op jit(solution)/shard_map/ppermute | solution.py:180
  54.8 5.3 %collective-permute-done.5.refs_6_ = bf16[128,1536]{1,0:T(8,128)(2,1)S(1)} collective-permute-done((bf16[128,1536]{1,0:T(8,128)(2,1)S(1)}, bf16[128,1536]{1,0:T(8,128)(2,1)S(1)}, u32[]{:S(2)}, u32[]{:S(2)}) %collective-permute-start.5) | collective-permute-done | bytes 393248 | tf_op jit(solution)/shard_map/ppermute | solution.py:177
  60.1 0.0 copy-done.5
  60.1 0.0 copy-start.6
  60.1 1.9 collective-permute-start.6
  62.0 0.0 collective-permute-done.2.refs_2_
  62.0 0.0 copy-done.6
  62.0 5.1 %collective-permute-start.3 = (bf16[128,1536]{1,0:T(8,128)(2,1)}, bf16[128,1536]{1,0:T(8,128)(2,1)}, u32[]{:S(2)}, u32[]{:S(2)}) collective-permute-start(bf16[128,1536]{1,0:T(8,128)(2,1)} %collective-permute-done.2.refs_2_), channel_id=1, source_target_pairs={{0,448},{64,0},{128,64},{192,128},{256,192},{320,256},{384,320},{4... | collective-permute-start | bytes 1179656 | tf_op jit(solution)/shard_map/ppermute | solution.py:180
  67.2 4.5 %collective-permute-done.6.refs_5_ = bf16[128,1536]{1,0:T(8,128)(2,1)} collective-permute-done((bf16[128,1536]{1,0:T(8,128)(2,1)S(1)}, bf16[128,1536]{1,0:T(8,128)(2,1)}, u32[]{:S(2)}, u32[]{:S(2)}) %collective-permute-start.6) | collective-permute-done | bytes 393248 | tf_op jit(solution)/shard_map/ppermute | solution.py:177
  71.6 1.9 collective-permute-start.7
  73.6 0.0 collective-permute-done.3.refs_3_
  73.6 9.3 %collective-permute-done.7.refs_4_ = bf16[128,1536]{1,0:T(8,128)(2,1)} collective-permute-done((bf16[128,1536]{1,0:T(8,128)(2,1)}, bf16[128,1536]{1,0:T(8,128)(2,1)}, u32[]{:S(2)}, u32[]{:S(2)}) %collective-permute-start.7) | collective-permute-done | bytes 393248 | tf_op jit(solution)/shard_map/ppermute | solution.py:177
  82.8 0.0 copy-done.3
  82.8 96.5 %order.1.own_hbm = bf16[8,128,1536]{2,1,0:T(8,128)(2,1)} custom-call(s32[1]{0:T(128)} %bitcast.4.place_ref, bf16[128,1536]{1,0:T(8,128)(2,1)} %copy-done.3, bf16[128,1536]{1,0:T(8,128)(2,1)} %copy-done.5, bf16[128,1536]{1,0:T(8,128)(2,1)} %collective-permute-done.2.refs_2_, bf16[128,1536]{1,0:T(8,128)(2,1)} %collective-permute-done.3.refs_3_, ...), custom_call_target="tpu_custom_call" | custom-call | bytes 6291456 | tf_op jit(solution)/shard_map/order/pallas_call | solution.py:157
  179.3 1.9 collective-permute-start.8
  181.2 6.0 %collective-permute-done.8.other_hbm = bf16[8,128,1536]{2,1,0:T(8,128)(2,1)} collective-permute-done((bf16[8,128,1536]{2,1,0:T(8,128)(2,1)}, bf16[8,128,1536]{2,1,0:T(8,128)(2,1)}, u32[]{:S(2)}, u32[]{:S(2)}) %collective-permute-start.8) | collective-permute-done | bytes 3145760 | tf_op jit(solution)/shard_map/ppermute | solution.py:465
  187.2 0.0 all-to-all-done
  187.2 7.4 %forward.1 = (bf16[384,1024]{1,0:T(8,128)(2,1)S(1)}, bf16[384,512]{1,0:T(8,128)(2,1)S(1)}, bf16[384,128]{1,0:T(8,128)(2,1)S(1)}, bf16[1024,1536]{1,0:T(8,128)(2,1)S(1)}, bf16[8,2,128,1536]{3,2,1,0:T(8,128)(2,1)S(1)}) custom-call(s32[1]{0:T(128)} %bitcast.core_ref, bf16[384,4096]{1,0:T(8,128)(2,1)S(1)} %bitcast.9, bf16[8,128,1536]{2,1,0:T(8,128)(2,1)} %order.1.own_hbm, ...), custom_call_target="tpu_custom_call" | custom-call | flops 3623878656 | bytes 14680064 | tf_op jit(solution)/shard_map/forward/pallas_call | solution.py:272
  194.6 2.0 collective-permute-start.9
  196.7 3.0 %input_terms.1 = bf16[384,2176]{1,0:T(8,128)(2,1)} custom-call(bf16[384,1024]{1,0:T(8,128)(2,1)S(1)} %get-tuple-element.22.grads_ref, bf16[8,2,128,1536]{3,2,1,0:T(8,128)(2,1)S(1)} %get-tuple-element.23.held_ref, bf16[384,128]{1,0:T(8,128)(2,1)S(1)} %get-tuple-element.24.gate_ref), custom_call_target="tpu_custom_call" | custom-call | flops 1610612736 | bytes 9437184 | tf_op jit(solution)/shard_map/input_terms/pallas_call | solution.py:315
  199.7 1.8 own_terms.1.own_ref
  201.6 0.6 collective-permute-done.9.arrived_ref
  202.2 1.8 add.4
  204.0 0.0 copy-start.1
  204.0 0.0 copy-start.2
  204.0 0.0 reduce-scatter.2.cloned.1.call-update
  204.1 7.4 %all-to-all-start.1 = ((bf16[16,24,2176]{2,1,0:T(8,128)(2,1)}), bf16[16,24,2176]{2,1,0:T(8,128)(2,1)S(1)}, u32[]{:S(2)}, u32[]{:S(2)}) async-start(bf16[16,24,2176]{2,1,0:T(8,128)(2,1)} %bitcast.5), calls=%async_computation.1 | async-start | bytes 3342336 | tf_op jit(solution)/shard_map/all_to_all | solution.py:474
  211.5 41.5 %reduce-scatter.2.cloned.1.call-done.reduced_ref = bf16[128,1536]{1,0:T(8,128)(2,1)} async-done(((bf16[1024,1536]{1,0:T(8,128)(2,1)}), bf16[128,1536]{1,0:T(8,128)(2,1)}) %reduce-scatter.2.cloned.1.call-update) | async-done | bytes 393232 | tf_op jit(solution)/shard_map/reduce_scatter | solution.py:473
  253.0 0.0 copy-start
  253.0 1.0 slice.4
  254.0 2.4 collective-permute-start.10
  256.4 0.0 all-to-all-done.1
  256.4 0.0 copy-done.1
  256.4 0.0 copy-done.2
  256.5 2.9 %unpack.1 = (bf16[2,128,2048]{2,1,0:T(8,128)(2,1)}, bf16[2,128]{1,0:T(2,128)(2,1)}) custom-call(bf16[384,2176]{1,0:T(8,128)(2,1)S(1)} %bitcast.7, bf16[384,2176]{1,0:T(8,128)(2,1)S(1)} %bitcast.8, bf16[2,128]{1,0:T(2,128)(2,1)S(1)} %copy-done.2, s32[2,128]{1,0:T(2,128)S(1)} %bitcast.12), custom_call_target="tpu_custom_call" | custom-call | flops 402653184 | bytes 3145728 | tf_op jit(solution)/shard_map/unpack/pallas_call | solution.py:397
  259.3 2.2 collective-permute-done.10.partner_ref
  261.6 0.0 copy-done
  261.6 0.8 finish.1
Async XLA Ops:
  10.8 176.4 %all-to-all-start = ((bf16[16,24,4096]{2,1,0:T(8,128)(2,1)}), bf16[16,24,4096]{2,1,0:T(8,128)(2,1)S(1)}, u32[]{:S(2)}, u32[]{:S(2)}) async-start(bf16[16,24,4096]{2,1,0:T(8,128)(2,1)} %bitcast.13), calls=%async_computation | async-start | bytes 6291456 | tf_op jit(solution)/shard_map/all_to_all | solution.py:461
  22.8 230.2 %reduce-scatter.2.cloned.1.call-start = ((), (), s32[]{:S(2)}) async-start(), calls=%async_computation.3 | async-start | bytes 3538944 | tf_op jit(solution)/shard_map/reduce_scatter | solution.py:473
  24.5 8.7 %collective-permute-start = (bf16[128,768]{1,0:T(8,128)(2,1)}, bf16[128,768]{1,0:T(8,128)(2,1)S(1)}, u32[]{:S(2)}, u32[]{:S(2)}) collective-permute-start(bf16[128,768]{1,0:T(8,128)(2,1)} %join.1), channel_id=1, source_target_pairs={{0,1},{1,0},{2,3},{3,2},{4,5},{5,4},{6,7},{7,6},{8,9},{9,8},{10,11... | collective-permute-start | bytes 589832 | tf_op jit(solution)/shard_map/ppermute | solution.py:460
  34.1 48.7 %copy-start.3 = (bf16[128,1536]{1,0:T(8,128)(2,1)}, bf16[128,1536]{1,0:T(8,128)(2,1)S(1)}, u32[]{:S(2)}) copy-start(bf16[128,1536]{1,0:T(8,128)(2,1)S(1)} %pad_maximum_fusion.refs_0_) | copy-start | bytes 1179652
  34.1 13.6 %collective-permute-start.4 = (bf16[128,1536]{1,0:T(8,128)(2,1)S(1)}, bf16[128,1536]{1,0:T(8,128)(2,1)S(1)}, u32[]{:S(2)}, u32[]{:S(2)}) collective-permute-start(bf16[128,1536]{1,0:T(8,128)(2,1)S(1)} %pad_maximum_fusion.refs_0_), channel_id=1, source_target_pairs={{0,64},{64,128},{128,192},{192,256},{256,320},{320,384},{384,448},... | collective-permute-start | bytes 1179656 | tf_op jit(solution)/shard_map/ppermute | solution.py:177
  37.6 12.0 %collective-permute-start.1 = (bf16[128,1536]{1,0:T(8,128)(2,1)S(1)}, bf16[128,1536]{1,0:T(8,128)(2,1)S(1)}, u32[]{:S(2)}, u32[]{:S(2)}) collective-permute-start(bf16[128,1536]{1,0:T(8,128)(2,1)S(1)} %pad_maximum_fusion.refs_0_), channel_id=1, source_target_pairs={{0,448},{64,0},{128,64},{192,128},{256,192},{320,256},{384,320},{4... | collective-permute-start | bytes 1179656 | tf_op jit(solution)/shard_map/ppermute | solution.py:180
  47.7 1.9 copy-start.4
  47.7 12.4 %collective-permute-start.5 = (bf16[128,1536]{1,0:T(8,128)(2,1)S(1)}, bf16[128,1536]{1,0:T(8,128)(2,1)S(1)}, u32[]{:S(2)}, u32[]{:S(2)}) collective-permute-start(bf16[128,1536]{1,0:T(8,128)(2,1)S(1)} %collective-permute-done.4.refs_7_), channel_id=1, source_target_pairs={{0,64},{64,128},{128,192},{192,256},{256,320},{320,384},{384,448},... | collective-permute-start | bytes 1179656 | tf_op jit(solution)/shard_map/ppermute | solution.py:177
  49.6 10.4 %copy-start.5 = (bf16[128,1536]{1,0:T(8,128)(2,1)}, bf16[128,1536]{1,0:T(8,128)(2,1)S(1)}, u32[]{:S(2)}) copy-start(bf16[128,1536]{1,0:T(8,128)(2,1)S(1)} %collective-permute-done.1.refs_1_) | copy-start | bytes 1179652
  49.6 12.4 %collective-permute-start.2 = (bf16[128,1536]{1,0:T(8,128)(2,1)S(1)}, bf16[128,1536]{1,0:T(8,128)(2,1)}, u32[]{:S(2)}, u32[]{:S(2)}) collective-permute-start(bf16[128,1536]{1,0:T(8,128)(2,1)S(1)} %collective-permute-done.1.refs_1_), channel_id=1, source_target_pairs={{0,448},{64,0},{128,64},{192,128},{256,192},{320,256},{384,320},{4... | collective-permute-start | bytes 1179656 | tf_op jit(solution)/shard_map/ppermute | solution.py:180
  60.1 1.9 copy-start.6
  60.1 11.6 %collective-permute-start.6 = (bf16[128,1536]{1,0:T(8,128)(2,1)S(1)}, bf16[128,1536]{1,0:T(8,128)(2,1)}, u32[]{:S(2)}, u32[]{:S(2)}) collective-permute-start(bf16[128,1536]{1,0:T(8,128)(2,1)S(1)} %collective-permute-done.5.refs_6_), channel_id=1, source_target_pairs={{0,64},{64,128},{128,192},{192,256},{256,320},{320,384},{384,448},... | collective-permute-start | bytes 1179656 | tf_op jit(solution)/shard_map/ppermute | solution.py:177
  62.0 11.5 %collective-permute-start.3 = (bf16[128,1536]{1,0:T(8,128)(2,1)}, bf16[128,1536]{1,0:T(8,128)(2,1)}, u32[]{:S(2)}, u32[]{:S(2)}) collective-permute-start(bf16[128,1536]{1,0:T(8,128)(2,1)} %collective-permute-done.2.refs_2_), channel_id=1, source_target_pairs={{0,448},{64,0},{128,64},{192,128},{256,192},{320,256},{384,320},{4... | collective-permute-start | bytes 1179656 | tf_op jit(solution)/shard_map/ppermute | solution.py:180
  71.6 11.2 %collective-permute-start.7 = (bf16[128,1536]{1,0:T(8,128)(2,1)}, bf16[128,1536]{1,0:T(8,128)(2,1)}, u32[]{:S(2)}, u32[]{:S(2)}) collective-permute-start(bf16[128,1536]{1,0:T(8,128)(2,1)} %collective-permute-done.6.refs_5_), channel_id=1, source_target_pairs={{0,64},{64,128},{128,192},{192,256},{256,320},{320,384},{384,448},... | collective-permute-start | bytes 1179656 | tf_op jit(solution)/shard_map/ppermute | solution.py:177
  179.3 7.9 %collective-permute-start.8 = (bf16[8,128,1536]{2,1,0:T(8,128)(2,1)}, bf16[8,128,1536]{2,1,0:T(8,128)(2,1)}, u32[]{:S(2)}, u32[]{:S(2)}) collective-permute-start(bf16[8,128,1536]{2,1,0:T(8,128)(2,1)} %order.1.own_hbm), channel_id=1, source_target_pairs={{0,32},{32,0},{1,33},{33,1},{2,34},{34,2},{3,35},{35,3},{4,36},{36... | collective-permute-start | bytes 9437192 | tf_op jit(solution)/shard_map/ppermute | solution.py:465
  194.6 7.6 %collective-permute-start.9 = (bf16[1024,1536]{1,0:T(8,128)(2,1)S(1)}, bf16[1024,1536]{1,0:T(8,128)(2,1)S(1)}, u32[]{:S(2)}, u32[]{:S(2)}) collective-permute-start(bf16[1024,1536]{1,0:T(8,128)(2,1)S(1)} %get-tuple-element.29), channel_id=1, source_target_pairs={{0,32},{32,0},{1,33},{33,1},{2,34},{34,2},{3,35},{35,3},{4,36},{36... | collective-permute-start | bytes 9437192 | tf_op jit(solution)/shard_map/ppermute | solution.py:468
  204.0 52.4 %copy-start.1 = (s32[2,128,1]{1,2,0:T(1,128)S(1)}, s32[2,128,1]{1,2,0:T(1,128)}, u32[]{:S(2)}) copy-start(s32[2,128,1]{1,2,0:T(1,128)} %param.10) | copy-start | bytes 3076
  204.0 52.4 %copy-start.2 = (bf16[2,128]{1,0:T(2,128)(2,1)S(1)}, bf16[2,128]{1,0:T(2,128)(2,1)}, u32[]{:S(2)}) copy-start(bf16[2,128]{1,0:T(2,128)(2,1)} %gate_ref.1) | copy-start | bytes 1540
  204.1 52.4 %all-to-all-start.1 = ((bf16[16,24,2176]{2,1,0:T(8,128)(2,1)}), bf16[16,24,2176]{2,1,0:T(8,128)(2,1)S(1)}, u32[]{:S(2)}, u32[]{:S(2)}) async-start(bf16[16,24,2176]{2,1,0:T(8,128)(2,1)} %bitcast.5), calls=%async_computation.1 | async-start | bytes 3342336 | tf_op jit(solution)/shard_map/all_to_all | solution.py:474
  253.0 8.6 %copy-start = (bf16[128,1536]{1,0:T(8,128)(2,1)S(1)}, bf16[128,1536]{1,0:T(8,128)(2,1)}, u32[]{:S(2)}) copy-start(bf16[128,1536]{1,0:T(8,128)(2,1)} %reduce-scatter.2.cloned.1.call-done.reduced_ref) | copy-start | bytes 1179652
  254.0 7.6 %collective-permute-start.10 = (bf16[128,768]{1,0:T(8,128)(2,1)S(1)}, bf16[128,768]{1,0:T(8,128)(2,1)S(1)}, u32[]{:S(2)}, u32[]{:S(2)}) collective-permute-start(bf16[128,768]{1,0:T(8,128)(2,1)S(1)} %slice.4), channel_id=1, source_target_pairs={{0,1},{1,0},{2,3},{3,2},{4,5},{5,4},{6,7},{7,6},{8,9},{9,8},{10,11... | collective-permute-start | bytes 589832 | tf_op jit(solution)/shard_map/ppermute | solution.py:478
Sparse Core Ops, SparseCore 0:
  204.2 48.7 reduce-scatter.1

commit v6 on v5

--- a/solution.py
+++ b/solution.py
@@ -141,9 +141,9 @@
 
 def order_kernel(place_ref, *refs):
     count = len(refs) - 2
-    out_hbm, sems = refs[count], refs[count + 1]
+    out_ref, sems = refs[count], refs[count + 1]
     copies = [
-        pltpu.make_async_copy(refs[i], out_hbm.at[lax.rem(place_ref[0] + i, count)], sems.at[i])
+        pltpu.make_async_copy(refs[i], out_ref.at[lax.rem(place_ref[0] + i, count)], sems.at[i])
         for i in range(count)
     ]
     for copy in copies:
@@ -158,7 +158,7 @@
         order_kernel,
         out_shape=pltpu.HBM(shape, blocks[0].dtype),
         in_specs=[whole(pltpu.SMEM)] + [whole(pl.ANY)] * len(blocks),
-        out_specs=whole(pl.ANY),
+        out_specs=whole(),
         scratch_shapes=[pltpu.SemaphoreType.DMA((len(blocks),))],
         compiler_params=pltpu.CompilerParams(vmem_limit_bytes=JOIN_LIMIT),
         cost_estimate=cost(0, 6 * MIB),

time: 270 us -> 177 us (0.66)
  Pallas kernels: 119 us -> 26.6 us
  waiting for transfers between devices: 80.9 us -> 84.6 us
  starting transfers between devices: 52.5 us -> 49.1 us
    pallas_call x1, Pallas kernels: 96.5 us -> 3.56 us  [order(): pl.pallas_call(order_kernel, out_shape=pltpu.HBM(shape, blocks[0].dtype),...]
    all_to_all x1, waiting for transfers between devices: 0.01 us -> 3.39 us  [local(): lax.all_to_all(sent.reshape(experts, layers * capacity, 2 * width), 'e',...]
    all_to_all x1, starting transfers between devices: 7.44 us -> 4.06 us  [local(): lax.all_to_all(back.reshape(experts, layers * capacity, back.shape[1]), '...]
  transfers between devices with their start and end apart: 14 -> 14, of which waited for: 9 -> 10; matrix products, arithmetic and copies ran while one was open for 1% -> 1% of each run, Pallas kernels for 39% -> 7%
where the time goes in v6:
time: 177 us
  waiting for transfers between devices  84.6 us (48%)
  starting transfers between devices  49.1 us (28%)
  Pallas kernels  26.6 us (15%)
  between operations  14.3 us (8%)
    reduce_scatter x1, waiting for transfers between devices, local(): reduced = lax.psum_scatter(total, 'y', scatter_dimension=0, tiled=True)  41.7 us
    ppermute x4, waiting for transfers between devices, ring_gather(): fromdown = lax.ppermute(fromdown, 'y', up)  25.3 us
    ppermute x3, starting transfers between devices, ring_gather(): fromup = lax.ppermute(fromup, 'y', down)  14.1 us
    all_to_all x1, starting transfers between devices, local(): lax.all_to_all(sent.reshape(experts, layers * capacity, 2 * width), 'e',...  12 us
    ppermute x4, starting transfers between devices, ring_gather(): fromdown = lax.ppermute(fromdown, 'y', up)  9.22 us
    pallas_call x1, Pallas kernels, forward(): pl.pallas_call(forward_kernel, out_shape=(jax.ShapeDtypeStruct((rows, col...  7.44 us
    ppermute x1, waiting for transfers between devices, local(): other = lax.ppermute(own, 'c', swap)  5.96 us
    ppermute x1, waiting for transfers between devices, local(): paired = lax.ppermute(mine, 'k', swap)  5.38 us
  transfers between devices with their start and end apart: 14, of which 10 were waited for; matrix products, arithmetic and copies ran while one was open for 1% of the time, Pallas kernels for 7%

profile of v6, /device:TPU:2, one launch (start us, length us, event | category | flops | bytes accessed | tf_op | source)
XLA Modules:
  0.0 176.5 jit_solution(4043439860509510331)
XLA Ops:
  7.2 3.6 %pack.1 = bf16[384,4096]{1,0:T(8,128)(2,1)} custom-call(bf16[2,128,2048]{2,1,0:T(8,128)(2,1)} %x_hbm.1, bf16[2,128,2048]{2,1,0:T(8,128)(2,1)} %dy_hbm.1, bf16[2,128]{1,0:T(2,128)(2,1)} %gate_ref.1, s32[2,128]{1,0:T(2,128)} %bitcast.11), custom_call_target="tpu_custom_call" | custom-call | flops 805306368 | bytes 5242880 | tf_op jit(solution)/shard_map/pack/pallas_call | solution.py:92
  10.8 12.0 %all-to-all-start = ((bf16[16,24,4096]{2,1,0:T(8,128)(2,1)}), bf16[16,24,4096]{2,1,0:T(8,128)(2,1)S(1)}, u32[]{:S(2)}, u32[]{:S(2)}) async-start(bf16[16,24,4096]{2,1,0:T(8,128)(2,1)} %bitcast.13), calls=%async_computation | async-start | bytes 6291456 | tf_op jit(solution)/shard_map/all_to_all | solution.py:461
  22.8 0.0 reduce-scatter.2.cloned.1.call-start
  22.8 1.6 join.1
  24.5 3.3 %collective-permute-start = (bf16[128,768]{1,0:T(8,128)(2,1)}, bf16[128,768]{1,0:T(8,128)(2,1)S(1)}, u32[]{:S(2)}, u32[]{:S(2)}) collective-permute-start(bf16[128,768]{1,0:T(8,128)(2,1)} %join.1), channel_id=1, source_target_pairs={{0,1},{1,0},{2,3},{3,2},{4,5},{5,4},{6,7},{7,6},{8,9},{9,8},{10,11... | collective-permute-start | bytes 589832 | tf_op jit(solution)/shard_map/ppermute | solution.py:460
  27.8 5.4 %collective-permute-done = bf16[128,768]{1,0:T(8,128)(2,1)S(1)} collective-permute-done((bf16[128,768]{1,0:T(8,128)(2,1)}, bf16[128,768]{1,0:T(8,128)(2,1)S(1)}, u32[]{:S(2)}, u32[]{:S(2)}) %collective-permute-start) | collective-permute-done | bytes 196640 | tf_op jit(solution)/shard_map/ppermute | solution.py:460
  33.2 1.0 pad_maximum_fusion.refs_0_
  34.1 0.0 copy-start.3
  34.1 3.5 %collective-permute-start.4 = (bf16[128,1536]{1,0:T(8,128)(2,1)S(1)}, bf16[128,1536]{1,0:T(8,128)(2,1)S(1)}, u32[]{:S(2)}, u32[]{:S(2)}) collective-permute-start(bf16[128,1536]{1,0:T(8,128)(2,1)S(1)} %pad_maximum_fusion.refs_0_), channel_id=1, source_target_pairs={{0,64},{64,128},{128,192},{192,256},{256,320},{320,384},{384,448},... | collective-permute-start | bytes 1179656 | tf_op jit(solution)/shard_map/ppermute | solution.py:177
  37.6 3.8 %collective-permute-start.1 = (bf16[128,1536]{1,0:T(8,128)(2,1)S(1)}, bf16[128,1536]{1,0:T(8,128)(2,1)S(1)}, u32[]{:S(2)}, u32[]{:S(2)}) collective-permute-start(bf16[128,1536]{1,0:T(8,128)(2,1)S(1)} %pad_maximum_fusion.refs_0_), channel_id=1, source_target_pairs={{0,448},{64,0},{128,64},{192,128},{256,192},{320,256},{384,320},{4... | collective-permute-start | bytes 1179656 | tf_op jit(solution)/shard_map/ppermute | solution.py:180
  41.5 6.2 %collective-permute-done.4.refs_7_ = bf16[128,1536]{1,0:T(8,128)(2,1)S(1)} collective-permute-done((bf16[128,1536]{1,0:T(8,128)(2,1)S(1)}, bf16[128,1536]{1,0:T(8,128)(2,1)S(1)}, u32[]{:S(2)}, u32[]{:S(2)}) %collective-permute-start.4) | collective-permute-done | bytes 393248 | tf_op jit(solution)/shard_map/ppermute | solution.py:177
  47.7 0.0 copy-start.4
  47.7 1.9 %collective-permute-start.5 = (bf16[128,1536]{1,0:T(8,128)(2,1)S(1)}, bf16[128,1536]{1,0:T(8,128)(2,1)S(1)}, u32[]{:S(2)}, u32[]{:S(2)}) collective-permute-start(bf16[128,1536]{1,0:T(8,128)(2,1)S(1)} %collective-permute-done.4.refs_7_), channel_id=1, source_target_pairs={{0,64},{64,128},{128,192},{192,256},{256,320},{320,384},{384,448},... | collective-permute-start | bytes 1179656 | tf_op jit(solution)/shard_map/ppermute | solution.py:177
  49.6 0.0 collective-permute-done.1.refs_1_
  49.6 0.0 copy-done.4
  49.6 0.0 copy-start.5
  49.6 5.1 %collective-permute-start.2 = (bf16[128,1536]{1,0:T(8,128)(2,1)S(1)}, bf16[128,1536]{1,0:T(8,128)(2,1)}, u32[]{:S(2)}, u32[]{:S(2)}) collective-permute-start(bf16[128,1536]{1,0:T(8,128)(2,1)S(1)} %collective-permute-done.1.refs_1_), channel_id=1, source_target_pairs={{0,448},{64,0},{128,64},{192,128},{256,192},{320,256},{384,320},{4... | collective-permute-start | bytes 1179656 | tf_op jit(solution)/shard_map/ppermute | solution.py:180
  54.8 5.3 %collective-permute-done.5.refs_6_ = bf16[128,1536]{1,0:T(8,128)(2,1)S(1)} collective-permute-done((bf16[128,1536]{1,0:T(8,128)(2,1)S(1)}, bf16[128,1536]{1,0:T(8,128)(2,1)S(1)}, u32[]{:S(2)}, u32[]{:S(2)}) %collective-permute-start.5) | collective-permute-done | bytes 393248 | tf_op jit(solution)/shard_map/ppermute | solution.py:177
  60.1 0.0 copy-done.5
  60.1 0.0 copy-start.6
  60.1 1.9 %collective-permute-start.6 = (bf16[128,1536]{1,0:T(8,128)(2,1)S(1)}, bf16[128,1536]{1,0:T(8,128)(2,1)}, u32[]{:S(2)}, u32[]{:S(2)}) collective-permute-start(bf16[128,1536]{1,0:T(8,128)(2,1)S(1)} %collective-permute-done.5.refs_6_), channel_id=1, source_target_pairs={{0,64},{64,128},{128,192},{192,256},{256,320},{320,384},{384,448},... | collective-permute-start | bytes 1179656 | tf_op jit(solution)/shard_map/ppermute | solution.py:177
  62.0 0.0 collective-permute-done.2.refs_2_
  62.0 0.0 copy-done.6
  62.0 5.1 %collective-permute-start.3 = (bf16[128,1536]{1,0:T(8,128)(2,1)}, bf16[128,1536]{1,0:T(8,128)(2,1)}, u32[]{:S(2)}, u32[]{:S(2)}) collective-permute-start(bf16[128,1536]{1,0:T(8,128)(2,1)} %collective-permute-done.2.refs_2_), channel_id=1, source_target_pairs={{0,448},{64,0},{128,64},{192,128},{256,192},{320,256},{384,320},{4... | collective-permute-start | bytes 1179656 | tf_op jit(solution)/shard_map/ppermute | solution.py:180
  67.2 4.5 %collective-permute-done.6.refs_5_ = bf16[128,1536]{1,0:T(8,128)(2,1)} collective-permute-done((bf16[128,1536]{1,0:T(8,128)(2,1)S(1)}, bf16[128,1536]{1,0:T(8,128)(2,1)}, u32[]{:S(2)}, u32[]{:S(2)}) %collective-permute-start.6) | collective-permute-done | bytes 393248 | tf_op jit(solution)/shard_map/ppermute | solution.py:177
  71.6 1.9 %collective-permute-start.7 = (bf16[128,1536]{1,0:T(8,128)(2,1)}, bf16[128,1536]{1,0:T(8,128)(2,1)}, u32[]{:S(2)}, u32[]{:S(2)}) collective-permute-start(bf16[128,1536]{1,0:T(8,128)(2,1)} %collective-permute-done.6.refs_5_), channel_id=1, source_target_pairs={{0,64},{64,128},{128,192},{192,256},{256,320},{320,384},{384,448},... | collective-permute-start | bytes 1179656 | tf_op jit(solution)/shard_map/ppermute | solution.py:177
  73.6 0.0 collective-permute-done.3.refs_3_
  73.6 9.3 %collective-permute-done.7.refs_4_ = bf16[128,1536]{1,0:T(8,128)(2,1)} collective-permute-done((bf16[128,1536]{1,0:T(8,128)(2,1)}, bf16[128,1536]{1,0:T(8,128)(2,1)}, u32[]{:S(2)}, u32[]{:S(2)}) %collective-permute-start.7) | collective-permute-done | bytes 393248 | tf_op jit(solution)/shard_map/ppermute | solution.py:177
  82.8 0.0 copy-done.3
  82.8 3.6 %order.1.own_hbm = bf16[8,128,1536]{2,1,0:T(8,128)(2,1)} custom-call(s32[1]{0:T(128)} %bitcast.4.place_ref, bf16[128,1536]{1,0:T(8,128)(2,1)} %copy-done.3, bf16[128,1536]{1,0:T(8,128)(2,1)} %copy-done.5, bf16[128,1536]{1,0:T(8,128)(2,1)} %collective-permute-done.2.refs_2_, bf16[128,1536]{1,0:T(8,128)(2,1)} %collective-permute-done.3.refs_3_, ...), custom_call_target="tpu_custom_call" | custom-call | bytes 6291456 | tf_op jit(solution)/shard_map/order/pallas_call | solution.py:157
  86.4 1.9 %collective-permute-start.8 = (bf16[8,128,1536]{2,1,0:T(8,128)(2,1)}, bf16[8,128,1536]{2,1,0:T(8,128)(2,1)}, u32[]{:S(2)}, u32[]{:S(2)}) collective-permute-start(bf16[8,128,1536]{2,1,0:T(8,128)(2,1)} %order.1.own_hbm), channel_id=1, source_target_pairs={{0,32},{32,0},{1,33},{33,1},{2,34},{34,2},{3,35},{35,3},{4,36},{36... | collective-permute-start | bytes 9437192 | tf_op jit(solution)/shard_map/ppermute | solution.py:465
  88.3 6.0 %collective-permute-done.8.other_hbm = bf16[8,128,1536]{2,1,0:T(8,128)(2,1)} collective-permute-done((bf16[8,128,1536]{2,1,0:T(8,128)(2,1)}, bf16[8,128,1536]{2,1,0:T(8,128)(2,1)}, u32[]{:S(2)}, u32[]{:S(2)}) %collective-permute-start.8) | collective-permute-done | bytes 3145760 | tf_op jit(solution)/shard_map/ppermute | solution.py:465
  94.3 3.4 %all-to-all-done = bf16[16,24,4096]{2,1,0:T(8,128)(2,1)S(1)} async-done(((bf16[16,24,4096]{2,1,0:T(8,128)(2,1)}), bf16[16,24,4096]{2,1,0:T(8,128)(2,1)S(1)}, u32[]{:S(2)}, u32[]{:S(2)}) %all-to-all-start) | async-done | bytes 3145760 | tf_op jit(solution)/shard_map/all_to_all | solution.py:461
  97.7 7.4 %forward.1 = (bf16[384,1024]{1,0:T(8,128)(2,1)S(1)}, bf16[384,512]{1,0:T(8,128)(2,1)S(1)}, bf16[384,128]{1,0:T(8,128)(2,1)S(1)}, bf16[1024,1536]{1,0:T(8,128)(2,1)S(1)}, bf16[8,2,128,1536]{3,2,1,0:T(8,128)(2,1)S(1)}) custom-call(s32[1]{0:T(128)} %bitcast.core_ref, bf16[384,4096]{1,0:T(8,128)(2,1)S(1)} %bitcast.9, bf16[8,128,1536]{2,1,0:T(8,128)(2,1)} %order.1.own_hbm, ...), custom_call_target="tpu_custom_call" | custom-call | flops 3623878656 | bytes 14680064 | tf_op jit(solution)/shard_map/forward/pallas_call | solution.py:272
  105.1 1.9 %collective-permute-start.9 = (bf16[1024,1536]{1,0:T(8,128)(2,1)S(1)}, bf16[1024,1536]{1,0:T(8,128)(2,1)S(1)}, u32[]{:S(2)}, u32[]{:S(2)}) collective-permute-start(bf16[1024,1536]{1,0:T(8,128)(2,1)S(1)} %get-tuple-element.29), channel_id=1, source_target_pairs={{0,32},{32,0},{1,33},{33,1},{2,34},{34,2},{3,35},{35,3},{4,36},{36... | collective-permute-start | bytes 9437192 | tf_op jit(solution)/shard_map/ppermute | solution.py:468
  107.1 3.0 %input_terms.1 = bf16[384,2176]{1,0:T(8,128)(2,1)} custom-call(bf16[384,1024]{1,0:T(8,128)(2,1)S(1)} %get-tuple-element.22.grads_ref, bf16[8,2,128,1536]{3,2,1,0:T(8,128)(2,1)S(1)} %get-tuple-element.23.held_ref, bf16[384,128]{1,0:T(8,128)(2,1)S(1)} %get-tuple-element.24.gate_ref), custom_call_target="tpu_custom_call" | custom-call | flops 1610612736 | bytes 9437184 | tf_op jit(solution)/shard_map/input_terms/pallas_call | solution.py:315
  110.1 1.8 %own_terms.1.own_ref = f32[1024,1536]{1,0:T(8,128)S(1)} custom-call(s32[1]{0:T(128)} %bitcast.core_ref, bf16[384,4096]{1,0:T(8,128)(2,1)S(1)} %bitcast.10, bf16[384,1024]{1,0:T(8,128)(2,1)S(1)} %get-tuple-element.22.grads_ref, bf16[384,512]{1,0:T(8,128)(2,1)S(1)} %get-tuple-element.28.hidden_ref), custom_call_target="tpu_custom_call" | custom-call | flops 1207959552 | bytes 10485760 | tf_op jit(solution)/shard_map/own_terms/pallas_call | solution.py:332
  111.9 0.7 collective-permute-done.9.arrived_ref
  112.7 1.8 %add.4 = bf16[1024,1536]{1,0:T(8,128)(2,1)} custom-call(f32[1024,1536]{1,0:T(8,128)S(1)} %own_terms.1.own_ref, bf16[1024,1536]{1,0:T(8,128)(2,1)S(1)} %collective-permute-done.9.arrived_ref), custom_call_target="tpu_custom_call" | custom-call | flops 1572864 | bytes 12582912 | tf_op jit(solution)/shard_map/add/pallas_call | solution.py:358
  114.5 0.0 copy-start.1
  114.5 0.0 copy-start.2
  114.5 0.0 reduce-scatter.2.cloned.1.call-update
  114.5 4.1 %all-to-all-start.1 = ((bf16[16,24,2176]{2,1,0:T(8,128)(2,1)}), bf16[16,24,2176]{2,1,0:T(8,128)(2,1)S(1)}, u32[]{:S(2)}, u32[]{:S(2)}) async-start(bf16[16,24,2176]{2,1,0:T(8,128)(2,1)} %bitcast.5), calls=%async_computation.1 | async-start | bytes 3342336 | tf_op jit(solution)/shard_map/all_to_all | solution.py:474
  118.6 41.7 %reduce-scatter.2.cloned.1.call-done.reduced_ref = bf16[128,1536]{1,0:T(8,128)(2,1)} async-done(((bf16[1024,1536]{1,0:T(8,128)(2,1)}), bf16[128,1536]{1,0:T(8,128)(2,1)}) %reduce-scatter.2.cloned.1.call-update) | async-done | bytes 393232 | tf_op jit(solution)/shard_map/reduce_scatter | solution.py:473
  160.3 0.0 copy-start
  160.3 1.0 slice.4
  161.3 2.5 %collective-permute-start.10 = (bf16[128,768]{1,0:T(8,128)(2,1)S(1)}, bf16[128,768]{1,0:T(8,128)(2,1)S(1)}, u32[]{:S(2)}, u32[]{:S(2)}) collective-permute-start(bf16[128,768]{1,0:T(8,128)(2,1)S(1)} %slice.4), channel_id=1, source_target_pairs={{0,1},{1,0},{2,3},{3,2},{4,5},{5,4},{6,7},{7,6},{8,9},{9,8},{10,11... | collective-permute-start | bytes 589832 | tf_op jit(solution)/shard_map/ppermute | solution.py:478
  163.9 0.0 all-to-all-done.1
  163.9 0.0 copy-done.1
  163.9 0.0 copy-done.2
  163.9 2.9 %unpack.1 = (bf16[2,128,2048]{2,1,0:T(8,128)(2,1)}, bf16[2,128]{1,0:T(2,128)(2,1)}) custom-call(bf16[384,2176]{1,0:T(8,128)(2,1)S(1)} %bitcast.7, bf16[384,2176]{1,0:T(8,128)(2,1)S(1)} %bitcast.8, bf16[2,128]{1,0:T(2,128)(2,1)S(1)} %copy-done.2, s32[2,128]{1,0:T(2,128)S(1)} %bitcast.12), custom_call_target="tpu_custom_call" | custom-call | flops 402653184 | bytes 3145728 | tf_op jit(solution)/shard_map/unpack/pallas_call | solution.py:397
  166.8 2.1 %collective-permute-done.10.partner_ref = bf16[128,768]{1,0:T(8,128)(2,1)S(1)} collective-permute-done((bf16[128,768]{1,0:T(8,128)(2,1)S(1)}, bf16[128,768]{1,0:T(8,128)(2,1)S(1)}, u32[]{:S(2)}, u32[]{:S(2)}) %collective-permute-start.10) | collective-permute-done | bytes 196640 | tf_op jit(solution)/shard_map/ppermute | solution.py:478
  168.9 0.0 copy-done
  168.9 0.8 finish.1
Async XLA Ops:
  10.8 86.9 %all-to-all-start = ((bf16[16,24,4096]{2,1,0:T(8,128)(2,1)}), bf16[16,24,4096]{2,1,0:T(8,128)(2,1)S(1)}, u32[]{:S(2)}, u32[]{:S(2)}) async-start(bf16[16,24,4096]{2,1,0:T(8,128)(2,1)} %bitcast.13), calls=%async_computation | async-start | bytes 6291456 | tf_op jit(solution)/shard_map/all_to_all | solution.py:461
  22.8 137.5 %reduce-scatter.2.cloned.1.call-start = ((), (), s32[]{:S(2)}) async-start(), calls=%async_computation.3 | async-start | bytes 3538944 | tf_op jit(solution)/shard_map/reduce_scatter | solution.py:473
  24.5 8.7 %collective-permute-start = (bf16[128,768]{1,0:T(8,128)(2,1)}, bf16[128,768]{1,0:T(8,128)(2,1)S(1)}, u32[]{:S(2)}, u32[]{:S(2)}) collective-permute-start(bf16[128,768]{1,0:T(8,128)(2,1)} %join.1), channel_id=1, source_target_pairs={{0,1},{1,0},{2,3},{3,2},{4,5},{5,4},{6,7},{7,6},{8,9},{9,8},{10,11... | collective-permute-start | bytes 589832 | tf_op jit(solution)/shard_map/ppermute | solution.py:460
  34.1 48.7 %copy-start.3 = (bf16[128,1536]{1,0:T(8,128)(2,1)}, bf16[128,1536]{1,0:T(8,128)(2,1)S(1)}, u32[]{:S(2)}) copy-start(bf16[128,1536]{1,0:T(8,128)(2,1)S(1)} %pad_maximum_fusion.refs_0_) | copy-start | bytes 1179652
  34.1 13.6 %collective-permute-start.4 = (bf16[128,1536]{1,0:T(8,128)(2,1)S(1)}, bf16[128,1536]{1,0:T(8,128)(2,1)S(1)}, u32[]{:S(2)}, u32[]{:S(2)}) collective-permute-start(bf16[128,1536]{1,0:T(8,128)(2,1)S(1)} %pad_maximum_fusion.refs_0_), channel_id=1, source_target_pairs={{0,64},{64,128},{128,192},{192,256},{256,320},{320,384},{384,448},... | collective-permute-start | bytes 1179656 | tf_op jit(solution)/shard_map/ppermute | solution.py:177
  37.6 12.0 %collective-permute-start.1 = (bf16[128,1536]{1,0:T(8,128)(2,1)S(1)}, bf16[128,1536]{1,0:T(8,128)(2,1)S(1)}, u32[]{:S(2)}, u32[]{:S(2)}) collective-permute-start(bf16[128,1536]{1,0:T(8,128)(2,1)S(1)} %pad_maximum_fusion.refs_0_), channel_id=1, source_target_pairs={{0,448},{64,0},{128,64},{192,128},{256,192},{320,256},{384,320},{4... | collective-permute-start | bytes 1179656 | tf_op jit(solution)/shard_map/ppermute | solution.py:180
  47.7 1.9 %copy-start.4 = (bf16[128,1536]{1,0:T(8,128)(2,1)}, bf16[128,1536]{1,0:T(8,128)(2,1)S(1)}, u32[]{:S(2)}) copy-start(bf16[128,1536]{1,0:T(8,128)(2,1)S(1)} %collective-permute-done.4.refs_7_) | copy-start | bytes 1179652
  47.7 12.4 %collective-permute-start.5 = (bf16[128,1536]{1,0:T(8,128)(2,1)S(1)}, bf16[128,1536]{1,0:T(8,128)(2,1)S(1)}, u32[]{:S(2)}, u32[]{:S(2)}) collective-permute-start(bf16[128,1536]{1,0:T(8,128)(2,1)S(1)} %collective-permute-done.4.refs_7_), channel_id=1, source_target_pairs={{0,64},{64,128},{128,192},{192,256},{256,320},{320,384},{384,448},... | collective-permute-start | bytes 1179656 | tf_op jit(solution)/shard_map/ppermute | solution.py:177
  49.6 10.4 %copy-start.5 = (bf16[128,1536]{1,0:T(8,128)(2,1)}, bf16[128,1536]{1,0:T(8,128)(2,1)S(1)}, u32[]{:S(2)}) copy-start(bf16[128,1536]{1,0:T(8,128)(2,1)S(1)} %collective-permute-done.1.refs_1_) | copy-start | bytes 1179652
  49.6 12.4 %collective-permute-start.2 = (bf16[128,1536]{1,0:T(8,128)(2,1)S(1)}, bf16[128,1536]{1,0:T(8,128)(2,1)}, u32[]{:S(2)}, u32[]{:S(2)}) collective-permute-start(bf16[128,1536]{1,0:T(8,128)(2,1)S(1)} %collective-permute-done.1.refs_1_), channel_id=1, source_target_pairs={{0,448},{64,0},{128,64},{192,128},{256,192},{320,256},{384,320},{4... | collective-permute-start | bytes 1179656 | tf_op jit(solution)/shard_map/ppermute | solution.py:180
  60.1 1.9 %copy-start.6 = (bf16[128,1536]{1,0:T(8,128)(2,1)}, bf16[128,1536]{1,0:T(8,128)(2,1)S(1)}, u32[]{:S(2)}) copy-start(bf16[128,1536]{1,0:T(8,128)(2,1)S(1)} %collective-permute-done.5.refs_6_) | copy-start | bytes 1179652
  60.1 11.6 %collective-permute-start.6 = (bf16[128,1536]{1,0:T(8,128)(2,1)S(1)}, bf16[128,1536]{1,0:T(8,128)(2,1)}, u32[]{:S(2)}, u32[]{:S(2)}) collective-permute-start(bf16[128,1536]{1,0:T(8,128)(2,1)S(1)} %collective-permute-done.5.refs_6_), channel_id=1, source_target_pairs={{0,64},{64,128},{128,192},{192,256},{256,320},{320,384},{384,448},... | collective-permute-start | bytes 1179656 | tf_op jit(solution)/shard_map/ppermute | solution.py:177
  62.0 11.5 %collective-permute-start.3 = (bf16[128,1536]{1,0:T(8,128)(2,1)}, bf16[128,1536]{1,0:T(8,128)(2,1)}, u32[]{:S(2)}, u32[]{:S(2)}) collective-permute-start(bf16[128,1536]{1,0:T(8,128)(2,1)} %collective-permute-done.2.refs_2_), channel_id=1, source_target_pairs={{0,448},{64,0},{128,64},{192,128},{256,192},{320,256},{384,320},{4... | collective-permute-start | bytes 1179656 | tf_op jit(solution)/shard_map/ppermute | solution.py:180
  71.6 11.2 %collective-permute-start.7 = (bf16[128,1536]{1,0:T(8,128)(2,1)}, bf16[128,1536]{1,0:T(8,128)(2,1)}, u32[]{:S(2)}, u32[]{:S(2)}) collective-permute-start(bf16[128,1536]{1,0:T(8,128)(2,1)} %collective-permute-done.6.refs_5_), channel_id=1, source_target_pairs={{0,64},{64,128},{128,192},{192,256},{256,320},{320,384},{384,448},... | collective-permute-start | bytes 1179656 | tf_op jit(solution)/shard_map/ppermute | solution.py:177
  86.4 7.9 %collective-permute-start.8 = (bf16[8,128,1536]{2,1,0:T(8,128)(2,1)}, bf16[8,128,1536]{2,1,0:T(8,128)(2,1)}, u32[]{:S(2)}, u32[]{:S(2)}) collective-permute-start(bf16[8,128,1536]{2,1,0:T(8,128)(2,1)} %order.1.own_hbm), channel_id=1, source_target_pairs={{0,32},{32,0},{1,33},{33,1},{2,34},{34,2},{3,35},{35,3},{4,36},{36... | collective-permute-start | bytes 9437192 | tf_op jit(solution)/shard_map/ppermute | solution.py:465
  105.1 7.6 %collective-permute-start.9 = (bf16[1024,1536]{1,0:T(8,128)(2,1)S(1)}, bf16[1024,1536]{1,0:T(8,128)(2,1)S(1)}, u32[]{:S(2)}, u32[]{:S(2)}) collective-permute-start(bf16[1024,1536]{1,0:T(8,128)(2,1)S(1)} %get-tuple-element.29), channel_id=1, source_target_pairs={{0,32},{32,0},{1,33},{33,1},{2,34},{34,2},{3,35},{35,3},{4,36},{36... | collective-permute-start | bytes 9437192 | tf_op jit(solution)/shard_map/ppermute | solution.py:468
  114.5 49.4 %copy-start.1 = (s32[2,128,1]{1,2,0:T(1,128)S(1)}, s32[2,128,1]{1,2,0:T(1,128)}, u32[]{:S(2)}) copy-start(s32[2,128,1]{1,2,0:T(1,128)} %param.10) | copy-start | bytes 3076
  114.5 49.4 %copy-start.2 = (bf16[2,128]{1,0:T(2,128)(2,1)S(1)}, bf16[2,128]{1,0:T(2,128)(2,1)}, u32[]{:S(2)}) copy-start(bf16[2,128]{1,0:T(2,128)(2,1)} %gate_ref.1) | copy-start | bytes 1540
  114.5 49.3 %all-to-all-start.1 = ((bf16[16,24,2176]{2,1,0:T(8,128)(2,1)}), bf16[16,24,2176]{2,1,0:T(8,128)(2,1)S(1)}, u32[]{:S(2)}, u32[]{:S(2)}) async-start(bf16[16,24,2176]{2,1,0:T(8,128)(2,1)} %bitcast.5), calls=%async_computation.1 | async-start | bytes 3342336 | tf_op jit(solution)/shard_map/all_to_all | solution.py:474
  160.3 8.6 %copy-start = (bf16[128,1536]{1,0:T(8,128)(2,1)S(1)}, bf16[128,1536]{1,0:T(8,128)(2,1)}, u32[]{:S(2)}) copy-start(bf16[128,1536]{1,0:T(8,128)(2,1)} %reduce-scatter.2.cloned.1.call-done.reduced_ref) | copy-start | bytes 1179652
  161.3 7.6 %collective-permute-start.10 = (bf16[128,768]{1,0:T(8,128)(2,1)S(1)}, bf16[128,768]{1,0:T(8,128)(2,1)S(1)}, u32[]{:S(2)}, u32[]{:S(2)}) collective-permute-start(bf16[128,768]{1,0:T(8,128)(2,1)S(1)} %slice.4), channel_id=1, source_target_pairs={{0,1},{1,0},{2,3},{3,2},{4,5},{5,4},{6,7},{7,6},{8,9},{9,8},{10,11... | collective-permute-start | bytes 589832 | tf_op jit(solution)/shard_map/ppermute | solution.py:478
Sparse Core Ops, SparseCore 0:
  114.7 45.6 reduce-scatter.1

commit v7 on v6

--- a/solution.py
+++ b/solution.py
@@ -188,48 +188,46 @@
     count, piece, columns = own_hbm.shape
     width = 2 * count * piece
     unit = columns // 6
-    pieces = []
+    def side_copies(part):
+        at = pl.ds(pl.multiple_of(3 * part * unit, unit), 3 * unit)
+        return [
+            pltpu.make_async_copy(
+                src.at[:, :, at],
+                held_ref.at[:, lax.rem(core_ref[0] + side, 2), :, at],
+                sems.at[2 * part + side],
+            )
+            for side, src in enumerate((own_hbm, other_hbm))
+        ]
+
     for part in range(2):
-        base = part * 3 * unit
-        pieces += [slice(base, base + 2 * unit), slice(base + 2 * unit, base + 3 * unit)]
-    copies = []
-    for part in range(2):
-        at = slice(3 * part * unit, 3 * (part + 1) * unit)
-        for side, src in enumerate((own_hbm, other_hbm)):
-            copies.append(
-                pltpu.make_async_copy(
-                    src.at[:, :, at],
-                    held_ref.at[:, lax.rem(core_ref[0] + side, 2), :, at],
-                    sems.at[2 * part + side],
-                )
-            )
-    for copy in copies:
-        copy.start()
-    gate_sum = 0.0
-    for part in range(2):
-        copies[2 * part].wait()
-        copies[2 * part + 1].wait()
-        pre = jnp.dot(
-            recv_ref[:, :width],
-            held_ref[:, :, :, pieces[2 * part]].reshape(width, 2 * unit),
-            preferred_element_type=jnp.float32,
-        )
-        back = jnp.dot(
-            recv_ref[:, width:],
-            held_ref[:, :, :, pieces[2 * part + 1]].reshape(width, unit),
-            preferred_element_type=jnp.float32,
-        )
+        for copy in side_copies(part):
+            copy.start()
+
+    def half(part, gate_sum):
+        for copy in side_copies(part):
+            copy.wait()
+
+        def weights(first, units):
+            at = pl.ds(pl.multiple_of((3 * part + first) * unit, unit), units * unit)
+            return held_ref[:, :, :, at].reshape(width, units * unit)
+
+        def column(ref, first):
+            return ref.at[:, pl.ds(pl.multiple_of(first * unit, unit), unit)]
+
+        pre = jnp.dot(recv_ref[:, :width], weights(0, 2), preferred_element_type=jnp.float32)
+        back = jnp.dot(recv_ref[:, width:], weights(2, 1), preferred_element_type=jnp.float32)
         gate_pre, up_value = pre[:, :unit], pre[:, unit:]
         sigmoid = jax.nn.sigmoid(gate_pre)
         swish = gate_pre * sigmoid
         hidden = swish * up_value
-        gate_sum = gate_sum + jnp.sum(hidden * back, axis=1, keepdims=True)
         grad_pre = back * up_value * sigmoid * (1.0 + gate_pre * (1.0 - sigmoid))
-        grads_ref[:, 2 * part * unit : (2 * part + 1) * unit] = grad_pre.astype(jnp.bfloat16)
-        grads_ref[:, (2 * part + 1) * unit : (2 * part + 2) * unit] = (back * swish).astype(
-            jnp.bfloat16
-        )
-        hidden_ref[:, part * unit : (part + 1) * unit] = hidden.astype(jnp.bfloat16)
+        column(grads_ref, 2 * part)[...] = grad_pre.astype(jnp.bfloat16)
+        column(grads_ref, 2 * part + 1)[...] = (back * swish).astype(jnp.bfloat16)
+        column(hidden_ref, part)[...] = hidden.astype(jnp.bfloat16)
+        return gate_sum + jnp.sum(hidden * back, axis=1, keepdims=True)
+
+    rows = recv_ref.shape[0]
+    gate_sum = lax.fori_loop(0, 2, half, jnp.zeros((rows, 1), jnp.float32))
     gate_ref[...] = jnp.broadcast_to(gate_sum, gate_ref.shape).astype(jnp.bfloat16)
     weight_terms(recv_ref, grads_ref, hidden_ref, 1 - core_ref[0], term_ref)
 

time: 177 us -> 177 us (level)
  no operation moved by 1% of the time
where the time goes in v7:
time: 177 us; the launch traced here: 176 us
  waiting for transfers between devices  84.4 us (48%)
  starting transfers between devices  49.2 us (28%)
  Pallas kernels  26 us (15%)
  between operations  14.3 us (8%)
    reduce_scatter x1, waiting for transfers between devices, local(): reduced = lax.psum_scatter(total, 'y', scatter_dimension=0, tiled=True)  41.6 us
    ppermute x4, waiting for transfers between devices, ring_gather(): fromdown = lax.ppermute(fromdown, 'y', up)  25.3 us
    ppermute x3, starting transfers between devices, ring_gather(): fromup = lax.ppermute(fromup, 'y', down)  14.1 us
    all_to_all x1, starting transfers between devices, local(): lax.all_to_all(sent.reshape(experts, layers * capacity, 2 * width), 'e',...  12 us
    ppermute x4, starting transfers between devices, ring_gather(): fromdown = lax.ppermute(fromdown, 'y', up)  9.22 us
    pallas_call x1, Pallas kernels, forward(): pl.pallas_call(forward_kernel, out_shape=(jax.ShapeDtypeStruct((rows, col...  6.88 us
    ppermute x1, waiting for transfers between devices, local(): other = lax.ppermute(own, 'c', swap)  5.96 us
    ppermute x1, waiting for transfers between devices, local(): paired = lax.ppermute(mine, 'k', swap)  5.38 us
  transfers between devices with their start and end apart: 14, of which 10 were waited for; matrix products, arithmetic and copies ran while one was open for 1% of the time, Pallas kernels for 7%

profile of v7, /device:TPU:2, one launch (start us, length us, event | category | flops | bytes accessed | tf_op | source)
XLA Modules:
  0.0 175.9 jit_solution(14511735711378404152)
XLA Ops:
  7.2 3.6 %pack.1 = bf16[384,4096]{1,0:T(8,128)(2,1)} custom-call(bf16[2,128,2048]{2,1,0:T(8,128)(2,1)} %x_hbm.1, bf16[2,128,2048]{2,1,0:T(8,128)(2,1)} %dy_hbm.1, bf16[2,128]{1,0:T(2,128)(2,1)} %gate_ref.1, s32[2,128]{1,0:T(2,128)} %bitcast.11), custom_call_target="tpu_custom_call" | custom-call | flops 805306368 | bytes 5242880 | tf_op jit(solution)/shard_map/pack/pallas_call | solution.py:92
  10.8 12.0 %all-to-all-start = ((bf16[16,24,4096]{2,1,0:T(8,128)(2,1)}), bf16[16,24,4096]{2,1,0:T(8,128)(2,1)S(1)}, u32[]{:S(2)}, u32[]{:S(2)}) async-start(bf16[16,24,4096]{2,1,0:T(8,128)(2,1)} %bitcast.13), calls=%async_computation | async-start | bytes 6291456 | tf_op jit(solution)/shard_map/all_to_all | solution.py:459
  22.8 0.0 reduce-scatter.2.cloned.1.call-start
  22.8 1.6 join.1
  24.5 3.3 %collective-permute-start = (bf16[128,768]{1,0:T(8,128)(2,1)}, bf16[128,768]{1,0:T(8,128)(2,1)S(1)}, u32[]{:S(2)}, u32[]{:S(2)}) collective-permute-start(bf16[128,768]{1,0:T(8,128)(2,1)} %join.1), channel_id=1, source_target_pairs={{0,1},{1,0},{2,3},{3,2},{4,5},{5,4},{6,7},{7,6},{8,9},{9,8},{10,11... | collective-permute-start | bytes 589832 | tf_op jit(solution)/shard_map/ppermute | solution.py:458
  27.8 5.4 %collective-permute-done = bf16[128,768]{1,0:T(8,128)(2,1)S(1)} collective-permute-done((bf16[128,768]{1,0:T(8,128)(2,1)}, bf16[128,768]{1,0:T(8,128)(2,1)S(1)}, u32[]{:S(2)}, u32[]{:S(2)}) %collective-permute-start) | collective-permute-done | bytes 196640 | tf_op jit(solution)/shard_map/ppermute | solution.py:458
  33.2 1.0 pad_maximum_fusion.refs_0_
  34.1 0.0 copy-start.3
  34.1 3.5 %collective-permute-start.4 = (bf16[128,1536]{1,0:T(8,128)(2,1)S(1)}, bf16[128,1536]{1,0:T(8,128)(2,1)S(1)}, u32[]{:S(2)}, u32[]{:S(2)}) collective-permute-start(bf16[128,1536]{1,0:T(8,128)(2,1)S(1)} %pad_maximum_fusion.refs_0_), channel_id=1, source_target_pairs={{0,64},{64,128},{128,192},{192,256},{256,320},{320,384},{384,448},... | collective-permute-start | bytes 1179656 | tf_op jit(solution)/shard_map/ppermute | solution.py:177
  37.6 3.8 %collective-permute-start.1 = (bf16[128,1536]{1,0:T(8,128)(2,1)S(1)}, bf16[128,1536]{1,0:T(8,128)(2,1)S(1)}, u32[]{:S(2)}, u32[]{:S(2)}) collective-permute-start(bf16[128,1536]{1,0:T(8,128)(2,1)S(1)} %pad_maximum_fusion.refs_0_), channel_id=1, source_target_pairs={{0,448},{64,0},{128,64},{192,128},{256,192},{320,256},{384,320},{4... | collective-permute-start | bytes 1179656 | tf_op jit(solution)/shard_map/ppermute | solution.py:180
  41.5 6.2 %collective-permute-done.4.refs_7_ = bf16[128,1536]{1,0:T(8,128)(2,1)S(1)} collective-permute-done((bf16[128,1536]{1,0:T(8,128)(2,1)S(1)}, bf16[128,1536]{1,0:T(8,128)(2,1)S(1)}, u32[]{:S(2)}, u32[]{:S(2)}) %collective-permute-start.4) | collective-permute-done | bytes 393248 | tf_op jit(solution)/shard_map/ppermute | solution.py:177
  47.7 0.0 copy-start.4
  47.7 1.9 %collective-permute-start.5 = (bf16[128,1536]{1,0:T(8,128)(2,1)S(1)}, bf16[128,1536]{1,0:T(8,128)(2,1)S(1)}, u32[]{:S(2)}, u32[]{:S(2)}) collective-permute-start(bf16[128,1536]{1,0:T(8,128)(2,1)S(1)} %collective-permute-done.4.refs_7_), channel_id=1, source_target_pairs={{0,64},{64,128},{128,192},{192,256},{256,320},{320,384},{384,448},... | collective-permute-start | bytes 1179656 | tf_op jit(solution)/shard_map/ppermute | solution.py:177
  49.6 0.0 collective-permute-done.1.refs_1_
  49.6 0.0 copy-done.4
  49.6 0.0 copy-start.5
  49.6 5.1 %collective-permute-start.2 = (bf16[128,1536]{1,0:T(8,128)(2,1)S(1)}, bf16[128,1536]{1,0:T(8,128)(2,1)}, u32[]{:S(2)}, u32[]{:S(2)}) collective-permute-start(bf16[128,1536]{1,0:T(8,128)(2,1)S(1)} %collective-permute-done.1.refs_1_), channel_id=1, source_target_pairs={{0,448},{64,0},{128,64},{192,128},{256,192},{320,256},{384,320},{4... | collective-permute-start | bytes 1179656 | tf_op jit(solution)/shard_map/ppermute | solution.py:180
  54.8 5.3 %collective-permute-done.5.refs_6_ = bf16[128,1536]{1,0:T(8,128)(2,1)S(1)} collective-permute-done((bf16[128,1536]{1,0:T(8,128)(2,1)S(1)}, bf16[128,1536]{1,0:T(8,128)(2,1)S(1)}, u32[]{:S(2)}, u32[]{:S(2)}) %collective-permute-start.5) | collective-permute-done | bytes 393248 | tf_op jit(solution)/shard_map/ppermute | solution.py:177
  60.1 0.0 copy-done.5
  60.1 0.0 copy-start.6
  60.1 1.9 %collective-permute-start.6 = (bf16[128,1536]{1,0:T(8,128)(2,1)S(1)}, bf16[128,1536]{1,0:T(8,128)(2,1)}, u32[]{:S(2)}, u32[]{:S(2)}) collective-permute-start(bf16[128,1536]{1,0:T(8,128)(2,1)S(1)} %collective-permute-done.5.refs_6_), channel_id=1, source_target_pairs={{0,64},{64,128},{128,192},{192,256},{256,320},{320,384},{384,448},... | collective-permute-start | bytes 1179656 | tf_op jit(solution)/shard_map/ppermute | solution.py:177
  62.0 0.0 collective-permute-done.2.refs_2_
  62.0 0.0 copy-done.6
  62.0 5.1 %collective-permute-start.3 = (bf16[128,1536]{1,0:T(8,128)(2,1)}, bf16[128,1536]{1,0:T(8,128)(2,1)}, u32[]{:S(2)}, u32[]{:S(2)}) collective-permute-start(bf16[128,1536]{1,0:T(8,128)(2,1)} %collective-permute-done.2.refs_2_), channel_id=1, source_target_pairs={{0,448},{64,0},{128,64},{192,128},{256,192},{320,256},{384,320},{4... | collective-permute-start | bytes 1179656 | tf_op jit(solution)/shard_map/ppermute | solution.py:180
  67.2 4.5 %collective-permute-done.6.refs_5_ = bf16[128,1536]{1,0:T(8,128)(2,1)} collective-permute-done((bf16[128,1536]{1,0:T(8,128)(2,1)S(1)}, bf16[128,1536]{1,0:T(8,128)(2,1)}, u32[]{:S(2)}, u32[]{:S(2)}) %collective-permute-start.6) | collective-permute-done | bytes 393248 | tf_op jit(solution)/shard_map/ppermute | solution.py:177
  71.6 1.9 %collective-permute-start.7 = (bf16[128,1536]{1,0:T(8,128)(2,1)}, bf16[128,1536]{1,0:T(8,128)(2,1)}, u32[]{:S(2)}, u32[]{:S(2)}) collective-permute-start(bf16[128,1536]{1,0:T(8,128)(2,1)} %collective-permute-done.6.refs_5_), channel_id=1, source_target_pairs={{0,64},{64,128},{128,192},{192,256},{256,320},{320,384},{384,448},... | collective-permute-start | bytes 1179656 | tf_op jit(solution)/shard_map/ppermute | solution.py:177
  73.6 0.0 collective-permute-done.3.refs_3_
  73.6 9.3 %collective-permute-done.7.refs_4_ = bf16[128,1536]{1,0:T(8,128)(2,1)} collective-permute-done((bf16[128,1536]{1,0:T(8,128)(2,1)}, bf16[128,1536]{1,0:T(8,128)(2,1)}, u32[]{:S(2)}, u32[]{:S(2)}) %collective-permute-start.7) | collective-permute-done | bytes 393248 | tf_op jit(solution)/shard_map/ppermute | solution.py:177
  82.8 0.0 copy-done.3
  82.8 3.6 %order.1.own_hbm = bf16[8,128,1536]{2,1,0:T(8,128)(2,1)} custom-call(s32[1]{0:T(128)} %bitcast.4.place_ref, bf16[128,1536]{1,0:T(8,128)(2,1)} %copy-done.3, bf16[128,1536]{1,0:T(8,128)(2,1)} %copy-done.5, bf16[128,1536]{1,0:T(8,128)(2,1)} %collective-permute-done.2.refs_2_, bf16[128,1536]{1,0:T(8,128)(2,1)} %collective-permute-done.3.refs_3_, ...), custom_call_target="tpu_custom_call" | custom-call | bytes 6291456 | tf_op jit(solution)/shard_map/order/pallas_call | solution.py:157
  86.4 1.9 %collective-permute-start.8 = (bf16[8,128,1536]{2,1,0:T(8,128)(2,1)}, bf16[8,128,1536]{2,1,0:T(8,128)(2,1)}, u32[]{:S(2)}, u32[]{:S(2)}) collective-permute-start(bf16[8,128,1536]{2,1,0:T(8,128)(2,1)} %order.1.own_hbm), channel_id=1, source_target_pairs={{0,32},{32,0},{1,33},{33,1},{2,34},{34,2},{3,35},{35,3},{4,36},{36... | collective-permute-start | bytes 9437192 | tf_op jit(solution)/shard_map/ppermute | solution.py:463
  88.3 6.0 %collective-permute-done.8.other_hbm = bf16[8,128,1536]{2,1,0:T(8,128)(2,1)} collective-permute-done((bf16[8,128,1536]{2,1,0:T(8,128)(2,1)}, bf16[8,128,1536]{2,1,0:T(8,128)(2,1)}, u32[]{:S(2)}, u32[]{:S(2)}) %collective-permute-start.8) | collective-permute-done | bytes 3145760 | tf_op jit(solution)/shard_map/ppermute | solution.py:463
  94.3 3.4 %all-to-all-done = bf16[16,24,4096]{2,1,0:T(8,128)(2,1)S(1)} async-done(((bf16[16,24,4096]{2,1,0:T(8,128)(2,1)}), bf16[16,24,4096]{2,1,0:T(8,128)(2,1)S(1)}, u32[]{:S(2)}, u32[]{:S(2)}) %all-to-all-start) | async-done | bytes 3145760 | tf_op jit(solution)/shard_map/all_to_all | solution.py:459
  97.7 6.9 %forward.1 = (bf16[384,1024]{1,0:T(8,128)(2,1)S(1)}, bf16[384,512]{1,0:T(8,128)(2,1)S(1)}, bf16[384,128]{1,0:T(8,128)(2,1)S(1)}, bf16[1024,1536]{1,0:T(8,128)(2,1)S(1)}, bf16[8,2,128,1536]{3,2,1,0:T(8,128)(2,1)S(1)}) custom-call(s32[1]{0:T(128)} %bitcast.core_ref, bf16[384,4096]{1,0:T(8,128)(2,1)S(1)} %bitcast.9, bf16[8,128,1536]{2,1,0:T(8,128)(2,1)} %order.1.own_hbm, ...), custom_call_target="tpu_custom_call" | custom-call | flops 3623878656 | bytes 14680064 | tf_op jit(solution)/shard_map/forward/pallas_call | solution.py:270
  104.6 1.9 %collective-permute-start.9 = (bf16[1024,1536]{1,0:T(8,128)(2,1)S(1)}, bf16[1024,1536]{1,0:T(8,128)(2,1)S(1)}, u32[]{:S(2)}, u32[]{:S(2)}) collective-permute-start(bf16[1024,1536]{1,0:T(8,128)(2,1)S(1)} %get-tuple-element.29), channel_id=1, source_target_pairs={{0,32},{32,0},{1,33},{33,1},{2,34},{34,2},{3,35},{35,3},{4,36},{36... | collective-permute-start | bytes 9437192 | tf_op jit(solution)/shard_map/ppermute | solution.py:466
  106.5 3.0 %input_terms.1 = bf16[384,2176]{1,0:T(8,128)(2,1)} custom-call(bf16[384,1024]{1,0:T(8,128)(2,1)S(1)} %get-tuple-element.22.grads_ref, bf16[8,2,128,1536]{3,2,1,0:T(8,128)(2,1)S(1)} %get-tuple-element.23.held_ref, bf16[384,128]{1,0:T(8,128)(2,1)S(1)} %get-tuple-element.24.gate_ref), custom_call_target="tpu_custom_call" | custom-call | flops 1610612736 | bytes 9437184 | tf_op jit(solution)/shard_map/input_terms/pallas_call | solution.py:313
  109.5 1.8 %own_terms.1.own_ref = f32[1024,1536]{1,0:T(8,128)S(1)} custom-call(s32[1]{0:T(128)} %bitcast.core_ref, bf16[384,4096]{1,0:T(8,128)(2,1)S(1)} %bitcast.10, bf16[384,1024]{1,0:T(8,128)(2,1)S(1)} %get-tuple-element.22.grads_ref, bf16[384,512]{1,0:T(8,128)(2,1)S(1)} %get-tuple-element.28.hidden_ref), custom_call_target="tpu_custom_call" | custom-call | flops 1207959552 | bytes 10485760 | tf_op jit(solution)/shard_map/own_terms/pallas_call | solution.py:330
  111.4 0.7 collective-permute-done.9.arrived_ref
  112.1 1.8 %add.4 = bf16[1024,1536]{1,0:T(8,128)(2,1)} custom-call(f32[1024,1536]{1,0:T(8,128)S(1)} %own_terms.1.own_ref, bf16[1024,1536]{1,0:T(8,128)(2,1)S(1)} %collective-permute-done.9.arrived_ref), custom_call_target="tpu_custom_call" | custom-call | flops 1572864 | bytes 12582912 | tf_op jit(solution)/shard_map/add/pallas_call | solution.py:356
  113.9 0.0 copy-start.1
  113.9 0.0 copy-start.2
  114.0 0.0 reduce-scatter.2.cloned.1.call-update
  114.0 4.1 %all-to-all-start.1 = ((bf16[16,24,2176]{2,1,0:T(8,128)(2,1)}), bf16[16,24,2176]{2,1,0:T(8,128)(2,1)S(1)}, u32[]{:S(2)}, u32[]{:S(2)}) async-start(bf16[16,24,2176]{2,1,0:T(8,128)(2,1)} %bitcast.5), calls=%async_computation.1 | async-start | bytes 3342336 | tf_op jit(solution)/shard_map/all_to_all | solution.py:472
  118.0 41.6 %reduce-scatter.2.cloned.1.call-done.reduced_ref = bf16[128,1536]{1,0:T(8,128)(2,1)} async-done(((bf16[1024,1536]{1,0:T(8,128)(2,1)}), bf16[128,1536]{1,0:T(8,128)(2,1)}) %reduce-scatter.2.cloned.1.call-update) | async-done | bytes 393232 | tf_op jit(solution)/shard_map/reduce_scatter | solution.py:471
  159.7 0.0 copy-start
  159.7 1.0 slice.4
  160.7 2.6 %collective-permute-start.10 = (bf16[128,768]{1,0:T(8,128)(2,1)S(1)}, bf16[128,768]{1,0:T(8,128)(2,1)S(1)}, u32[]{:S(2)}, u32[]{:S(2)}) collective-permute-start(bf16[128,768]{1,0:T(8,128)(2,1)S(1)} %slice.4), channel_id=1, source_target_pairs={{0,1},{1,0},{2,3},{3,2},{4,5},{5,4},{6,7},{7,6},{8,9},{9,8},{10,11... | collective-permute-start | bytes 589832 | tf_op jit(solution)/shard_map/ppermute | solution.py:476
  163.4 0.0 all-to-all-done.1
  163.4 0.0 copy-done.1
  163.4 0.0 copy-done.2
  163.4 2.9 %unpack.1 = (bf16[2,128,2048]{2,1,0:T(8,128)(2,1)}, bf16[2,128]{1,0:T(2,128)(2,1)}) custom-call(bf16[384,2176]{1,0:T(8,128)(2,1)S(1)} %bitcast.7, bf16[384,2176]{1,0:T(8,128)(2,1)S(1)} %bitcast.8, bf16[2,128]{1,0:T(2,128)(2,1)S(1)} %copy-done.2, s32[2,128]{1,0:T(2,128)S(1)} %bitcast.12), custom_call_target="tpu_custom_call" | custom-call | flops 402653184 | bytes 3145728 | tf_op jit(solution)/shard_map/unpack/pallas_call | solution.py:395
  166.3 2.0 %collective-permute-done.10.partner_ref = bf16[128,768]{1,0:T(8,128)(2,1)S(1)} collective-permute-done((bf16[128,768]{1,0:T(8,128)(2,1)S(1)}, bf16[128,768]{1,0:T(8,128)(2,1)S(1)}, u32[]{:S(2)}, u32[]{:S(2)}) %collective-permute-start.10) | collective-permute-done | bytes 196640 | tf_op jit(solution)/shard_map/ppermute | solution.py:476
  168.3 0.0 copy-done
  168.3 0.8 finish.1
Async XLA Ops:
  10.8 86.9 %all-to-all-start = ((bf16[16,24,4096]{2,1,0:T(8,128)(2,1)}), bf16[16,24,4096]{2,1,0:T(8,128)(2,1)S(1)}, u32[]{:S(2)}, u32[]{:S(2)}) async-start(bf16[16,24,4096]{2,1,0:T(8,128)(2,1)} %bitcast.13), calls=%async_computation | async-start | bytes 6291456 | tf_op jit(solution)/shard_map/all_to_all | solution.py:459
  22.8 136.9 %reduce-scatter.2.cloned.1.call-start = ((), (), s32[]{:S(2)}) async-start(), calls=%async_computation.3 | async-start | bytes 3538944 | tf_op jit(solution)/shard_map/reduce_scatter | solution.py:471
  24.5 8.7 %collective-permute-start = (bf16[128,768]{1,0:T(8,128)(2,1)}, bf16[128,768]{1,0:T(8,128)(2,1)S(1)}, u32[]{:S(2)}, u32[]{:S(2)}) collective-permute-start(bf16[128,768]{1,0:T(8,128)(2,1)} %join.1), channel_id=1, source_target_pairs={{0,1},{1,0},{2,3},{3,2},{4,5},{5,4},{6,7},{7,6},{8,9},{9,8},{10,11... | collective-permute-start | bytes 589832 | tf_op jit(solution)/shard_map/ppermute | solution.py:458
  34.1 48.7 %copy-start.3 = (bf16[128,1536]{1,0:T(8,128)(2,1)}, bf16[128,1536]{1,0:T(8,128)(2,1)S(1)}, u32[]{:S(2)}) copy-start(bf16[128,1536]{1,0:T(8,128)(2,1)S(1)} %pad_maximum_fusion.refs_0_) | copy-start | bytes 1179652
  34.1 13.6 %collective-permute-start.4 = (bf16[128,1536]{1,0:T(8,128)(2,1)S(1)}, bf16[128,1536]{1,0:T(8,128)(2,1)S(1)}, u32[]{:S(2)}, u32[]{:S(2)}) collective-permute-start(bf16[128,1536]{1,0:T(8,128)(2,1)S(1)} %pad_maximum_fusion.refs_0_), channel_id=1, source_target_pairs={{0,64},{64,128},{128,192},{192,256},{256,320},{320,384},{384,448},... | collective-permute-start | bytes 1179656 | tf_op jit(solution)/shard_map/ppermute | solution.py:177
  37.6 12.0 %collective-permute-start.1 = (bf16[128,1536]{1,0:T(8,128)(2,1)S(1)}, bf16[128,1536]{1,0:T(8,128)(2,1)S(1)}, u32[]{:S(2)}, u32[]{:S(2)}) collective-permute-start(bf16[128,1536]{1,0:T(8,128)(2,1)S(1)} %pad_maximum_fusion.refs_0_), channel_id=1, source_target_pairs={{0,448},{64,0},{128,64},{192,128},{256,192},{320,256},{384,320},{4... | collective-permute-start | bytes 1179656 | tf_op jit(solution)/shard_map/ppermute | solution.py:180
  47.7 1.9 %copy-start.4 = (bf16[128,1536]{1,0:T(8,128)(2,1)}, bf16[128,1536]{1,0:T(8,128)(2,1)S(1)}, u32[]{:S(2)}) copy-start(bf16[128,1536]{1,0:T(8,128)(2,1)S(1)} %collective-permute-done.4.refs_7_) | copy-start | bytes 1179652
  47.7 12.4 %collective-permute-start.5 = (bf16[128,1536]{1,0:T(8,128)(2,1)S(1)}, bf16[128,1536]{1,0:T(8,128)(2,1)S(1)}, u32[]{:S(2)}, u32[]{:S(2)}) collective-permute-start(bf16[128,1536]{1,0:T(8,128)(2,1)S(1)} %collective-permute-done.4.refs_7_), channel_id=1, source_target_pairs={{0,64},{64,128},{128,192},{192,256},{256,320},{320,384},{384,448},... | collective-permute-start | bytes 1179656 | tf_op jit(solution)/shard_map/ppermute | solution.py:177
  49.6 10.4 %copy-start.5 = (bf16[128,1536]{1,0:T(8,128)(2,1)}, bf16[128,1536]{1,0:T(8,128)(2,1)S(1)}, u32[]{:S(2)}) copy-start(bf16[128,1536]{1,0:T(8,128)(2,1)S(1)} %collective-permute-done.1.refs_1_) | copy-start | bytes 1179652
  49.6 12.4 %collective-permute-start.2 = (bf16[128,1536]{1,0:T(8,128)(2,1)S(1)}, bf16[128,1536]{1,0:T(8,128)(2,1)}, u32[]{:S(2)}, u32[]{:S(2)}) collective-permute-start(bf16[128,1536]{1,0:T(8,128)(2,1)S(1)} %collective-permute-done.1.refs_1_), channel_id=1, source_target_pairs={{0,448},{64,0},{128,64},{192,128},{256,192},{320,256},{384,320},{4... | collective-permute-start | bytes 1179656 | tf_op jit(solution)/shard_map/ppermute | solution.py:180
  60.1 1.9 %copy-start.6 = (bf16[128,1536]{1,0:T(8,128)(2,1)}, bf16[128,1536]{1,0:T(8,128)(2,1)S(1)}, u32[]{:S(2)}) copy-start(bf16[128,1536]{1,0:T(8,128)(2,1)S(1)} %collective-permute-done.5.refs_6_) | copy-start | bytes 1179652
  60.1 11.6 %collective-permute-start.6 = (bf16[128,1536]{1,0:T(8,128)(2,1)S(1)}, bf16[128,1536]{1,0:T(8,128)(2,1)}, u32[]{:S(2)}, u32[]{:S(2)}) collective-permute-start(bf16[128,1536]{1,0:T(8,128)(2,1)S(1)} %collective-permute-done.5.refs_6_), channel_id=1, source_target_pairs={{0,64},{64,128},{128,192},{192,256},{256,320},{320,384},{384,448},... | collective-permute-start | bytes 1179656 | tf_op jit(solution)/shard_map/ppermute | solution.py:177
  62.0 11.5 %collective-permute-start.3 = (bf16[128,1536]{1,0:T(8,128)(2,1)}, bf16[128,1536]{1,0:T(8,128)(2,1)}, u32[]{:S(2)}, u32[]{:S(2)}) collective-permute-start(bf16[128,1536]{1,0:T(8,128)(2,1)} %collective-permute-done.2.refs_2_), channel_id=1, source_target_pairs={{0,448},{64,0},{128,64},{192,128},{256,192},{320,256},{384,320},{4... | collective-permute-start | bytes 1179656 | tf_op jit(solution)/shard_map/ppermute | solution.py:180
  71.6 11.2 %collective-permute-start.7 = (bf16[128,1536]{1,0:T(8,128)(2,1)}, bf16[128,1536]{1,0:T(8,128)(2,1)}, u32[]{:S(2)}, u32[]{:S(2)}) collective-permute-start(bf16[128,1536]{1,0:T(8,128)(2,1)} %collective-permute-done.6.refs_5_), channel_id=1, source_target_pairs={{0,64},{64,128},{128,192},{192,256},{256,320},{320,384},{384,448},... | collective-permute-start | bytes 1179656 | tf_op jit(solution)/shard_map/ppermute | solution.py:177
  86.4 7.9 %collective-permute-start.8 = (bf16[8,128,1536]{2,1,0:T(8,128)(2,1)}, bf16[8,128,1536]{2,1,0:T(8,128)(2,1)}, u32[]{:S(2)}, u32[]{:S(2)}) collective-permute-start(bf16[8,128,1536]{2,1,0:T(8,128)(2,1)} %order.1.own_hbm), channel_id=1, source_target_pairs={{0,32},{32,0},{1,33},{33,1},{2,34},{34,2},{3,35},{35,3},{4,36},{36... | collective-permute-start | bytes 9437192 | tf_op jit(solution)/shard_map/ppermute | solution.py:463
  104.6 7.6 %collective-permute-start.9 = (bf16[1024,1536]{1,0:T(8,128)(2,1)S(1)}, bf16[1024,1536]{1,0:T(8,128)(2,1)S(1)}, u32[]{:S(2)}, u32[]{:S(2)}) collective-permute-start(bf16[1024,1536]{1,0:T(8,128)(2,1)S(1)} %get-tuple-element.29), channel_id=1, source_target_pairs={{0,32},{32,0},{1,33},{33,1},{2,34},{34,2},{3,35},{35,3},{4,36},{36... | collective-permute-start | bytes 9437192 | tf_op jit(solution)/shard_map/ppermute | solution.py:466
  113.9 49.4 %copy-start.1 = (s32[2,128,1]{1,2,0:T(1,128)S(1)}, s32[2,128,1]{1,2,0:T(1,128)}, u32[]{:S(2)}) copy-start(s32[2,128,1]{1,2,0:T(1,128)} %param.10) | copy-start | bytes 3076
  113.9 49.4 %copy-start.2 = (bf16[2,128]{1,0:T(2,128)(2,1)S(1)}, bf16[2,128]{1,0:T(2,128)(2,1)}, u32[]{:S(2)}) copy-start(bf16[2,128]{1,0:T(2,128)(2,1)} %gate_ref.1) | copy-start | bytes 1540
  114.0 49.4 %all-to-all-start.1 = ((bf16[16,24,2176]{2,1,0:T(8,128)(2,1)}), bf16[16,24,2176]{2,1,0:T(8,128)(2,1)S(1)}, u32[]{:S(2)}, u32[]{:S(2)}) async-start(bf16[16,24,2176]{2,1,0:T(8,128)(2,1)} %bitcast.5), calls=%async_computation.1 | async-start | bytes 3342336 | tf_op jit(solution)/shard_map/all_to_all | solution.py:472
  159.7 8.6 %copy-start = (bf16[128,1536]{1,0:T(8,128)(2,1)S(1)}, bf16[128,1536]{1,0:T(8,128)(2,1)}, u32[]{:S(2)}) copy-start(bf16[128,1536]{1,0:T(8,128)(2,1)} %reduce-scatter.2.cloned.1.call-done.reduced_ref) | copy-start | bytes 1179652
  160.7 7.6 %collective-permute-start.10 = (bf16[128,768]{1,0:T(8,128)(2,1)S(1)}, bf16[128,768]{1,0:T(8,128)(2,1)S(1)}, u32[]{:S(2)}, u32[]{:S(2)}) collective-permute-start(bf16[128,768]{1,0:T(8,128)(2,1)S(1)} %slice.4), channel_id=1, source_target_pairs={{0,1},{1,0},{2,3},{3,2},{4,5},{5,4},{6,7},{7,6},{8,9},{9,8},{10,11... | collective-permute-start | bytes 589832 | tf_op jit(solution)/shard_map/ppermute | solution.py:476
Sparse Core Ops, SparseCore 0:
  114.1 45.5 reduce-scatter.1

commit v8 on v7

--- a/solution.py
+++ b/solution.py
@@ -340,25 +340,35 @@
 
 def add_kernel(own_ref, arrived_ref, out_hbm, out_ref, sems):
     count = sems.shape[0]
-    rows = out_ref.shape[0] // count
+    rows, columns = own_ref.shape
+    rows, columns = rows // count, columns // 2
     copies = []
     for i in range(count):
         at = slice(i * rows, (i + 1) * rows)
-        total = own_ref[at, :] + arrived_ref[at, :].astype(jnp.float32)
-        out_ref[at, :] = total.astype(jnp.bfloat16)
-        copies.append(pltpu.make_async_copy(out_ref.at[at], out_hbm.at[at], sems.at[i]))
+        for part in range(2):
+            side = slice(part * columns, (part + 1) * columns)
+            total = own_ref[at, side] + arrived_ref[at, side].astype(jnp.float32)
+            first = (2 * i + part) * rows
+            out_ref[first : first + rows, :] = total.astype(jnp.bfloat16)
+        both = pl.ds(2 * i * rows, 2 * rows)
+        copies.append(pltpu.make_async_copy(out_ref.at[both], out_hbm.at[both], sems.at[i]))
         copies[-1].start()
     for copy in copies:
         copy.wait()
 
 
-def add(own, arrived):
+def add(own, arrived, piece):
+    rows, columns = arrived.shape
+    shape = (2 * rows, columns // 2)
     return pl.pallas_call(
         add_kernel,
-        out_shape=pltpu.HBM(arrived.shape, jnp.bfloat16),
+        out_shape=pltpu.HBM(shape, jnp.bfloat16),
         in_specs=[whole()] * 2,
         out_specs=whole(pl.ANY),
-        scratch_shapes=[pltpu.VMEM(arrived.shape, jnp.bfloat16), pltpu.SemaphoreType.DMA((4,))],
+        scratch_shapes=[
+            pltpu.VMEM(shape, jnp.bfloat16),
+            pltpu.SemaphoreType.DMA((rows // piece,)),
+        ],
         compiler_params=pltpu.CompilerParams(vmem_limit_bytes=20 * MIB),
         cost_estimate=cost(arrived.size, 12 * MIB),
         name="add",
@@ -467,13 +477,13 @@
     back = input_terms(grads, held, gate_sum)
     hidden, back = lax.optimization_barrier((hidden, back))
     total = own_terms(core, recv, grads, hidden, own.shape[2])
-    total = add(total, arrived)
+    total = add(total, arrived, w_gate.shape[0])
     reduced = lax.psum_scatter(total, "y", scatter_dimension=0, tiled=True)
     back = lax.all_to_all(
         back.reshape(experts, layers * capacity, back.shape[1]), "e", 0, 0, tiled=True
     ).reshape(back.shape)
     grad_inputs, grad_gates = unpack(back, gates, route, capacity)
-    partner = lax.ppermute(reduced[:, 3 * unit :], "k", swap)
+    partner = lax.ppermute(reduced[w_gate.shape[0] :], "k", swap)
     return (grad_inputs, grad_gates, *finish(reduced, partner))
 
 

time: 177 us -> 177 us (level)
  no operation moved by 1% of the time
where the time goes in v8:
time: 177 us; the launch traced here: 176 us
  waiting for transfers between devices  84.4 us (48%)
  starting transfers between devices  49.2 us (28%)
  Pallas kernels  26 us (15%)
  between operations  14.3 us (8%)
    reduce_scatter x1, waiting for transfers between devices, local(): reduced = lax.psum_scatter(total, 'y', scatter_dimension=0, tiled=True)  41.6 us
    ppermute x4, waiting for transfers between devices, ring_gather(): fromdown = lax.ppermute(fromdown, 'y', up)  25.3 us
    ppermute x3, starting transfers between devices, ring_gather(): fromup = lax.ppermute(fromup, 'y', down)  14.1 us
    all_to_all x1, starting transfers between devices, local(): lax.all_to_all(sent.reshape(experts, layers * capacity, 2 * width), 'e',...  12 us
    ppermute x4, starting transfers between devices, ring_gather(): fromdown = lax.ppermute(fromdown, 'y', up)  9.22 us
    pallas_call x1, Pallas kernels, forward(): pl.pallas_call(forward_kernel, out_shape=(jax.ShapeDtypeStruct((rows, col...  6.88 us
    ppermute x1, waiting for transfers between devices, local(): other = lax.ppermute(own, 'c', swap)  5.96 us
    ppermute x1, waiting for transfers between devices, local(): paired = lax.ppermute(mine, 'k', swap)  5.38 us
  transfers between devices with their start and end apart: 14, of which 10 were waited for; matrix products, arithmetic and copies ran while one was open for 1% of the time, Pallas kernels for 7%

profile of v8, /device:TPU:2, one launch (start us, length us, event | category | flops | bytes accessed | tf_op | source)
XLA Modules:
  0.0 175.9 jit_solution(13613057519410959329)
XLA Ops:
  7.2 3.6 %pack.1 = bf16[384,4096]{1,0:T(8,128)(2,1)} custom-call(bf16[2,128,2048]{2,1,0:T(8,128)(2,1)} %x_hbm.1, bf16[2,128,2048]{2,1,0:T(8,128)(2,1)} %dy_hbm.1, bf16[2,128]{1,0:T(2,128)(2,1)} %gate_ref.1, s32[2,128]{1,0:T(2,128)} %bitcast.11), custom_call_target="tpu_custom_call" | custom-call | flops 805306368 | bytes 5242880 | tf_op jit(solution)/shard_map/pack/pallas_call | solution.py:92
  10.8 12.0 %all-to-all-start = ((bf16[16,24,4096]{2,1,0:T(8,128)(2,1)}), bf16[16,24,4096]{2,1,0:T(8,128)(2,1)S(1)}, u32[]{:S(2)}, u32[]{:S(2)}) async-start(bf16[16,24,4096]{2,1,0:T(8,128)(2,1)} %bitcast.13), calls=%async_computation | async-start | bytes 6291456 | tf_op jit(solution)/shard_map/all_to_all | solution.py:469
  22.8 0.0 reduce-scatter.2.cloned.1.call-start
  22.8 1.6 join.1
  24.5 3.3 %collective-permute-start = (bf16[128,768]{1,0:T(8,128)(2,1)}, bf16[128,768]{1,0:T(8,128)(2,1)S(1)}, u32[]{:S(2)}, u32[]{:S(2)}) collective-permute-start(bf16[128,768]{1,0:T(8,128)(2,1)} %join.1), channel_id=1, source_target_pairs={{0,1},{1,0},{2,3},{3,2},{4,5},{5,4},{6,7},{7,6},{8,9},{9,8},{10,11... | collective-permute-start | bytes 589832 | tf_op jit(solution)/shard_map/ppermute | solution.py:468
  27.8 5.4 %collective-permute-done = bf16[128,768]{1,0:T(8,128)(2,1)S(1)} collective-permute-done((bf16[128,768]{1,0:T(8,128)(2,1)}, bf16[128,768]{1,0:T(8,128)(2,1)S(1)}, u32[]{:S(2)}, u32[]{:S(2)}) %collective-permute-start) | collective-permute-done | bytes 196640 | tf_op jit(solution)/shard_map/ppermute | solution.py:468
  33.2 1.0 pad_maximum_fusion.refs_0_
  34.1 0.0 copy-start.3
  34.1 3.5 %collective-permute-start.4 = (bf16[128,1536]{1,0:T(8,128)(2,1)S(1)}, bf16[128,1536]{1,0:T(8,128)(2,1)S(1)}, u32[]{:S(2)}, u32[]{:S(2)}) collective-permute-start(bf16[128,1536]{1,0:T(8,128)(2,1)S(1)} %pad_maximum_fusion.refs_0_), channel_id=1, source_target_pairs={{0,64},{64,128},{128,192},{192,256},{256,320},{320,384},{384,448},... | collective-permute-start | bytes 1179656 | tf_op jit(solution)/shard_map/ppermute | solution.py:177
  37.6 3.8 %collective-permute-start.1 = (bf16[128,1536]{1,0:T(8,128)(2,1)S(1)}, bf16[128,1536]{1,0:T(8,128)(2,1)S(1)}, u32[]{:S(2)}, u32[]{:S(2)}) collective-permute-start(bf16[128,1536]{1,0:T(8,128)(2,1)S(1)} %pad_maximum_fusion.refs_0_), channel_id=1, source_target_pairs={{0,448},{64,0},{128,64},{192,128},{256,192},{320,256},{384,320},{4... | collective-permute-start | bytes 1179656 | tf_op jit(solution)/shard_map/ppermute | solution.py:180
  41.5 6.2 %collective-permute-done.4.refs_7_ = bf16[128,1536]{1,0:T(8,128)(2,1)S(1)} collective-permute-done((bf16[128,1536]{1,0:T(8,128)(2,1)S(1)}, bf16[128,1536]{1,0:T(8,128)(2,1)S(1)}, u32[]{:S(2)}, u32[]{:S(2)}) %collective-permute-start.4) | collective-permute-done | bytes 393248 | tf_op jit(solution)/shard_map/ppermute | solution.py:177
  47.7 0.0 copy-start.4
  47.7 1.9 %collective-permute-start.5 = (bf16[128,1536]{1,0:T(8,128)(2,1)S(1)}, bf16[128,1536]{1,0:T(8,128)(2,1)S(1)}, u32[]{:S(2)}, u32[]{:S(2)}) collective-permute-start(bf16[128,1536]{1,0:T(8,128)(2,1)S(1)} %collective-permute-done.4.refs_7_), channel_id=1, source_target_pairs={{0,64},{64,128},{128,192},{192,256},{256,320},{320,384},{384,448},... | collective-permute-start | bytes 1179656 | tf_op jit(solution)/shard_map/ppermute | solution.py:177
  49.6 0.0 collective-permute-done.1.refs_1_
  49.6 0.0 copy-done.4
  49.6 0.0 copy-start.5
  49.6 5.1 %collective-permute-start.2 = (bf16[128,1536]{1,0:T(8,128)(2,1)S(1)}, bf16[128,1536]{1,0:T(8,128)(2,1)}, u32[]{:S(2)}, u32[]{:S(2)}) collective-permute-start(bf16[128,1536]{1,0:T(8,128)(2,1)S(1)} %collective-permute-done.1.refs_1_), channel_id=1, source_target_pairs={{0,448},{64,0},{128,64},{192,128},{256,192},{320,256},{384,320},{4... | collective-permute-start | bytes 1179656 | tf_op jit(solution)/shard_map/ppermute | solution.py:180
  54.8 5.3 %collective-permute-done.5.refs_6_ = bf16[128,1536]{1,0:T(8,128)(2,1)S(1)} collective-permute-done((bf16[128,1536]{1,0:T(8,128)(2,1)S(1)}, bf16[128,1536]{1,0:T(8,128)(2,1)S(1)}, u32[]{:S(2)}, u32[]{:S(2)}) %collective-permute-start.5) | collective-permute-done | bytes 393248 | tf_op jit(solution)/shard_map/ppermute | solution.py:177
  60.1 0.0 copy-done.5
  60.1 0.0 copy-start.6
  60.1 1.9 %collective-permute-start.6 = (bf16[128,1536]{1,0:T(8,128)(2,1)S(1)}, bf16[128,1536]{1,0:T(8,128)(2,1)}, u32[]{:S(2)}, u32[]{:S(2)}) collective-permute-start(bf16[128,1536]{1,0:T(8,128)(2,1)S(1)} %collective-permute-done.5.refs_6_), channel_id=1, source_target_pairs={{0,64},{64,128},{128,192},{192,256},{256,320},{320,384},{384,448},... | collective-permute-start | bytes 1179656 | tf_op jit(solution)/shard_map/ppermute | solution.py:177
  62.0 0.0 collective-permute-done.2.refs_2_
  62.0 0.0 copy-done.6
  62.0 5.1 %collective-permute-start.3 = (bf16[128,1536]{1,0:T(8,128)(2,1)}, bf16[128,1536]{1,0:T(8,128)(2,1)}, u32[]{:S(2)}, u32[]{:S(2)}) collective-permute-start(bf16[128,1536]{1,0:T(8,128)(2,1)} %collective-permute-done.2.refs_2_), channel_id=1, source_target_pairs={{0,448},{64,0},{128,64},{192,128},{256,192},{320,256},{384,320},{4... | collective-permute-start | bytes 1179656 | tf_op jit(solution)/shard_map/ppermute | solution.py:180
  67.2 4.5 %collective-permute-done.6.refs_5_ = bf16[128,1536]{1,0:T(8,128)(2,1)} collective-permute-done((bf16[128,1536]{1,0:T(8,128)(2,1)S(1)}, bf16[128,1536]{1,0:T(8,128)(2,1)}, u32[]{:S(2)}, u32[]{:S(2)}) %collective-permute-start.6) | collective-permute-done | bytes 393248 | tf_op jit(solution)/shard_map/ppermute | solution.py:177
  71.6 1.9 %collective-permute-start.7 = (bf16[128,1536]{1,0:T(8,128)(2,1)}, bf16[128,1536]{1,0:T(8,128)(2,1)}, u32[]{:S(2)}, u32[]{:S(2)}) collective-permute-start(bf16[128,1536]{1,0:T(8,128)(2,1)} %collective-permute-done.6.refs_5_), channel_id=1, source_target_pairs={{0,64},{64,128},{128,192},{192,256},{256,320},{320,384},{384,448},... | collective-permute-start | bytes 1179656 | tf_op jit(solution)/shard_map/ppermute | solution.py:177
  73.6 0.0 collective-permute-done.3.refs_3_
  73.6 9.3 %collective-permute-done.7.refs_4_ = bf16[128,1536]{1,0:T(8,128)(2,1)} collective-permute-done((bf16[128,1536]{1,0:T(8,128)(2,1)}, bf16[128,1536]{1,0:T(8,128)(2,1)}, u32[]{:S(2)}, u32[]{:S(2)}) %collective-permute-start.7) | collective-permute-done | bytes 393248 | tf_op jit(solution)/shard_map/ppermute | solution.py:177
  82.8 0.0 copy-done.3
  82.8 3.6 %order.1.own_hbm = bf16[8,128,1536]{2,1,0:T(8,128)(2,1)} custom-call(s32[1]{0:T(128)} %bitcast.4.place_ref, bf16[128,1536]{1,0:T(8,128)(2,1)} %copy-done.3, bf16[128,1536]{1,0:T(8,128)(2,1)} %copy-done.5, bf16[128,1536]{1,0:T(8,128)(2,1)} %collective-permute-done.2.refs_2_, bf16[128,1536]{1,0:T(8,128)(2,1)} %collective-permute-done.3.refs_3_, ...), custom_call_target="tpu_custom_call" | custom-call | bytes 6291456 | tf_op jit(solution)/shard_map/order/pallas_call | solution.py:157
  86.4 1.9 %collective-permute-start.8 = (bf16[8,128,1536]{2,1,0:T(8,128)(2,1)}, bf16[8,128,1536]{2,1,0:T(8,128)(2,1)}, u32[]{:S(2)}, u32[]{:S(2)}) collective-permute-start(bf16[8,128,1536]{2,1,0:T(8,128)(2,1)} %order.1.own_hbm), channel_id=1, source_target_pairs={{0,32},{32,0},{1,33},{33,1},{2,34},{34,2},{3,35},{35,3},{4,36},{36... | collective-permute-start | bytes 9437192 | tf_op jit(solution)/shard_map/ppermute | solution.py:473
  88.3 6.0 %collective-permute-done.8.other_hbm = bf16[8,128,1536]{2,1,0:T(8,128)(2,1)} collective-permute-done((bf16[8,128,1536]{2,1,0:T(8,128)(2,1)}, bf16[8,128,1536]{2,1,0:T(8,128)(2,1)}, u32[]{:S(2)}, u32[]{:S(2)}) %collective-permute-start.8) | collective-permute-done | bytes 3145760 | tf_op jit(solution)/shard_map/ppermute | solution.py:473
  94.3 3.4 %all-to-all-done = bf16[16,24,4096]{2,1,0:T(8,128)(2,1)S(1)} async-done(((bf16[16,24,4096]{2,1,0:T(8,128)(2,1)}), bf16[16,24,4096]{2,1,0:T(8,128)(2,1)S(1)}, u32[]{:S(2)}, u32[]{:S(2)}) %all-to-all-start) | async-done | bytes 3145760 | tf_op jit(solution)/shard_map/all_to_all | solution.py:469
  97.7 6.9 %forward.1 = (bf16[384,1024]{1,0:T(8,128)(2,1)S(1)}, bf16[384,512]{1,0:T(8,128)(2,1)S(1)}, bf16[384,128]{1,0:T(8,128)(2,1)S(1)}, bf16[1024,1536]{1,0:T(8,128)(2,1)S(1)}, bf16[8,2,128,1536]{3,2,1,0:T(8,128)(2,1)S(1)}) custom-call(s32[1]{0:T(128)} %bitcast.core_ref, bf16[384,4096]{1,0:T(8,128)(2,1)S(1)} %bitcast.9, bf16[8,128,1536]{2,1,0:T(8,128)(2,1)} %order.1.own_hbm, ...), custom_call_target="tpu_custom_call" | custom-call | flops 3623878656 | bytes 14680064 | tf_op jit(solution)/shard_map/forward/pallas_call | solution.py:270
  104.6 1.9 %collective-permute-start.9 = (bf16[1024,1536]{1,0:T(8,128)(2,1)S(1)}, bf16[1024,1536]{1,0:T(8,128)(2,1)S(1)}, u32[]{:S(2)}, u32[]{:S(2)}) collective-permute-start(bf16[1024,1536]{1,0:T(8,128)(2,1)S(1)} %get-tuple-element.29), channel_id=1, source_target_pairs={{0,32},{32,0},{1,33},{33,1},{2,34},{34,2},{3,35},{35,3},{4,36},{36... | collective-permute-start | bytes 9437192 | tf_op jit(solution)/shard_map/ppermute | solution.py:476
  106.5 3.0 %input_terms.1 = bf16[384,2176]{1,0:T(8,128)(2,1)} custom-call(bf16[384,1024]{1,0:T(8,128)(2,1)S(1)} %get-tuple-element.22.grads_ref, bf16[8,2,128,1536]{3,2,1,0:T(8,128)(2,1)S(1)} %get-tuple-element.23.held_ref, bf16[384,128]{1,0:T(8,128)(2,1)S(1)} %get-tuple-element.24.gate_ref), custom_call_target="tpu_custom_call" | custom-call | flops 1610612736 | bytes 9437184 | tf_op jit(solution)/shard_map/input_terms/pallas_call | solution.py:313
  109.5 1.8 %own_terms.1.own_ref = f32[1024,1536]{1,0:T(8,128)S(1)} custom-call(s32[1]{0:T(128)} %bitcast.core_ref, bf16[384,4096]{1,0:T(8,128)(2,1)S(1)} %bitcast.10, bf16[384,1024]{1,0:T(8,128)(2,1)S(1)} %get-tuple-element.22.grads_ref, bf16[384,512]{1,0:T(8,128)(2,1)S(1)} %get-tuple-element.28.hidden_ref), custom_call_target="tpu_custom_call" | custom-call | flops 1207959552 | bytes 10485760 | tf_op jit(solution)/shard_map/own_terms/pallas_call | solution.py:330
  111.4 0.7 collective-permute-done.9.arrived_ref
  112.1 1.8 %add.4 = bf16[2048,768]{1,0:T(8,128)(2,1)} custom-call(f32[1024,1536]{1,0:T(8,128)S(1)} %own_terms.1.own_ref, bf16[1024,1536]{1,0:T(8,128)(2,1)S(1)} %collective-permute-done.9.arrived_ref), custom_call_target="tpu_custom_call" | custom-call | flops 1572864 | bytes 12582912 | tf_op jit(solution)/shard_map/add/pallas_call | solution.py:363
  113.9 0.0 copy-start.1
  113.9 0.0 copy-start.2
  113.9 0.0 reduce-scatter.2.cloned.1.call-update
  114.0 4.1 %all-to-all-start.1 = ((bf16[16,24,2176]{2,1,0:T(8,128)(2,1)}), bf16[16,24,2176]{2,1,0:T(8,128)(2,1)S(1)}, u32[]{:S(2)}, u32[]{:S(2)}) async-start(bf16[16,24,2176]{2,1,0:T(8,128)(2,1)} %bitcast.5), calls=%async_computation.1 | async-start | bytes 3342336 | tf_op jit(solution)/shard_map/all_to_all | solution.py:482
  118.0 41.6 %reduce-scatter.2.cloned.1.call-done.reduced_ref = bf16[256,768]{1,0:T(8,128)(2,1)} async-done(((bf16[2048,768]{1,0:T(8,128)(2,1)}), bf16[256,768]{1,0:T(8,128)(2,1)}) %reduce-scatter.2.cloned.1.call-update) | async-done | bytes 393232 | tf_op jit(solution)/shard_map/reduce_scatter | solution.py:481
  159.7 0.0 copy-start
  159.7 1.0 slice.4
  160.7 2.6 %collective-permute-start.10 = (bf16[128,768]{1,0:T(8,128)(2,1)S(1)}, bf16[128,768]{1,0:T(8,128)(2,1)S(1)}, u32[]{:S(2)}, u32[]{:S(2)}) collective-permute-start(bf16[128,768]{1,0:T(8,128)(2,1)S(1)} %slice.4), channel_id=1, source_target_pairs={{0,1},{1,0},{2,3},{3,2},{4,5},{5,4},{6,7},{7,6},{8,9},{9,8},{10,11... | collective-permute-start | bytes 589832 | tf_op jit(solution)/shard_map/ppermute | solution.py:486
  163.3 0.0 all-to-all-done.1
  163.3 0.0 copy-done.1
  163.4 0.0 copy-done.2
  163.4 2.9 %unpack.1 = (bf16[2,128,2048]{2,1,0:T(8,128)(2,1)}, bf16[2,128]{1,0:T(2,128)(2,1)}) custom-call(bf16[384,2176]{1,0:T(8,128)(2,1)S(1)} %bitcast.7, bf16[384,2176]{1,0:T(8,128)(2,1)S(1)} %bitcast.8, bf16[2,128]{1,0:T(2,128)(2,1)S(1)} %copy-done.2, s32[2,128]{1,0:T(2,128)S(1)} %bitcast.12), custom_call_target="tpu_custom_call" | custom-call | flops 402653184 | bytes 3145728 | tf_op jit(solution)/shard_map/unpack/pallas_call | solution.py:405
  166.3 2.0 %collective-permute-done.10.partner_ref = bf16[128,768]{1,0:T(8,128)(2,1)S(1)} collective-permute-done((bf16[128,768]{1,0:T(8,128)(2,1)S(1)}, bf16[128,768]{1,0:T(8,128)(2,1)S(1)}, u32[]{:S(2)}, u32[]{:S(2)}) %collective-permute-start.10) | collective-permute-done | bytes 196640 | tf_op jit(solution)/shard_map/ppermute | solution.py:486
  168.2 0.0 copy-done
  168.2 0.8 finish.1
Async XLA Ops:
  10.8 86.9 %all-to-all-start = ((bf16[16,24,4096]{2,1,0:T(8,128)(2,1)}), bf16[16,24,4096]{2,1,0:T(8,128)(2,1)S(1)}, u32[]{:S(2)}, u32[]{:S(2)}) async-start(bf16[16,24,4096]{2,1,0:T(8,128)(2,1)} %bitcast.13), calls=%async_computation | async-start | bytes 6291456 | tf_op jit(solution)/shard_map/all_to_all | solution.py:469
  22.8 136.9 %reduce-scatter.2.cloned.1.call-start = ((), (), s32[]{:S(2)}) async-start(), calls=%async_computation.3 | async-start | bytes 3538944 | tf_op jit(solution)/shard_map/reduce_scatter | solution.py:481
  24.5 8.7 %collective-permute-start = (bf16[128,768]{1,0:T(8,128)(2,1)}, bf16[128,768]{1,0:T(8,128)(2,1)S(1)}, u32[]{:S(2)}, u32[]{:S(2)}) collective-permute-start(bf16[128,768]{1,0:T(8,128)(2,1)} %join.1), channel_id=1, source_target_pairs={{0,1},{1,0},{2,3},{3,2},{4,5},{5,4},{6,7},{7,6},{8,9},{9,8},{10,11... | collective-permute-start | bytes 589832 | tf_op jit(solution)/shard_map/ppermute | solution.py:468
  34.1 48.7 %copy-start.3 = (bf16[128,1536]{1,0:T(8,128)(2,1)}, bf16[128,1536]{1,0:T(8,128)(2,1)S(1)}, u32[]{:S(2)}) copy-start(bf16[128,1536]{1,0:T(8,128)(2,1)S(1)} %pad_maximum_fusion.refs_0_) | copy-start | bytes 1179652
  34.1 13.6 %collective-permute-start.4 = (bf16[128,1536]{1,0:T(8,128)(2,1)S(1)}, bf16[128,1536]{1,0:T(8,128)(2,1)S(1)}, u32[]{:S(2)}, u32[]{:S(2)}) collective-permute-start(bf16[128,1536]{1,0:T(8,128)(2,1)S(1)} %pad_maximum_fusion.refs_0_), channel_id=1, source_target_pairs={{0,64},{64,128},{128,192},{192,256},{256,320},{320,384},{384,448},... | collective-permute-start | bytes 1179656 | tf_op jit(solution)/shard_map/ppermute | solution.py:177
  37.6 12.0 %collective-permute-start.1 = (bf16[128,1536]{1,0:T(8,128)(2,1)S(1)}, bf16[128,1536]{1,0:T(8,128)(2,1)S(1)}, u32[]{:S(2)}, u32[]{:S(2)}) collective-permute-start(bf16[128,1536]{1,0:T(8,128)(2,1)S(1)} %pad_maximum_fusion.refs_0_), channel_id=1, source_target_pairs={{0,448},{64,0},{128,64},{192,128},{256,192},{320,256},{384,320},{4... | collective-permute-start | bytes 1179656 | tf_op jit(solution)/shard_map/ppermute | solution.py:180
  47.7 1.9 %copy-start.4 = (bf16[128,1536]{1,0:T(8,128)(2,1)}, bf16[128,1536]{1,0:T(8,128)(2,1)S(1)}, u32[]{:S(2)}) copy-start(bf16[128,1536]{1,0:T(8,128)(2,1)S(1)} %collective-permute-done.4.refs_7_) | copy-start | bytes 1179652
  47.7 12.4 %collective-permute-start.5 = (bf16[128,1536]{1,0:T(8,128)(2,1)S(1)}, bf16[128,1536]{1,0:T(8,128)(2,1)S(1)}, u32[]{:S(2)}, u32[]{:S(2)}) collective-permute-start(bf16[128,1536]{1,0:T(8,128)(2,1)S(1)} %collective-permute-done.4.refs_7_), channel_id=1, source_target_pairs={{0,64},{64,128},{128,192},{192,256},{256,320},{320,384},{384,448},... | collective-permute-start | bytes 1179656 | tf_op jit(solution)/shard_map/ppermute | solution.py:177
  49.6 10.4 %copy-start.5 = (bf16[128,1536]{1,0:T(8,128)(2,1)}, bf16[128,1536]{1,0:T(8,128)(2,1)S(1)}, u32[]{:S(2)}) copy-start(bf16[128,1536]{1,0:T(8,128)(2,1)S(1)} %collective-permute-done.1.refs_1_) | copy-start | bytes 1179652
  49.6 12.4 %collective-permute-start.2 = (bf16[128,1536]{1,0:T(8,128)(2,1)S(1)}, bf16[128,1536]{1,0:T(8,128)(2,1)}, u32[]{:S(2)}, u32[]{:S(2)}) collective-permute-start(bf16[128,1536]{1,0:T(8,128)(2,1)S(1)} %collective-permute-done.1.refs_1_), channel_id=1, source_target_pairs={{0,448},{64,0},{128,64},{192,128},{256,192},{320,256},{384,320},{4... | collective-permute-start | bytes 1179656 | tf_op jit(solution)/shard_map/ppermute | solution.py:180
  60.1 1.9 %copy-start.6 = (bf16[128,1536]{1,0:T(8,128)(2,1)}, bf16[128,1536]{1,0:T(8,128)(2,1)S(1)}, u32[]{:S(2)}) copy-start(bf16[128,1536]{1,0:T(8,128)(2,1)S(1)} %collective-permute-done.5.refs_6_) | copy-start | bytes 1179652
  60.1 11.6 %collective-permute-start.6 = (bf16[128,1536]{1,0:T(8,128)(2,1)S(1)}, bf16[128,1536]{1,0:T(8,128)(2,1)}, u32[]{:S(2)}, u32[]{:S(2)}) collective-permute-start(bf16[128,1536]{1,0:T(8,128)(2,1)S(1)} %collective-permute-done.5.refs_6_), channel_id=1, source_target_pairs={{0,64},{64,128},{128,192},{192,256},{256,320},{320,384},{384,448},... | collective-permute-start | bytes 1179656 | tf_op jit(solution)/shard_map/ppermute | solution.py:177
  62.0 11.5 %collective-permute-start.3 = (bf16[128,1536]{1,0:T(8,128)(2,1)}, bf16[128,1536]{1,0:T(8,128)(2,1)}, u32[]{:S(2)}, u32[]{:S(2)}) collective-permute-start(bf16[128,1536]{1,0:T(8,128)(2,1)} %collective-permute-done.2.refs_2_), channel_id=1, source_target_pairs={{0,448},{64,0},{128,64},{192,128},{256,192},{320,256},{384,320},{4... | collective-permute-start | bytes 1179656 | tf_op jit(solution)/shard_map/ppermute | solution.py:180
  71.6 11.2 %collective-permute-start.7 = (bf16[128,1536]{1,0:T(8,128)(2,1)}, bf16[128,1536]{1,0:T(8,128)(2,1)}, u32[]{:S(2)}, u32[]{:S(2)}) collective-permute-start(bf16[128,1536]{1,0:T(8,128)(2,1)} %collective-permute-done.6.refs_5_), channel_id=1, source_target_pairs={{0,64},{64,128},{128,192},{192,256},{256,320},{320,384},{384,448},... | collective-permute-start | bytes 1179656 | tf_op jit(solution)/shard_map/ppermute | solution.py:177
  86.4 7.9 %collective-permute-start.8 = (bf16[8,128,1536]{2,1,0:T(8,128)(2,1)}, bf16[8,128,1536]{2,1,0:T(8,128)(2,1)}, u32[]{:S(2)}, u32[]{:S(2)}) collective-permute-start(bf16[8,128,1536]{2,1,0:T(8,128)(2,1)} %order.1.own_hbm), channel_id=1, source_target_pairs={{0,32},{32,0},{1,33},{33,1},{2,34},{34,2},{3,35},{35,3},{4,36},{36... | collective-permute-start | bytes 9437192 | tf_op jit(solution)/shard_map/ppermute | solution.py:473
  104.6 7.6 %collective-permute-start.9 = (bf16[1024,1536]{1,0:T(8,128)(2,1)S(1)}, bf16[1024,1536]{1,0:T(8,128)(2,1)S(1)}, u32[]{:S(2)}, u32[]{:S(2)}) collective-permute-start(bf16[1024,1536]{1,0:T(8,128)(2,1)S(1)} %get-tuple-element.29), channel_id=1, source_target_pairs={{0,32},{32,0},{1,33},{33,1},{2,34},{34,2},{3,35},{35,3},{4,36},{36... | collective-permute-start | bytes 9437192 | tf_op jit(solution)/shard_map/ppermute | solution.py:476
  113.9 49.4 %copy-start.1 = (s32[2,128,1]{1,2,0:T(1,128)S(1)}, s32[2,128,1]{1,2,0:T(1,128)}, u32[]{:S(2)}) copy-start(s32[2,128,1]{1,2,0:T(1,128)} %param.10) | copy-start | bytes 3076
  113.9 49.4 %copy-start.2 = (bf16[2,128]{1,0:T(2,128)(2,1)S(1)}, bf16[2,128]{1,0:T(2,128)(2,1)}, u32[]{:S(2)}) copy-start(bf16[2,128]{1,0:T(2,128)(2,1)} %gate_ref.1) | copy-start | bytes 1540
  114.0 49.4 %all-to-all-start.1 = ((bf16[16,24,2176]{2,1,0:T(8,128)(2,1)}), bf16[16,24,2176]{2,1,0:T(8,128)(2,1)S(1)}, u32[]{:S(2)}, u32[]{:S(2)}) async-start(bf16[16,24,2176]{2,1,0:T(8,128)(2,1)} %bitcast.5), calls=%async_computation.1 | async-start | bytes 3342336 | tf_op jit(solution)/shard_map/all_to_all | solution.py:482
  159.7 8.6 %copy-start = (bf16[256,768]{1,0:T(8,128)(2,1)S(1)}, bf16[256,768]{1,0:T(8,128)(2,1)}, u32[]{:S(2)}) copy-start(bf16[256,768]{1,0:T(8,128)(2,1)} %reduce-scatter.2.cloned.1.call-done.reduced_ref) | copy-start | bytes 1179652
  160.7 7.6 %collective-permute-start.10 = (bf16[128,768]{1,0:T(8,128)(2,1)S(1)}, bf16[128,768]{1,0:T(8,128)(2,1)S(1)}, u32[]{:S(2)}, u32[]{:S(2)}) collective-permute-start(bf16[128,768]{1,0:T(8,128)(2,1)S(1)} %slice.4), channel_id=1, source_target_pairs={{0,1},{1,0},{2,3},{3,2},{4,5},{5,4},{6,7},{7,6},{8,9},{9,8},{10,11... | collective-permute-start | bytes 589832 | tf_op jit(solution)/shard_map/ppermute | solution.py:486
Sparse Core Ops, SparseCore 0:
  114.1 45.5 reduce-scatter.1

commit v9 on v7

--- a/solution.py
+++ b/solution.py
@@ -434,9 +434,8 @@
             jax.ShapeDtypeStruct((piece, unit), jnp.float32),
             jax.ShapeDtypeStruct((unit, piece), jnp.float32),
         ),
-        in_specs=[pl.BlockSpec((piece, columns), lambda t: (0, 0))] * 2,
-        out_specs=(fixed((piece, unit)), fixed((piece, unit)), fixed((unit, piece))),
-        grid=(1,),
+        in_specs=[whole()] * 2,
+        out_specs=(whole(),) * 3,
         compiler_params=pltpu.CompilerParams(vmem_limit_bytes=50 * MIB),
         cost_estimate=cost(piece * columns, MIB),
         name="finish",

time: 177 us -> 177 us (level)
  no operation moved by 1% of the time
where the time goes in v9:
time: 177 us; the launch traced here: 176 us
  waiting for transfers between devices  84.4 us (48%)
  starting transfers between devices  49.2 us (28%)
  Pallas kernels  26 us (15%)
  between operations  14.3 us (8%)
    reduce_scatter x1, waiting for transfers between devices, local(): reduced = lax.psum_scatter(total, 'y', scatter_dimension=0, tiled=True)  41.6 us
    ppermute x4, waiting for transfers between devices, ring_gather(): fromdown = lax.ppermute(fromdown, 'y', up)  25.3 us
    ppermute x3, starting transfers between devices, ring_gather(): fromup = lax.ppermute(fromup, 'y', down)  14.1 us
    all_to_all x1, starting transfers between devices, local(): lax.all_to_all(sent.reshape(experts, layers * capacity, 2 * width), 'e',...  12 us
    ppermute x4, starting transfers between devices, ring_gather(): fromdown = lax.ppermute(fromdown, 'y', up)  9.22 us
    pallas_call x1, Pallas kernels, forward(): pl.pallas_call(forward_kernel, out_shape=(jax.ShapeDtypeStruct((rows, col...  6.88 us
    ppermute x1, waiting for transfers between devices, local(): other = lax.ppermute(own, 'c', swap)  5.96 us
    ppermute x1, waiting for transfers between devices, local(): paired = lax.ppermute(mine, 'k', swap)  5.38 us
  transfers between devices with their start and end apart: 14, of which 10 were waited for; matrix products, arithmetic and copies ran while one was open for 1% of the time, Pallas kernels for 7%

profile of v9, /device:TPU:2, one launch (start us, length us, event | category | flops | bytes accessed | tf_op | source)
XLA Modules:
  0.0 175.9 jit_solution(14511735711378404152)
XLA Ops:
  7.2 3.6 %pack.1 = bf16[384,4096]{1,0:T(8,128)(2,1)} custom-call(bf16[2,128,2048]{2,1,0:T(8,128)(2,1)} %x_hbm.1, bf16[2,128,2048]{2,1,0:T(8,128)(2,1)} %dy_hbm.1, bf16[2,128]{1,0:T(2,128)(2,1)} %gate_ref.1, s32[2,128]{1,0:T(2,128)} %bitcast.11), custom_call_target="tpu_custom_call" | custom-call | flops 805306368 | bytes 5242880 | tf_op jit(solution)/shard_map/pack/pallas_call | solution.py:92
  10.8 12.0 %all-to-all-start = ((bf16[16,24,4096]{2,1,0:T(8,128)(2,1)}), bf16[16,24,4096]{2,1,0:T(8,128)(2,1)S(1)}, u32[]{:S(2)}, u32[]{:S(2)}) async-start(bf16[16,24,4096]{2,1,0:T(8,128)(2,1)} %bitcast.13), calls=%async_computation | async-start | bytes 6291456 | tf_op jit(solution)/shard_map/all_to_all | solution.py:458
  22.8 0.0 reduce-scatter.2.cloned.1.call-start
  22.8 1.6 join.1
  24.5 3.3 %collective-permute-start = (bf16[128,768]{1,0:T(8,128)(2,1)}, bf16[128,768]{1,0:T(8,128)(2,1)S(1)}, u32[]{:S(2)}, u32[]{:S(2)}) collective-permute-start(bf16[128,768]{1,0:T(8,128)(2,1)} %join.1), channel_id=1, source_target_pairs={{0,1},{1,0},{2,3},{3,2},{4,5},{5,4},{6,7},{7,6},{8,9},{9,8},{10,11... | collective-permute-start | bytes 589832 | tf_op jit(solution)/shard_map/ppermute | solution.py:457
  27.8 5.4 %collective-permute-done = bf16[128,768]{1,0:T(8,128)(2,1)S(1)} collective-permute-done((bf16[128,768]{1,0:T(8,128)(2,1)}, bf16[128,768]{1,0:T(8,128)(2,1)S(1)}, u32[]{:S(2)}, u32[]{:S(2)}) %collective-permute-start) | collective-permute-done | bytes 196640 | tf_op jit(solution)/shard_map/ppermute | solution.py:457
  33.2 1.0 pad_maximum_fusion.refs_0_
  34.1 0.0 copy-start.3
  34.1 3.5 %collective-permute-start.4 = (bf16[128,1536]{1,0:T(8,128)(2,1)S(1)}, bf16[128,1536]{1,0:T(8,128)(2,1)S(1)}, u32[]{:S(2)}, u32[]{:S(2)}) collective-permute-start(bf16[128,1536]{1,0:T(8,128)(2,1)S(1)} %pad_maximum_fusion.refs_0_), channel_id=1, source_target_pairs={{0,64},{64,128},{128,192},{192,256},{256,320},{320,384},{384,448},... | collective-permute-start | bytes 1179656 | tf_op jit(solution)/shard_map/ppermute | solution.py:177
  37.6 3.8 %collective-permute-start.1 = (bf16[128,1536]{1,0:T(8,128)(2,1)S(1)}, bf16[128,1536]{1,0:T(8,128)(2,1)S(1)}, u32[]{:S(2)}, u32[]{:S(2)}) collective-permute-start(bf16[128,1536]{1,0:T(8,128)(2,1)S(1)} %pad_maximum_fusion.refs_0_), channel_id=1, source_target_pairs={{0,448},{64,0},{128,64},{192,128},{256,192},{320,256},{384,320},{4... | collective-permute-start | bytes 1179656 | tf_op jit(solution)/shard_map/ppermute | solution.py:180
  41.5 6.2 %collective-permute-done.4.refs_7_ = bf16[128,1536]{1,0:T(8,128)(2,1)S(1)} collective-permute-done((bf16[128,1536]{1,0:T(8,128)(2,1)S(1)}, bf16[128,1536]{1,0:T(8,128)(2,1)S(1)}, u32[]{:S(2)}, u32[]{:S(2)}) %collective-permute-start.4) | collective-permute-done | bytes 393248 | tf_op jit(solution)/shard_map/ppermute | solution.py:177
  47.7 0.0 copy-start.4
  47.7 1.9 %collective-permute-start.5 = (bf16[128,1536]{1,0:T(8,128)(2,1)S(1)}, bf16[128,1536]{1,0:T(8,128)(2,1)S(1)}, u32[]{:S(2)}, u32[]{:S(2)}) collective-permute-start(bf16[128,1536]{1,0:T(8,128)(2,1)S(1)} %collective-permute-done.4.refs_7_), channel_id=1, source_target_pairs={{0,64},{64,128},{128,192},{192,256},{256,320},{320,384},{384,448},... | collective-permute-start | bytes 1179656 | tf_op jit(solution)/shard_map/ppermute | solution.py:177
  49.6 0.0 collective-permute-done.1.refs_1_
  49.6 0.0 copy-done.4
  49.6 0.0 copy-start.5
  49.6 5.1 %collective-permute-start.2 = (bf16[128,1536]{1,0:T(8,128)(2,1)S(1)}, bf16[128,1536]{1,0:T(8,128)(2,1)}, u32[]{:S(2)}, u32[]{:S(2)}) collective-permute-start(bf16[128,1536]{1,0:T(8,128)(2,1)S(1)} %collective-permute-done.1.refs_1_), channel_id=1, source_target_pairs={{0,448},{64,0},{128,64},{192,128},{256,192},{320,256},{384,320},{4... | collective-permute-start | bytes 1179656 | tf_op jit(solution)/shard_map/ppermute | solution.py:180
  54.8 5.3 %collective-permute-done.5.refs_6_ = bf16[128,1536]{1,0:T(8,128)(2,1)S(1)} collective-permute-done((bf16[128,1536]{1,0:T(8,128)(2,1)S(1)}, bf16[128,1536]{1,0:T(8,128)(2,1)S(1)}, u32[]{:S(2)}, u32[]{:S(2)}) %collective-permute-start.5) | collective-permute-done | bytes 393248 | tf_op jit(solution)/shard_map/ppermute | solution.py:177
  60.1 0.0 copy-done.5
  60.1 0.0 copy-start.6
  60.1 1.9 %collective-permute-start.6 = (bf16[128,1536]{1,0:T(8,128)(2,1)S(1)}, bf16[128,1536]{1,0:T(8,128)(2,1)}, u32[]{:S(2)}, u32[]{:S(2)}) collective-permute-start(bf16[128,1536]{1,0:T(8,128)(2,1)S(1)} %collective-permute-done.5.refs_6_), channel_id=1, source_target_pairs={{0,64},{64,128},{128,192},{192,256},{256,320},{320,384},{384,448},... | collective-permute-start | bytes 1179656 | tf_op jit(solution)/shard_map/ppermute | solution.py:177
  62.0 0.0 collective-permute-done.2.refs_2_
  62.0 0.0 copy-done.6
  62.0 5.1 %collective-permute-start.3 = (bf16[128,1536]{1,0:T(8,128)(2,1)}, bf16[128,1536]{1,0:T(8,128)(2,1)}, u32[]{:S(2)}, u32[]{:S(2)}) collective-permute-start(bf16[128,1536]{1,0:T(8,128)(2,1)} %collective-permute-done.2.refs_2_), channel_id=1, source_target_pairs={{0,448},{64,0},{128,64},{192,128},{256,192},{320,256},{384,320},{4... | collective-permute-start | bytes 1179656 | tf_op jit(solution)/shard_map/ppermute | solution.py:180
  67.2 4.5 %collective-permute-done.6.refs_5_ = bf16[128,1536]{1,0:T(8,128)(2,1)} collective-permute-done((bf16[128,1536]{1,0:T(8,128)(2,1)S(1)}, bf16[128,1536]{1,0:T(8,128)(2,1)}, u32[]{:S(2)}, u32[]{:S(2)}) %collective-permute-start.6) | collective-permute-done | bytes 393248 | tf_op jit(solution)/shard_map/ppermute | solution.py:177
  71.6 1.9 %collective-permute-start.7 = (bf16[128,1536]{1,0:T(8,128)(2,1)}, bf16[128,1536]{1,0:T(8,128)(2,1)}, u32[]{:S(2)}, u32[]{:S(2)}) collective-permute-start(bf16[128,1536]{1,0:T(8,128)(2,1)} %collective-permute-done.6.refs_5_), channel_id=1, source_target_pairs={{0,64},{64,128},{128,192},{192,256},{256,320},{320,384},{384,448},... | collective-permute-start | bytes 1179656 | tf_op jit(solution)/shard_map/ppermute | solution.py:177
  73.6 0.0 collective-permute-done.3.refs_3_
  73.6 9.3 %collective-permute-done.7.refs_4_ = bf16[128,1536]{1,0:T(8,128)(2,1)} collective-permute-done((bf16[128,1536]{1,0:T(8,128)(2,1)}, bf16[128,1536]{1,0:T(8,128)(2,1)}, u32[]{:S(2)}, u32[]{:S(2)}) %collective-permute-start.7) | collective-permute-done | bytes 393248 | tf_op jit(solution)/shard_map/ppermute | solution.py:177
  82.8 0.0 copy-done.3
  82.8 3.6 %order.1.own_hbm = bf16[8,128,1536]{2,1,0:T(8,128)(2,1)} custom-call(s32[1]{0:T(128)} %bitcast.4.place_ref, bf16[128,1536]{1,0:T(8,128)(2,1)} %copy-done.3, bf16[128,1536]{1,0:T(8,128)(2,1)} %copy-done.5, bf16[128,1536]{1,0:T(8,128)(2,1)} %collective-permute-done.2.refs_2_, bf16[128,1536]{1,0:T(8,128)(2,1)} %collective-permute-done.3.refs_3_, ...), custom_call_target="tpu_custom_call" | custom-call | bytes 6291456 | tf_op jit(solution)/shard_map/order/pallas_call | solution.py:157
  86.4 1.9 %collective-permute-start.8 = (bf16[8,128,1536]{2,1,0:T(8,128)(2,1)}, bf16[8,128,1536]{2,1,0:T(8,128)(2,1)}, u32[]{:S(2)}, u32[]{:S(2)}) collective-permute-start(bf16[8,128,1536]{2,1,0:T(8,128)(2,1)} %order.1.own_hbm), channel_id=1, source_target_pairs={{0,32},{32,0},{1,33},{33,1},{2,34},{34,2},{3,35},{35,3},{4,36},{36... | collective-permute-start | bytes 9437192 | tf_op jit(solution)/shard_map/ppermute | solution.py:462
  88.3 6.0 %collective-permute-done.8.other_hbm = bf16[8,128,1536]{2,1,0:T(8,128)(2,1)} collective-permute-done((bf16[8,128,1536]{2,1,0:T(8,128)(2,1)}, bf16[8,128,1536]{2,1,0:T(8,128)(2,1)}, u32[]{:S(2)}, u32[]{:S(2)}) %collective-permute-start.8) | collective-permute-done | bytes 3145760 | tf_op jit(solution)/shard_map/ppermute | solution.py:462
  94.3 3.4 %all-to-all-done = bf16[16,24,4096]{2,1,0:T(8,128)(2,1)S(1)} async-done(((bf16[16,24,4096]{2,1,0:T(8,128)(2,1)}), bf16[16,24,4096]{2,1,0:T(8,128)(2,1)S(1)}, u32[]{:S(2)}, u32[]{:S(2)}) %all-to-all-start) | async-done | bytes 3145760 | tf_op jit(solution)/shard_map/all_to_all | solution.py:458
  97.7 6.9 %forward.1 = (bf16[384,1024]{1,0:T(8,128)(2,1)S(1)}, bf16[384,512]{1,0:T(8,128)(2,1)S(1)}, bf16[384,128]{1,0:T(8,128)(2,1)S(1)}, bf16[1024,1536]{1,0:T(8,128)(2,1)S(1)}, bf16[8,2,128,1536]{3,2,1,0:T(8,128)(2,1)S(1)}) custom-call(s32[1]{0:T(128)} %bitcast.core_ref, bf16[384,4096]{1,0:T(8,128)(2,1)S(1)} %bitcast.9, bf16[8,128,1536]{2,1,0:T(8,128)(2,1)} %order.1.own_hbm, ...), custom_call_target="tpu_custom_call" | custom-call | flops 3623878656 | bytes 14680064 | tf_op jit(solution)/shard_map/forward/pallas_call | solution.py:270
  104.6 1.9 %collective-permute-start.9 = (bf16[1024,1536]{1,0:T(8,128)(2,1)S(1)}, bf16[1024,1536]{1,0:T(8,128)(2,1)S(1)}, u32[]{:S(2)}, u32[]{:S(2)}) collective-permute-start(bf16[1024,1536]{1,0:T(8,128)(2,1)S(1)} %get-tuple-element.29), channel_id=1, source_target_pairs={{0,32},{32,0},{1,33},{33,1},{2,34},{34,2},{3,35},{35,3},{4,36},{36... | collective-permute-start | bytes 9437192 | tf_op jit(solution)/shard_map/ppermute | solution.py:465
  106.5 3.0 %input_terms.1 = bf16[384,2176]{1,0:T(8,128)(2,1)} custom-call(bf16[384,1024]{1,0:T(8,128)(2,1)S(1)} %get-tuple-element.22.grads_ref, bf16[8,2,128,1536]{3,2,1,0:T(8,128)(2,1)S(1)} %get-tuple-element.23.held_ref, bf16[384,128]{1,0:T(8,128)(2,1)S(1)} %get-tuple-element.24.gate_ref), custom_call_target="tpu_custom_call" | custom-call | flops 1610612736 | bytes 9437184 | tf_op jit(solution)/shard_map/input_terms/pallas_call | solution.py:313
  109.5 1.8 %own_terms.1.own_ref = f32[1024,1536]{1,0:T(8,128)S(1)} custom-call(s32[1]{0:T(128)} %bitcast.core_ref, bf16[384,4096]{1,0:T(8,128)(2,1)S(1)} %bitcast.10, bf16[384,1024]{1,0:T(8,128)(2,1)S(1)} %get-tuple-element.22.grads_ref, bf16[384,512]{1,0:T(8,128)(2,1)S(1)} %get-tuple-element.28.hidden_ref), custom_call_target="tpu_custom_call" | custom-call | flops 1207959552 | bytes 10485760 | tf_op jit(solution)/shard_map/own_terms/pallas_call | solution.py:330
  111.4 0.7 collective-permute-done.9.arrived_ref
  112.1 1.8 %add.4 = bf16[1024,1536]{1,0:T(8,128)(2,1)} custom-call(f32[1024,1536]{1,0:T(8,128)S(1)} %own_terms.1.own_ref, bf16[1024,1536]{1,0:T(8,128)(2,1)S(1)} %collective-permute-done.9.arrived_ref), custom_call_target="tpu_custom_call" | custom-call | flops 1572864 | bytes 12582912 | tf_op jit(solution)/shard_map/add/pallas_call | solution.py:356
  113.9 0.0 copy-start.1
  113.9 0.0 copy-start.2
  114.0 0.0 reduce-scatter.2.cloned.1.call-update
  114.0 4.1 %all-to-all-start.1 = ((bf16[16,24,2176]{2,1,0:T(8,128)(2,1)}), bf16[16,24,2176]{2,1,0:T(8,128)(2,1)S(1)}, u32[]{:S(2)}, u32[]{:S(2)}) async-start(bf16[16,24,2176]{2,1,0:T(8,128)(2,1)} %bitcast.5), calls=%async_computation.1 | async-start | bytes 3342336 | tf_op jit(solution)/shard_map/all_to_all | solution.py:471
  118.0 41.6 %reduce-scatter.2.cloned.1.call-done.reduced_ref = bf16[128,1536]{1,0:T(8,128)(2,1)} async-done(((bf16[1024,1536]{1,0:T(8,128)(2,1)}), bf16[128,1536]{1,0:T(8,128)(2,1)}) %reduce-scatter.2.cloned.1.call-update) | async-done | bytes 393232 | tf_op jit(solution)/shard_map/reduce_scatter | solution.py:470
  159.7 0.0 copy-start
  159.7 1.0 slice.4
  160.7 2.6 %collective-permute-start.10 = (bf16[128,768]{1,0:T(8,128)(2,1)S(1)}, bf16[128,768]{1,0:T(8,128)(2,1)S(1)}, u32[]{:S(2)}, u32[]{:S(2)}) collective-permute-start(bf16[128,768]{1,0:T(8,128)(2,1)S(1)} %slice.4), channel_id=1, source_target_pairs={{0,1},{1,0},{2,3},{3,2},{4,5},{5,4},{6,7},{7,6},{8,9},{9,8},{10,11... | collective-permute-start | bytes 589832 | tf_op jit(solution)/shard_map/ppermute | solution.py:475
  163.4 0.0 all-to-all-done.1
  163.4 0.0 copy-done.1
  163.4 0.0 copy-done.2
  163.4 2.9 %unpack.1 = (bf16[2,128,2048]{2,1,0:T(8,128)(2,1)}, bf16[2,128]{1,0:T(2,128)(2,1)}) custom-call(bf16[384,2176]{1,0:T(8,128)(2,1)S(1)} %bitcast.7, bf16[384,2176]{1,0:T(8,128)(2,1)S(1)} %bitcast.8, bf16[2,128]{1,0:T(2,128)(2,1)S(1)} %copy-done.2, s32[2,128]{1,0:T(2,128)S(1)} %bitcast.12), custom_call_target="tpu_custom_call" | custom-call | flops 402653184 | bytes 3145728 | tf_op jit(solution)/shard_map/unpack/pallas_call | solution.py:395
  166.3 2.0 %collective-permute-done.10.partner_ref = bf16[128,768]{1,0:T(8,128)(2,1)S(1)} collective-permute-done((bf16[128,768]{1,0:T(8,128)(2,1)S(1)}, bf16[128,768]{1,0:T(8,128)(2,1)S(1)}, u32[]{:S(2)}, u32[]{:S(2)}) %collective-permute-start.10) | collective-permute-done | bytes 196640 | tf_op jit(solution)/shard_map/ppermute | solution.py:475
  168.3 0.0 copy-done
  168.3 0.8 finish.1
Async XLA Ops:
  10.8 86.9 %all-to-all-start = ((bf16[16,24,4096]{2,1,0:T(8,128)(2,1)}), bf16[16,24,4096]{2,1,0:T(8,128)(2,1)S(1)}, u32[]{:S(2)}, u32[]{:S(2)}) async-start(bf16[16,24,4096]{2,1,0:T(8,128)(2,1)} %bitcast.13), calls=%async_computation | async-start | bytes 6291456 | tf_op jit(solution)/shard_map/all_to_all | solution.py:458
  22.8 136.9 %reduce-scatter.2.cloned.1.call-start = ((), (), s32[]{:S(2)}) async-start(), calls=%async_computation.3 | async-start | bytes 3538944 | tf_op jit(solution)/shard_map/reduce_scatter | solution.py:470
  24.5 8.7 %collective-permute-start = (bf16[128,768]{1,0:T(8,128)(2,1)}, bf16[128,768]{1,0:T(8,128)(2,1)S(1)}, u32[]{:S(2)}, u32[]{:S(2)}) collective-permute-start(bf16[128,768]{1,0:T(8,128)(2,1)} %join.1), channel_id=1, source_target_pairs={{0,1},{1,0},{2,3},{3,2},{4,5},{5,4},{6,7},{7,6},{8,9},{9,8},{10,11... | collective-permute-start | bytes 589832 | tf_op jit(solution)/shard_map/ppermute | solution.py:457
  34.1 48.7 %copy-start.3 = (bf16[128,1536]{1,0:T(8,128)(2,1)}, bf16[128,1536]{1,0:T(8,128)(2,1)S(1)}, u32[]{:S(2)}) copy-start(bf16[128,1536]{1,0:T(8,128)(2,1)S(1)} %pad_maximum_fusion.refs_0_) | copy-start | bytes 1179652
  34.1 13.6 %collective-permute-start.4 = (bf16[128,1536]{1,0:T(8,128)(2,1)S(1)}, bf16[128,1536]{1,0:T(8,128)(2,1)S(1)}, u32[]{:S(2)}, u32[]{:S(2)}) collective-permute-start(bf16[128,1536]{1,0:T(8,128)(2,1)S(1)} %pad_maximum_fusion.refs_0_), channel_id=1, source_target_pairs={{0,64},{64,128},{128,192},{192,256},{256,320},{320,384},{384,448},... | collective-permute-start | bytes 1179656 | tf_op jit(solution)/shard_map/ppermute | solution.py:177
  37.6 12.0 %collective-permute-start.1 = (bf16[128,1536]{1,0:T(8,128)(2,1)S(1)}, bf16[128,1536]{1,0:T(8,128)(2,1)S(1)}, u32[]{:S(2)}, u32[]{:S(2)}) collective-permute-start(bf16[128,1536]{1,0:T(8,128)(2,1)S(1)} %pad_maximum_fusion.refs_0_), channel_id=1, source_target_pairs={{0,448},{64,0},{128,64},{192,128},{256,192},{320,256},{384,320},{4... | collective-permute-start | bytes 1179656 | tf_op jit(solution)/shard_map/ppermute | solution.py:180
  47.7 1.9 %copy-start.4 = (bf16[128,1536]{1,0:T(8,128)(2,1)}, bf16[128,1536]{1,0:T(8,128)(2,1)S(1)}, u32[]{:S(2)}) copy-start(bf16[128,1536]{1,0:T(8,128)(2,1)S(1)} %collective-permute-done.4.refs_7_) | copy-start | bytes 1179652
  47.7 12.4 %collective-permute-start.5 = (bf16[128,1536]{1,0:T(8,128)(2,1)S(1)}, bf16[128,1536]{1,0:T(8,128)(2,1)S(1)}, u32[]{:S(2)}, u32[]{:S(2)}) collective-permute-start(bf16[128,1536]{1,0:T(8,128)(2,1)S(1)} %collective-permute-done.4.refs_7_), channel_id=1, source_target_pairs={{0,64},{64,128},{128,192},{192,256},{256,320},{320,384},{384,448},... | collective-permute-start | bytes 1179656 | tf_op jit(solution)/shard_map/ppermute | solution.py:177
  49.6 10.4 %copy-start.5 = (bf16[128,1536]{1,0:T(8,128)(2,1)}, bf16[128,1536]{1,0:T(8,128)(2,1)S(1)}, u32[]{:S(2)}) copy-start(bf16[128,1536]{1,0:T(8,128)(2,1)S(1)} %collective-permute-done.1.refs_1_) | copy-start | bytes 1179652
  49.6 12.4 %collective-permute-start.2 = (bf16[128,1536]{1,0:T(8,128)(2,1)S(1)}, bf16[128,1536]{1,0:T(8,128)(2,1)}, u32[]{:S(2)}, u32[]{:S(2)}) collective-permute-start(bf16[128,1536]{1,0:T(8,128)(2,1)S(1)} %collective-permute-done.1.refs_1_), channel_id=1, source_target_pairs={{0,448},{64,0},{128,64},{192,128},{256,192},{320,256},{384,320},{4... | collective-permute-start | bytes 1179656 | tf_op jit(solution)/shard_map/ppermute | solution.py:180
  60.1 1.9 %copy-start.6 = (bf16[128,1536]{1,0:T(8,128)(2,1)}, bf16[128,1536]{1,0:T(8,128)(2,1)S(1)}, u32[]{:S(2)}) copy-start(bf16[128,1536]{1,0:T(8,128)(2,1)S(1)} %collective-permute-done.5.refs_6_) | copy-start | bytes 1179652
  60.1 11.6 %collective-permute-start.6 = (bf16[128,1536]{1,0:T(8,128)(2,1)S(1)}, bf16[128,1536]{1,0:T(8,128)(2,1)}, u32[]{:S(2)}, u32[]{:S(2)}) collective-permute-start(bf16[128,1536]{1,0:T(8,128)(2,1)S(1)} %collective-permute-done.5.refs_6_), channel_id=1, source_target_pairs={{0,64},{64,128},{128,192},{192,256},{256,320},{320,384},{384,448},... | collective-permute-start | bytes 1179656 | tf_op jit(solution)/shard_map/ppermute | solution.py:177
  62.0 11.5 %collective-permute-start.3 = (bf16[128,1536]{1,0:T(8,128)(2,1)}, bf16[128,1536]{1,0:T(8,128)(2,1)}, u32[]{:S(2)}, u32[]{:S(2)}) collective-permute-start(bf16[128,1536]{1,0:T(8,128)(2,1)} %collective-permute-done.2.refs_2_), channel_id=1, source_target_pairs={{0,448},{64,0},{128,64},{192,128},{256,192},{320,256},{384,320},{4... | collective-permute-start | bytes 1179656 | tf_op jit(solution)/shard_map/ppermute | solution.py:180
  71.6 11.2 %collective-permute-start.7 = (bf16[128,1536]{1,0:T(8,128)(2,1)}, bf16[128,1536]{1,0:T(8,128)(2,1)}, u32[]{:S(2)}, u32[]{:S(2)}) collective-permute-start(bf16[128,1536]{1,0:T(8,128)(2,1)} %collective-permute-done.6.refs_5_), channel_id=1, source_target_pairs={{0,64},{64,128},{128,192},{192,256},{256,320},{320,384},{384,448},... | collective-permute-start | bytes 1179656 | tf_op jit(solution)/shard_map/ppermute | solution.py:177
  86.4 7.9 %collective-permute-start.8 = (bf16[8,128,1536]{2,1,0:T(8,128)(2,1)}, bf16[8,128,1536]{2,1,0:T(8,128)(2,1)}, u32[]{:S(2)}, u32[]{:S(2)}) collective-permute-start(bf16[8,128,1536]{2,1,0:T(8,128)(2,1)} %order.1.own_hbm), channel_id=1, source_target_pairs={{0,32},{32,0},{1,33},{33,1},{2,34},{34,2},{3,35},{35,3},{4,36},{36... | collective-permute-start | bytes 9437192 | tf_op jit(solution)/shard_map/ppermute | solution.py:462
  104.6 7.6 %collective-permute-start.9 = (bf16[1024,1536]{1,0:T(8,128)(2,1)S(1)}, bf16[1024,1536]{1,0:T(8,128)(2,1)S(1)}, u32[]{:S(2)}, u32[]{:S(2)}) collective-permute-start(bf16[1024,1536]{1,0:T(8,128)(2,1)S(1)} %get-tuple-element.29), channel_id=1, source_target_pairs={{0,32},{32,0},{1,33},{33,1},{2,34},{34,2},{3,35},{35,3},{4,36},{36... | collective-permute-start | bytes 9437192 | tf_op jit(solution)/shard_map/ppermute | solution.py:465
  113.9 49.4 %copy-start.1 = (s32[2,128,1]{1,2,0:T(1,128)S(1)}, s32[2,128,1]{1,2,0:T(1,128)}, u32[]{:S(2)}) copy-start(s32[2,128,1]{1,2,0:T(1,128)} %param.10) | copy-start | bytes 3076
  113.9 49.4 %copy-start.2 = (bf16[2,128]{1,0:T(2,128)(2,1)S(1)}, bf16[2,128]{1,0:T(2,128)(2,1)}, u32[]{:S(2)}) copy-start(bf16[2,128]{1,0:T(2,128)(2,1)} %gate_ref.1) | copy-start | bytes 1540
  114.0 49.4 %all-to-all-start.1 = ((bf16[16,24,2176]{2,1,0:T(8,128)(2,1)}), bf16[16,24,2176]{2,1,0:T(8,128)(2,1)S(1)}, u32[]{:S(2)}, u32[]{:S(2)}) async-start(bf16[16,24,2176]{2,1,0:T(8,128)(2,1)} %bitcast.5), calls=%async_computation.1 | async-start | bytes 3342336 | tf_op jit(solution)/shard_map/all_to_all | solution.py:471
  159.7 8.6 %copy-start = (bf16[128,1536]{1,0:T(8,128)(2,1)S(1)}, bf16[128,1536]{1,0:T(8,128)(2,1)}, u32[]{:S(2)}) copy-start(bf16[128,1536]{1,0:T(8,128)(2,1)} %reduce-scatter.2.cloned.1.call-done.reduced_ref) | copy-start | bytes 1179652
  160.7 7.6 %collective-permute-start.10 = (bf16[128,768]{1,0:T(8,128)(2,1)S(1)}, bf16[128,768]{1,0:T(8,128)(2,1)S(1)}, u32[]{:S(2)}, u32[]{:S(2)}) collective-permute-start(bf16[128,768]{1,0:T(8,128)(2,1)S(1)} %slice.4), channel_id=1, source_target_pairs={{0,1},{1,0},{2,3},{3,2},{4,5},{5,4},{6,7},{7,6},{8,9},{9,8},{10,11... | collective-permute-start | bytes 589832 | tf_op jit(solution)/shard_map/ppermute | solution.py:475
Sparse Core Ops, SparseCore 0:
  114.1 45.5 reduce-scatter.1
